TPU v7x, 32 devices: a whole 2x2x4 slice. The times are simulated.
32 devices in a mesh: dp: 8 (over y, x, core), axial: 4 (over z).
Axes of the slice: x: 2, y: 2, z: 4, core: 2. Of those that a mesh axis runs over, the one named last changes fastest.
Arguments:
- homolog_activity: bfloat16 [64, 32, 256], P(('dp', 'axial')), parts along dimension 0, may hold values from -6 to 6
- homolog_symbol_ids: int32 [64, 32], P(('dp', 'axial')), parts along dimension 0, may hold values from 0 to 22
- residue_present_mask: int32 [256], P('dp'), parts along dimension 0, may hold values 0 or 1
- pair_state: bfloat16 [256, 32, 128], P(('dp', 'axial')), parts along dimension 0, may hold values from -6 to 6
- pair_valid_mask: int32 [256, 32], P(('dp', 'axial')), parts along dimension 0, may hold values 0 or 1
- symbol_lookup_matrix: bfloat16 [23, 256], replicated, may hold values from -3 to 3
- row_query_weight: bfloat16 [256, 256], replicated, as said below
- horizontal_attention_matrix: bfloat16 [256, 768], replicated, may hold values from -0.375 to 0.375
- pair_bias_weight: bfloat16 [128, 8], replicated, may hold values from -0.5 to 0.5
- horizontal_final_matrix: bfloat16 [256, 256], replicated, may hold values from -0.375 to 0.375
- column_query_weight: bfloat16 [256, 256], replicated, as said below
- vertical_attention_matrix: bfloat16 [256, 768], replicated, may hold values from -0.375 to 0.375
- vertical_final_matrix: bfloat16 [256, 256], replicated, may hold values from -0.375 to 0.375
- tensor_mean_lift_matrix: bfloat16 [256, 64], replicated, may hold values from -0.375 to 0.375
- outer_product_output_weight: bfloat16 [1024, 128], replicated, may hold values from -0.75 to 0.75
- triangle_projection_weight: bfloat16 [128, 256], replicated, may hold values from -0.5 to 0.5
- triangle_projection_gate: bfloat16 [128, 256], replicated, may hold values from -0.5 to 0.5
- triangle_output_gate: bfloat16 [128, 128], replicated, may hold values from -0.5 to 0.5
- triangle_output_weight: bfloat16 [128, 128], replicated, may hold values from -0.5 to 0.5
Outputs:
- alignment_output: bfloat16 [64, 32, 256], P('dp', 'axial'), parts along dimension 0
- pair_output: bfloat16 [256, 32, 128], P(('dp', 'axial')), parts along dimension 0
There are 8 independent parts, one for each index of `dp`. A program takes and returns all parts, laid end to end along the dimension named above; an argument that names none is the same for every part. Nothing has to cross between parts.
Inputs may be any that keep to these rules, and one draw needn't show every extreme that they name: `row_query_weight`: a projection of 256 inputs. `column_query_weight`: a projection of 256 inputs.
All inputs are finite; a program needn't handle non-finite values. No bound on the sum of `pair_valid_mask` on one device may be relied on, other than what follows from the above.
Results may differ from a plain program's by a relative error of at most 0.03.
The roundings to bfloat16 on the way count: a program that leaves them out, or rounds other values in their place, can miss the bound.
Values may be sent and summed in bfloat16 or wider, within the bound.
No kernel may reach another device: no remote copies, remote signals or barrier semaphores. Data moves between devices by JAX's collectives and lax.ppermute only.
A program may use at most 64 MiB of HBM per device.

v0:
```python
import functools

import jax
import jax.numpy as jnp
from jax import lax
from jax.experimental import pallas as pl
from jax.experimental.pallas import tpu as pltpu
from jax.sharding import PartitionSpec as P

FOCUS_TOTAL = 8
FOCUS_SIZE = 32
MEAN_HIDDEN_SIZE = 32
C_TRI = 128


def layer_normalize(attended_entries):
    attended_entries = attended_entries.astype(jnp.float32)
    mean = jnp.mean(attended_entries, axis=-1, keepdims=True)
    centred = attended_entries - mean
    var = jnp.mean(centred * centred, axis=-1, keepdims=True)
    return centred * lax.rsqrt(var + 1e-05)


def gated_attend(evoformer_block, extra_axes, w_query, w_kvg, w_out):
    lines_list, residue_length, input_width = evoformer_block.shape
    width = FOCUS_TOTAL * FOCUS_SIZE
    flat = (
        layer_normalize(evoformer_block)
        .astype(jnp.bfloat16)
        .reshape(lines_list * residue_length, input_width)
    )
    query = (
        jnp.dot(flat, w_query, preferred_element_type=jnp.float32) * FOCUS_SIZE ** (-0.5)
    ).astype(jnp.bfloat16)
    query = query.reshape(lines_list, residue_length, FOCUS_TOTAL, FOCUS_SIZE)
    kvg = jnp.dot(flat, w_kvg, preferred_element_type=jnp.float32)
    keys = (
        kvg[:, :width]
        .astype(jnp.bfloat16)
        .reshape(lines_list, residue_length, FOCUS_TOTAL, FOCUS_SIZE)
    )
    attended_entries = (
        kvg[:, width : 2 * width]
        .astype(jnp.bfloat16)
        .reshape(lines_list, residue_length, FOCUS_TOTAL, FOCUS_SIZE)
    )
    gate = jax.nn.sigmoid(kvg[:, 2 * width :]).reshape(
        lines_list, residue_length, FOCUS_TOTAL, FOCUS_SIZE
    )
    scores = (
        jnp.einsum("bihd,bjhd->bhij", query, keys, preferred_element_type=jnp.float32) + extra_axes
    )
    top = jnp.max(scores, axis=-1, keepdims=True)
    expo = jnp.exp(scores - top)
    weights = (expo / jnp.sum(expo, axis=-1, keepdims=True)).astype(jnp.bfloat16)
    mixed = jnp.einsum(
        "bhij,bjhd->bihd", weights, attended_entries, preferred_element_type=jnp.float32
    )
    mixed = (mixed * gate).astype(jnp.bfloat16).reshape(lines_list * residue_length, width)
    return evoformer_block + jnp.dot(mixed, w_out, preferred_element_type=jnp.float32).reshape(
        lines_list, residue_length, input_width
    )


def finish_sums(evoformer_block, triangle_output_weight):
    mixed = layer_normalize(jnp.transpose(evoformer_block, (1, 2, 0))).astype(jnp.bfloat16)
    return jnp.einsum(
        "ijc,cz->ijz", mixed, triangle_output_weight, preferred_element_type=jnp.float32
    )


def local_sharded(
    homolog_activity,
    homolog_symbol_ids,
    residue_present_mask,
    pair_state,
    pair_valid_mask,
    symbol_lookup_matrix,
    row_query_weight,
    horizontal_attention_matrix,
    pair_bias_weight,
    horizontal_final_matrix,
    column_query_weight,
    vertical_attention_matrix,
    vertical_final_matrix,
    tensor_mean_lift_matrix,
    outer_product_output_weight,
    triangle_projection_weight,
    triangle_projection_gate,
    triangle_output_gate,
    triangle_output_weight,
):
    sequence_per_device, residue_length, input_width = homolog_activity.shape
    res_dev = pair_state.shape[0]
    group_size = lax.axis_size("axial")
    token_classes = symbol_lookup_matrix.shape[0]
    token_one_hot = (
        homolog_symbol_ids[..., None] == jnp.arange(token_classes, dtype=jnp.int32)
    ).astype(jnp.bfloat16)
    token_embedded = jnp.einsum(
        "slt,tc->slc", token_one_hot, symbol_lookup_matrix, preferred_element_type=jnp.float32
    )
    homolog_starting = homolog_activity.astype(jnp.float32) + token_embedded
    pair_norm = layer_normalize(pair_state).astype(jnp.bfloat16)
    bias_rows = jnp.einsum(
        "ijc,ch->hij", pair_norm, pair_bias_weight, preferred_element_type=jnp.float32
    ).astype(jnp.bfloat16)
    bias_full = lax.all_gather(bias_rows, "axial", axis=1, tiled=True)
    key_bias = 1000000000.0 * (residue_present_mask.astype(jnp.float32) - 1.0)
    extra_axes = bias_full.astype(jnp.float32)[None] + key_bias[None, None, None, :]
    cluster_total = homolog_starting.reshape(
        sequence_per_device // 2, 2, residue_length, input_width
    )
    homolog_across_update = lax.map(
        lambda evoformer_block: gated_attend(
            evoformer_block,
            extra_axes,
            row_query_weight,
            horizontal_attention_matrix,
            horizontal_final_matrix,
        ),
        cluster_total,
    )
    homolog_across_update = homolog_across_update.reshape(
        sequence_per_device, group_size, res_dev, input_width
    ).astype(jnp.bfloat16)
    moved = jnp.swapaxes(
        lax.all_to_all(homolog_across_update, "axial", split_axis=1, concat_axis=0, tiled=True)[
            :, 0
        ],
        0,
        1,
    )
    finished = lax.map(
        lambda item: gated_attend(
            item[None].astype(jnp.float32),
            0.0,
            column_query_weight,
            vertical_attention_matrix,
            vertical_final_matrix,
        )[0],
        moved,
    )
    exchanged = jnp.swapaxes(finished, 0, 1).astype(jnp.bfloat16)[:, None]
    sequence_count = exchanged.shape[0]
    alignment_after_columns = exchanged.reshape(sequence_count, res_dev, input_width)
    tensor_mean_scaler = layer_normalize(alignment_after_columns).astype(jnp.bfloat16)
    split_parts = jnp.einsum(
        "src,cf->rsf",
        tensor_mean_scaler,
        tensor_mean_lift_matrix,
        preferred_element_type=jnp.float32,
    ).astype(jnp.bfloat16)
    first_factor = split_parts[..., :MEAN_HIDDEN_SIZE]
    second_factor = split_parts[..., MEAN_HIDDEN_SIZE:].reshape(
        res_dev, sequence_count * MEAN_HIDDEN_SIZE
    )
    step_rows = 8
    left_blocks = first_factor.reshape(
        res_dev // step_rows, step_rows, sequence_count, MEAN_HIDDEN_SIZE
    )
    piece = lax.all_gather(second_factor, "axial", axis=0, tiled=True)
    count = piece.shape[0]
    right_part = piece.reshape(count, sequence_count, MEAN_HIDDEN_SIZE)

    def one_block(lines_list):
        tensor_mean = (
            jnp.einsum("isc,jsd->ijcd", lines_list, right_part, preferred_element_type=jnp.float32)
            / sequence_count
        )
        tensor_mean = tensor_mean.reshape(
            step_rows, count, MEAN_HIDDEN_SIZE * MEAN_HIDDEN_SIZE
        ).astype(jnp.bfloat16)
        return jnp.einsum(
            "ijf,fz->ijz",
            tensor_mean,
            outer_product_output_weight,
            preferred_element_type=jnp.float32,
        )

    update = lax.map(one_block, left_blocks).reshape(
        res_dev, count, outer_product_output_weight.shape[1]
    )
    pair_one = pair_state.astype(jnp.float32) + update
    tri_norm = layer_normalize(pair_one).astype(jnp.bfloat16)
    proj = jnp.einsum(
        "ikc,cf->fik", tri_norm, triangle_projection_weight, preferred_element_type=jnp.float32
    )
    gates = jnp.einsum(
        "ikc,cf->fik", tri_norm, triangle_projection_gate, preferred_element_type=jnp.float32
    )
    both = (jax.nn.sigmoid(gates) * proj * pair_valid_mask.astype(jnp.float32)[None]).astype(
        jnp.bfloat16
    )
    left_tri = both[:C_TRI]
    right_tri = both[C_TRI:]
    moved_left, moved_right = (
        lax.all_to_all(left_tri, "axial", split_axis=0, concat_axis=1, tiled=True),
        lax.all_to_all(right_tri, "axial", split_axis=0, concat_axis=1, tiled=True),
    )
    partial_sum = jnp.einsum(
        "cik,cjk->cij", moved_left, moved_right, preferred_element_type=jnp.float32
    )
    tri_sum = lax.all_to_all(
        partial_sum.astype(jnp.bfloat16), "axial", split_axis=1, concat_axis=0, tiled=True
    ).astype(partial_sum.dtype)
    tri_update = finish_sums(tri_sum, triangle_output_weight)
    out_gate = jax.nn.sigmoid(
        jnp.einsum(
            "ijc,cz->ijz", tri_norm, triangle_output_gate, preferred_element_type=jnp.float32
        )
    )
    pair_output = (pair_one + out_gate * tri_update).astype(jnp.bfloat16)
    return (alignment_after_columns, pair_output)


BF16 = jnp.bfloat16
F32 = jnp.float32
SMALL_ROWS = 16
FLOPS = 3 * 10**9
PACKET_ORDER = (3, 2, 1)
PAIR_ORDER = (2, 1, 3)


def mul(lhs, rhs, over=((1,), (0,))):
    return lax.dot_general(lhs, rhs, (over, ((), ())), preferred_element_type=F32)


def iota(shape, axis):
    return lax.broadcasted_iota(jnp.int32, shape, axis)


def zero_one(condition):
    return jnp.where(condition, 1.0, 0.0).astype(BF16)


def normal(x):
    mean = jnp.mean(x, axis=-1, keepdims=True)
    centred = x - mean
    var = jnp.mean(centred * centred, axis=-1, keepdims=True)
    return centred * lax.rsqrt(var + 1e-05)


def sigmoid(x):
    return 0.5 + 0.5 * jnp.tanh(0.5 * x)


def column_softmax(scores):
    expo = jnp.exp(scores - jnp.max(scores, axis=0, keepdims=True))
    return expo * (1.0 / jnp.sum(expo, axis=0, keepdims=True))


def bias_rows(pair_ref, weight_ref):
    rows, residues, width = pair_ref.shape
    lanes = FOCUS_TOTAL * rows
    spread = zero_one(iota((FOCUS_TOTAL, lanes), 1) // rows == iota((FOCUS_TOTAL, lanes), 0))
    row_of = iota((width, lanes), 1) % rows
    flat = normal(pair_ref[...].astype(F32).reshape(rows * residues, width)).astype(BF16)
    weight = mul(weight_ref[...], spread, ((0,), (0,)))
    bias = jnp.zeros((residues, lanes), F32)
    for i in range(rows):
        one_row = jnp.where(row_of == i, weight, 0.0).astype(BF16)
        bias += mul(flat[i * residues : (i + 1) * residues], one_row)
    return bias


def table_kernel(lanes, count, shift_ref, turn_ref, column_ref):
    shape = column_ref.shape
    column_ref[...] = zero_one(iota(shape, 1) // C_TRI == iota(shape, 0))
    shape = shift_ref.shape
    shift_ref[...] = zero_one(iota(shape, 1) == iota(shape, 0) + lanes)
    shape = turn_ref.shape
    row_at = iota(shape, 0)
    turn_ref[...] = zero_one(
        iota(shape, 1) == (row_at % count) * (shape[0] // count) + row_at // count
    )


def packet_kernel(*refs):
    pair_ref, weight_ref, valid_ref, ids_ref, act_ref, present_ref, shift_ref = refs[:7]
    packet_ref, hidden_ref = refs[7:]
    rows, residues, width = pair_ref.shape
    per, _, features = act_ref.shape
    lanes = FOCUS_TOTAL * rows
    bias = bias_rows(pair_ref, weight_ref)
    extra = jnp.concatenate(
        [
            valid_ref[...].astype(F32),
            ids_ref[...].astype(F32),
            jnp.zeros((SMALL_ROWS - rows - per, residues), F32),
        ],
        axis=0,
    )
    extra = mul(extra.astype(BF16), shift_ref[...])
    empty = jnp.zeros((SMALL_ROWS, 128 - lanes), F32)
    first = jnp.concatenate([bias[:SMALL_ROWS], empty], axis=1) + extra
    second = jnp.concatenate([bias[SMALL_ROWS:], empty], axis=1)
    small = jnp.concatenate([first, second], axis=1).astype(BF16)
    packet_ref[per * residues :, :] = small
    shown = present_ref[...].astype(F32).astype(BF16)
    shown = mul(shown, jnp.ones((1, hidden_ref.shape[1]), BF16), ((0,), (0,)))
    hidden_ref[...] = 1000000000.0 * (shown - 1.0)
    packet_ref[: per * residues, :] = act_ref[...].reshape(per * residues, features)


def split_small(packet, residues, res_dev, per):
    small = packet[per * residues :, :].astype(F32)
    lanes = FOCUS_TOTAL * res_dev
    bias = jnp.concatenate([small[:, :lanes], small[:, 128 : 128 + lanes]], axis=0)
    extra = small[:, lanes : lanes + residues]
    return bias, extra[:res_dev], extra[res_dev : res_dev + per]


def head_masks(width):
    return [
        zero_one(iota((1, width), 1) // FOCUS_SIZE == h) for h in range(FOCUS_TOTAL)
    ]


def project(x, w_query, w_kvg):
    width = FOCUS_TOTAL * FOCUS_SIZE
    flat = normal(x).astype(BF16)
    query = (mul(flat, w_query[...]) * FOCUS_SIZE ** (-0.5)).astype(BF16)
    keys = mul(flat, w_kvg[:, :width]).astype(BF16)
    values = mul(flat, w_kvg[:, width : 2 * width]).astype(BF16)
    gate = sigmoid(mul(flat, w_kvg[:, 2 * width :]))
    return query, keys, values, gate


def msa_kernel(n, res_dev, *refs):
    packets, turn, hidden_keys, table = refs[:n], refs[n], refs[n + 1], refs[n + 2]
    refs = refs[n + 3 :]
    row_q, row_kvg, row_out, col_q, col_kvg, col_out, lift, outer_w = refs[:8]
    align_ref, update_ref, lifted = refs[8:]
    kinds, width = table.shape
    residues, lanes = hidden_keys.shape
    pair_width = outer_w.shape[1]
    per = (packets[0].shape[0] - SMALL_ROWS) // residues
    count = per * n
    tokens = count * residues
    me = lax.axis_index("axial")

    place = iota((FOCUS_TOTAL * res_dev, lanes), 0)
    place = (place // res_dev) * residues + place % res_dev - iota(place.shape, 1)
    bias = jnp.zeros((residues, lanes), F32)
    rows = []
    for packet, r in zip(packets, (0, *PACKET_ORDER)):
        part, _, all_ids = split_small(packet, residues, res_dev, per)
        bias += mul(part.astype(BF16), zero_one(place == -(me ^ r) * res_dev))
        for q in range(per):
            hot = zero_one(iota((kinds, residues), 0).astype(F32) == all_ids[q : q + 1])
            act = packet[q * residues : (q + 1) * residues, :].astype(F32)
            rows.append(act + mul(hot, table[...], ((0,), (0,))))
    zero = jnp.concatenate(rows, axis=0)
    extra = bias + hidden_keys[...]
    masks = head_masks(width)

    query, keys, values, gate = project(zero, row_q, row_kvg)
    rows = []
    for s in range(count):
        here = slice(s * residues, (s + 1) * residues)
        spread = jnp.concatenate([query[here] * mask for mask in masks], axis=0)
        weights = column_softmax(mul(keys[here], spread, ((1,), (1,))) + extra).astype(BF16)
        heads = mul(weights, values[here], ((0,), (0,)))
        mixed = heads[:residues]
        for h in range(1, FOCUS_TOTAL):
            part = heads[h * residues : (h + 1) * residues]
            mixed = jnp.where(iota((1, width), 1) // FOCUS_SIZE == h, part, mixed)
        rows.append(mixed)
    mixed = (jnp.concatenate(rows, axis=0) * gate).astype(BF16)
    msa_one = (zero + mul(mixed, row_out[...])).astype(BF16)

    one = mul(turn[...], msa_one)
    query, keys, values, gate = project(one, col_q, col_kvg)
    group = min(tokens, 128)
    sites = group // count
    block_of = iota((1, group), 1) // count
    groups = []
    for g in range(tokens // group):
        here = slice(g * group, (g + 1) * group)
        all_weights, all_values = [], []
        for mask in masks:
            full = mul(keys[here], query[here] * mask, ((1,), (1,)))
            scores = full[:count]
            for b in range(1, sites):
                scores = jnp.where(block_of == b, full[b * count : (b + 1) * count], scores)
            weights = column_softmax(scores)
            weights = jnp.concatenate(
                [jnp.where(block_of == b, weights, 0.0) for b in range(sites)], axis=0
            )
            all_weights.append(weights.astype(BF16))
            all_values.append(values[here] * mask)
        groups.append(
            mul(
                jnp.concatenate(all_weights, axis=0),
                jnp.concatenate(all_values, axis=0),
                ((0,), (0,)),
            )
        )
    mixed = (jnp.concatenate(groups, axis=0) * gate).astype(BF16)
    align = (one + mul(mixed, col_out[...])).astype(BF16)
    own = count * res_dev
    row_at, lane_at = iota((own, tokens), 0), iota((own, tokens), 1)
    sequence = row_at // res_dev
    owner = (sequence // per) ^ me
    where_is = jnp.zeros_like(owner)
    for k, r in enumerate(PACKET_ORDER):
        where_is = jnp.where(owner == r, k + 1, where_is)
    pick = zero_one(
        lane_at
        == (row_at % res_dev + me * res_dev) * count + where_is * per + sequence % per
    )
    align_ref[...] = mul(pick, align).reshape(count, res_dev, width).astype(BF16)

    opm = normal(align.astype(F32)).astype(BF16)
    opm = mul(opm, lift[...], ((1,), (1,))).astype(BF16)
    hidden = MEAN_HIDDEN_SIZE
    deep = hidden * count
    spread = zero_one(
        iota((2 * hidden, deep), 1) // count == iota((2 * hidden, deep), 0)
    )
    left = mul(opm, spread)
    left = jnp.where(
        iota((tokens, deep), 0) % count == iota((tokens, deep), 1) % count, left, 0.0
    ).astype(BF16)
    gather = zero_one(iota((residues, tokens), 1) // count == iota((residues, tokens), 0))
    left = mul(gather, left).astype(BF16)
    right = opm[:, hidden:]
    for c in range(0, hidden, 2):
        pair_w = jnp.concatenate(
            [outer_w[(c + k) * hidden : (c + k + 1) * hidden, :] for k in range(2)], axis=1
        )
        part = mul(right, pair_w)
        lifted[c], lifted[c + 1] = part[:, :pair_width], part[:, pair_width:]
    for j in range(0, residues, 2):
        part = jnp.concatenate(
            [
                lifted[:, (j + k) * count : (j + k + 1) * count, :].reshape(deep, pair_width)
                for k in range(2)
            ],
            axis=1,
        )
        part = mul(left, part.astype(BF16)) * (1.0 / count)
        update_ref[j], update_ref[j + 1] = part[:, :pair_width], part[:, pair_width:]


def pair_kernel(*refs):
    pairs, packets, update, column, pair, own_mask = refs[:3], refs[3:6], *refs[6:10]
    proj, gates, gate_out, w_out, out_ref, state, one, right_at, left_at, valid = refs[10:]
    res_dev, residues, width = pair.shape
    per = (packets[0].shape[0] - SMALL_ROWS) // residues
    me = lax.axis_index("axial")
    own_valid = own_mask[...].astype(F32)
    for packet, r in zip((None, *packets), (0, *PACKET_ORDER)):
        shown = split_small(packet, residues, res_dev, per)[1] if r else own_valid
        valid[pl.ds(pl.multiple_of((me ^ r) * res_dev, res_dev), res_dev), :] = shown
    size = res_dev * residues
    for block, r in zip((pair, *pairs), (0, *PAIR_ORDER)):
        state[pl.ds(pl.multiple_of((me ^ r) * size, size), size), :] = (
            block[...].astype(F32).reshape(size, width)
        )
    for k in range(residues):
        one[k * residues : (k + 1) * residues, :] = (
            state[pl.ds(k, residues, stride=residues), :] + update[k]
        )

    shown = mul(valid[...].astype(BF16), column[...])
    right_w = jnp.concatenate([proj[:, C_TRI:], gates[:, C_TRI:]], axis=1)
    step = 8
    for k in range(0, residues, step):
        here = slice(k * residues, (k + step) * residues)
        both = mul(normal(one[here, :]).astype(BF16), right_w)
        both = sigmoid(both[:, C_TRI:]) * both[:, :C_TRI]
        for p in range(step):
            part = both[p * residues : (p + 1) * residues]
            part = part * shown[:, (k + p) * C_TRI : (k + p + 1) * C_TRI]
            right_at[(k + p) * residues : (k + p + 1) * residues, :] = part.astype(BF16).astype(F32)

    own = jnp.concatenate(
        [one[pl.ds(me * res_dev + i, residues, stride=residues), :] for i in range(res_dev)],
        axis=0,
    )
    left_w = jnp.concatenate([proj[:, :C_TRI], gates[:, :C_TRI], gate_out[...]], axis=1)
    own_all = mul(normal(own).astype(BF16), left_w)
    own_gate = sigmoid(own_all[:, 2 * C_TRI :])
    left = sigmoid(own_all[:, C_TRI : 2 * C_TRI]) * own_all[:, :C_TRI]
    shown = mul(own_valid.astype(BF16), column[:res_dev, : res_dev * C_TRI], ((0,), (0,)))
    for i in range(res_dev):
        part = left[i * residues : (i + 1) * residues] * shown[:, i * C_TRI : (i + 1) * C_TRI]
        left_at[i * residues : (i + 1) * residues, :] = part.astype(BF16).astype(F32)
    sums = [jnp.zeros((residues, C_TRI), F32) for _ in range(res_dev)]
    for k in range(residues):
        other = right_at[k * residues : (k + 1) * residues, :]
        for i in range(res_dev):
            sums[i] += left_at[i * residues + k : i * residues + k + 1, :] * other
    mixed = normal(jnp.concatenate(sums, axis=0)).astype(BF16)
    result = own + own_gate * mul(mixed, w_out[...])
    out_ref[...] = result.reshape(res_dev, residues, width).astype(BF16)


def call(kernel, out_shape, scratch, vmem_mib, *args):
    vmem = pl.BlockSpec(memory_space=pltpu.VMEM)
    return pl.pallas_call(
        kernel,
        out_shape=out_shape,
        in_specs=[vmem] * len(args),
        out_specs=jax.tree.map(lambda _: vmem, out_shape),
        scratch_shapes=scratch,
        compiler_params=pltpu.CompilerParams(vmem_limit_bytes=vmem_mib * 1024 * 1024),
        cost_estimate=pl.CostEstimate(flops=FLOPS, bytes_accessed=0, transcendentals=0),
    )(*args)


def swap(array, r, n):
    return lax.ppermute(array, "axial", [(i, i ^ r) for i in range(n)])


def local_whole(
    homolog_activity,
    homolog_symbol_ids,
    residue_present_mask,
    pair_state,
    pair_valid_mask,
    symbol_lookup_matrix,
    row_query_weight,
    horizontal_attention_matrix,
    pair_bias_weight,
    horizontal_final_matrix,
    column_query_weight,
    vertical_attention_matrix,
    vertical_final_matrix,
    tensor_mean_lift_matrix,
    outer_product_output_weight,
    triangle_projection_weight,
    triangle_projection_gate,
    triangle_output_gate,
    triangle_output_weight,
):
    n = lax.axis_size("axial")
    per, residues, width = homolog_activity.shape
    res_dev, _, pair_width = pair_state.shape
    count = per * n
    shift, turn, column = call(
        functools.partial(table_kernel, FOCUS_TOTAL * res_dev, count),
        (
            jax.ShapeDtypeStruct((residues, 128), BF16),
            jax.ShapeDtypeStruct((count * residues, count * residues), BF16),
            jax.ShapeDtypeStruct((residues, residues * C_TRI), BF16),
        ),
        [],
        2,
    )
    packet, hidden_keys = call(
        packet_kernel,
        (
            jax.ShapeDtypeStruct((per * residues + SMALL_ROWS, width), BF16),
            jax.ShapeDtypeStruct((residues, FOCUS_TOTAL * residues), F32),
        ),
        [],
        4,
        pair_state,
        pair_bias_weight.T,
        pair_valid_mask,
        homolog_symbol_ids,
        homolog_activity,
        residue_present_mask.reshape(1, residues),
        shift,
    )
    packets = [swap(packet, r, n) for r in PACKET_ORDER]
    _, later = lax.optimization_barrier((packet, pair_state))
    pairs = [swap(later, r, n) for r in PAIR_ORDER]
    alignment, update = call(
        functools.partial(msa_kernel, n, res_dev),
        (
            jax.ShapeDtypeStruct((count, res_dev, width), BF16),
            jax.ShapeDtypeStruct((residues, residues, pair_width), F32),
        ),
        [
            pltpu.VMEM((MEAN_HIDDEN_SIZE, count * residues, pair_width), F32),
        ],
        16,
        packet,
        *packets,
        turn,
        hidden_keys,
        symbol_lookup_matrix,
        row_query_weight,
        horizontal_attention_matrix,
        horizontal_final_matrix,
        column_query_weight,
        vertical_attention_matrix,
        vertical_final_matrix,
        tensor_mean_lift_matrix.T,
        outer_product_output_weight,
    )
    pair_output = call(
        pair_kernel,
        jax.ShapeDtypeStruct((res_dev, residues, pair_width), BF16),
        [
            pltpu.VMEM((residues * residues, pair_width), F32),
            pltpu.VMEM((residues * residues, pair_width), F32),
            pltpu.VMEM((residues * residues, C_TRI), F32),
            pltpu.VMEM((res_dev * residues, C_TRI), F32),
            pltpu.VMEM((residues, residues), F32),
        ],
        16,
        *pairs,
        *packets,
        update,
        column,
        pair_state,
        pair_valid_mask,
        triangle_projection_weight,
        triangle_projection_gate,
        triangle_output_gate,
        triangle_output_weight,
    )
    return (alignment, pair_output)


def local(homolog_activity, homolog_symbol_ids, residue_present_mask, pair_state, *others):
    n = lax.axis_size("axial")
    per, residues, _ = homolog_activity.shape
    small = n == 4 and per * n == 8 and residues == 32
    plan = local_whole if small else local_sharded
    return plan(homolog_activity, homolog_symbol_ids, residue_present_mask, pair_state, *others)


def solution(mesh):
    parts, copied = P(("dp", "axial")), P()
    return jax.shard_map(
        local,
        mesh=mesh,
        in_specs=(parts, parts, P("dp"), parts, parts) + (copied,) * 14,
        out_specs=(P("dp", "axial", None), P(("dp", "axial"), None, None)),
        check_vma=False,
    )
```

profile of v0, /device:TPU:0, one launch (start us, length us, event | category | flops | bytes accessed | tf_op | source)
XLA Modules:
  0.0 20.3 jit_solution(9369601359857120873)
XLA Ops:
  0.7 0.1 shard_map.194
  0.7 0.0 copy-start.15
  0.8 0.0 copy-start.17
  0.8 0.0 copy-start.18
  0.8 0.7 %copy-done.7 = bf16[8,32,128]{2,1,0:T(8,128)(2,1)S(1)} copy-done((bf16[8,32,128]{2,1,0:T(8,128)(2,1)S(1)}, bf16[8,32,128]{2,1,0:T(8,128)(2,1)}, u32[]{:S(2)}) %copy-start.7) | copy-done | bytes 65560
  1.5 0.0 copy-start
  1.5 0.0 copy-start.1
  1.5 0.0 copy-start.2
  1.5 0.0 copy-start.3
  1.5 0.0 copy-start.4
  1.6 0.0 copy-start.5
  1.6 0.0 copy-start.6
  1.6 0.0 copy-start.14
  1.6 0.4 %shard_map.195 = (bf16[80,256]{1,0:T(8,128)(2,1)S(1)}, f32[32,256]{1,0:T(8,128)S(1)}) custom-call(bf16[8,32,128]{2,1,0:T(8,128)(2,1)S(1)} %copy-done.7, bf16[8,128]{1,0:T(8,128)(2,1)S(1)} %bitcast.4, s32[8,32]{1,0:T(8,128)S(1)} %copy-done.15, s32[2,32]{1,0:T(2,128)S(1)} %copy-done.17, bf16[2,32,256]{2,1,0:T(8,128)(2,1)S(1)} %copy-done.10, ...), custom_call_target="tpu_custom_call" | custom-call | flops 3000000000 | tf_op jit(solution)/shard_map/pallas_call | solution.py:503
  2.0 5.1 %collective-permute-start = (bf16[80,256]{1,0:T(8,128)(2,1)S(1)}, bf16[80,256]{1,0:T(8,128)(2,1)S(1)}, u32[]{:S(2)}, u32[]{:S(2)}) collective-permute-start(bf16[80,256]{1,0:T(8,128)(2,1)S(1)} %get-tuple-element.11.refs_0_), channel_id=1, source_target_pairs={{0,3},{1,2},{2,1},{3,0},{4,7},{5,6},{6,5},{7,4},{8,11},{9,10},{10,... | collective-permute-start | bytes 122888 | tf_op jit(solution)/shard_map/ppermute | solution.py:515
  7.1 0.6 %collective-permute-start.2 = (bf16[80,256]{1,0:T(8,128)(2,1)S(1)}, bf16[80,256]{1,0:T(8,128)(2,1)S(1)}, u32[]{:S(2)}, u32[]{:S(2)}) collective-permute-start(bf16[80,256]{1,0:T(8,128)(2,1)S(1)} %get-tuple-element.11.refs_0_), channel_id=1, source_target_pairs={{0,1},{1,0},{2,3},{3,2},{4,5},{5,4},{6,7},{7,6},{8,9},{9,8},{10,11... | collective-permute-start | bytes 122888 | tf_op jit(solution)/shard_map/ppermute | solution.py:515
  7.8 2.3 %collective-permute-start.3 = (bf16[8,32,128]{2,1,0:T(8,128)(2,1)S(1)}, bf16[8,32,128]{2,1,0:T(8,128)(2,1)S(1)}, u32[]{:S(2)}, u32[]{:S(2)}) collective-permute-start(bf16[8,32,128]{2,1,0:T(8,128)(2,1)S(1)} %copy-done.7), channel_id=1, source_target_pairs={{0,2},{1,3},{2,0},{3,1},{4,6},{5,7},{6,4},{7,5},{8,10},{9,11},{10,... | collective-permute-start | bytes 196616 | tf_op jit(solution)/shard_map/ppermute | solution.py:515
  10.1 2.0 %collective-permute-start.4 = (bf16[8,32,128]{2,1,0:T(8,128)(2,1)S(1)}, bf16[8,32,128]{2,1,0:T(8,128)(2,1)S(1)}, u32[]{:S(2)}, u32[]{:S(2)}) collective-permute-start(bf16[8,32,128]{2,1,0:T(8,128)(2,1)S(1)} %copy-done.7), channel_id=1, source_target_pairs={{0,1},{1,0},{2,3},{3,2},{4,5},{5,4},{6,7},{7,6},{8,9},{9,8},{10,11... | collective-permute-start | bytes 196616 | tf_op jit(solution)/shard_map/ppermute | solution.py:515
  12.1 1.0 %collective-permute-start.5 = (bf16[8,32,128]{2,1,0:T(8,128)(2,1)S(1)}, bf16[8,32,128]{2,1,0:T(8,128)(2,1)S(1)}, u32[]{:S(2)}, u32[]{:S(2)}) collective-permute-start(bf16[8,32,128]{2,1,0:T(8,128)(2,1)S(1)} %copy-done.7), channel_id=1, source_target_pairs={{0,3},{1,2},{2,1},{3,0},{4,7},{5,6},{6,5},{7,4},{8,11},{9,10},{10,... | collective-permute-start | bytes 196616 | tf_op jit(solution)/shard_map/ppermute | solution.py:515
  13.2 0.0 copy-start.12
  13.2 0.0 copy-start.13
  13.3 4.6 %shard_map.196 = (bf16[8,8,256]{2,1,0:T(8,128)(2,1)}, f32[32,32,128]{2,1,0:T(8,128)S(1)}) custom-call(bf16[80,256]{1,0:T(8,128)(2,1)S(1)} %get-tuple-element.11.refs_0_, bf16[80,256]{1,0:T(8,128)(2,1)S(1)} %collective-permute-done.refs_1_.refs_3_, bf16[80,256]{1,0:T(8,128)(2,1)S(1)} %collective-permute-done.1.refs_2_.refs_4_, ...), custom_call_target="tpu_custom_call" | custom-call | flops 3000000000 | tf_op jit(solution)/shard_map/pallas_call | solution.py:503
  17.9 0.3 %collective-permute-done.5.refs_2_ = bf16[8,32,128]{2,1,0:T(8,128)(2,1)S(1)} collective-permute-done((bf16[8,32,128]{2,1,0:T(8,128)(2,1)S(1)}, bf16[8,32,128]{2,1,0:T(8,128)(2,1)S(1)}, u32[]{:S(2)}, u32[]{:S(2)}) %collective-permute-start.5) | collective-permute-done | bytes 65568 | tf_op jit(solution)/shard_map/ppermute | solution.py:515
  18.2 2.2 %shard_map.197 = bf16[8,32,128]{2,1,0:T(8,128)(2,1)} custom-call(bf16[8,32,128]{2,1,0:T(8,128)(2,1)S(1)} %collective-permute-done.3.refs_0_, bf16[8,32,128]{2,1,0:T(8,128)(2,1)S(1)} %collective-permute-done.4.refs_1_, bf16[8,32,128]{2,1,0:T(8,128)(2,1)S(1)} %collective-permute-done.5.refs_2_, bf16[80,256]{1,0:T(8,128)(2,1)S(1)} %collective-permute-done.refs_1_.refs_3_, ...), custom_call_target="tpu_custom_call" | custom-call | flops 3000000000 | tf_op jit(solution)/shard_map/pallas_call | solution.py:503
  (30 shorter events, 0.1 us)
Async XLA Ops:
  0.6 0.8 %copy-start.7 = (bf16[8,32,128]{2,1,0:T(8,128)(2,1)S(1)}, bf16[8,32,128]{2,1,0:T(8,128)(2,1)}, u32[]{:S(2)}) copy-start(bf16[8,32,128]{2,1,0:T(8,128)(2,1)} %refs_8_.3) | copy-start | bytes 196612
  0.6 0.8 %copy-start.10 = (bf16[2,32,256]{2,1,0:T(8,128)(2,1)S(1)}, bf16[2,32,256]{2,1,0:T(8,128)(2,1)}, u32[]{:S(2)}) copy-start(bf16[2,32,256]{2,1,0:T(8,128)(2,1)} %refs_4_.1) | copy-start | bytes 98308
  0.6 0.8 %copy-start.16 = (bf16[128,8]{0,1:T(8,128)(2,1)S(1)}, bf16[128,8]{0,1:T(8,128)(2,1)}, u32[]{:S(2)}) copy-start(bf16[128,8]{0,1:T(8,128)(2,1)} %param.27) | copy-start | bytes 6148
  0.7 0.7 %copy-start.15 = (s32[8,32]{1,0:T(8,128)S(1)}, s32[8,32]{1,0:T(8,128)}, u32[]{:S(2)}) copy-start(s32[8,32]{1,0:T(8,128)} %refs_9_.3) | copy-start | bytes 3076
  0.8 0.7 %copy-start.17 = (s32[2,32]{1,0:T(2,128)S(1)}, s32[2,32]{1,0:T(2,128)}, u32[]{:S(2)}) copy-start(s32[2,32]{1,0:T(2,128)} %refs_3_.1) | copy-start | bytes 772
  1.5 11.6 %copy-start = (bf16[256,768]{1,0:T(8,128)(2,1)S(1)}, bf16[256,768]{1,0:T(8,128)(2,1)}, u32[]{:S(2)}) copy-start(bf16[256,768]{1,0:T(8,128)(2,1)} %refs_8_.2) | copy-start | bytes 1179652
  1.5 11.6 %copy-start.1 = (bf16[256,768]{1,0:T(8,128)(2,1)S(1)}, bf16[256,768]{1,0:T(8,128)(2,1)}, u32[]{:S(2)}) copy-start(bf16[256,768]{1,0:T(8,128)(2,1)} %refs_11_.2) | copy-start | bytes 1179652
  1.5 11.6 %copy-start.2 = (bf16[1024,128]{1,0:T(8,128)(2,1)S(1)}, bf16[1024,128]{1,0:T(8,128)(2,1)}, u32[]{:S(2)}) copy-start(bf16[1024,128]{1,0:T(8,128)(2,1)} %refs_14_.1) | copy-start | bytes 786436
  1.5 11.6 %copy-start.3 = (bf16[256,256]{1,0:T(8,128)(2,1)S(1)}, bf16[256,256]{1,0:T(8,128)(2,1)}, u32[]{:S(2)}) copy-start(bf16[256,256]{1,0:T(8,128)(2,1)} %refs_7_.1) | copy-start | bytes 393220
  1.5 11.6 %copy-start.4 = (bf16[256,256]{1,0:T(8,128)(2,1)S(1)}, bf16[256,256]{1,0:T(8,128)(2,1)}, u32[]{:S(2)}) copy-start(bf16[256,256]{1,0:T(8,128)(2,1)} %refs_9_.2) | copy-start | bytes 393220
  1.6 11.6 %copy-start.5 = (bf16[256,256]{1,0:T(8,128)(2,1)S(1)}, bf16[256,256]{1,0:T(8,128)(2,1)}, u32[]{:S(2)}) copy-start(bf16[256,256]{1,0:T(8,128)(2,1)} %refs_10_.2) | copy-start | bytes 393220
  1.6 11.6 %copy-start.6 = (bf16[256,256]{1,0:T(8,128)(2,1)S(1)}, bf16[256,256]{1,0:T(8,128)(2,1)}, u32[]{:S(2)}) copy-start(bf16[256,256]{1,0:T(8,128)(2,1)} %refs_12_.2) | copy-start | bytes 393220
  1.6 11.6 %copy-start.11 = (bf16[256,64]{0,1:T(8,128)(2,1)S(1)}, bf16[256,64]{0,1:T(8,128)(2,1)}, u32[]{:S(2)}) copy-start(bf16[256,64]{0,1:T(8,128)(2,1)} %param.32) | copy-start | bytes 98308
  1.6 11.6 %copy-start.14 = (bf16[23,256]{1,0:T(8,128)(2,1)S(1)}, bf16[23,256]{1,0:T(8,128)(2,1)}, u32[]{:S(2)}) copy-start(bf16[23,256]{1,0:T(8,128)(2,1)} %refs_6_.1) | copy-start | bytes 35332
  2.0 10.1 %collective-permute-start = (bf16[80,256]{1,0:T(8,128)(2,1)S(1)}, bf16[80,256]{1,0:T(8,128)(2,1)S(1)}, u32[]{:S(2)}, u32[]{:S(2)}) collective-permute-start(bf16[80,256]{1,0:T(8,128)(2,1)S(1)} %get-tuple-element.11.refs_0_), channel_id=1, source_target_pairs={{0,3},{1,2},{2,1},{3,0},{4,7},{5,6},{6,5},{7,4},{8,11},{9,10},{10,... | collective-permute-start | bytes 122888 | tf_op jit(solution)/shard_map/ppermute | solution.py:515
  7.1 6.0 %collective-permute-start.1 = (bf16[80,256]{1,0:T(8,128)(2,1)S(1)}, bf16[80,256]{1,0:T(8,128)(2,1)S(1)}, u32[]{:S(2)}, u32[]{:S(2)}) collective-permute-start(bf16[80,256]{1,0:T(8,128)(2,1)S(1)} %get-tuple-element.11.refs_0_), channel_id=1, source_target_pairs={{0,2},{1,3},{2,0},{3,1},{4,6},{5,7},{6,4},{7,5},{8,10},{9,11},{10,... | collective-permute-start | bytes 122888 | tf_op jit(solution)/shard_map/ppermute | solution.py:515
  7.1 6.0 %collective-permute-start.2 = (bf16[80,256]{1,0:T(8,128)(2,1)S(1)}, bf16[80,256]{1,0:T(8,128)(2,1)S(1)}, u32[]{:S(2)}, u32[]{:S(2)}) collective-permute-start(bf16[80,256]{1,0:T(8,128)(2,1)S(1)} %get-tuple-element.11.refs_0_), channel_id=1, source_target_pairs={{0,1},{1,0},{2,3},{3,2},{4,5},{5,4},{6,7},{7,6},{8,9},{9,8},{10,11... | collective-permute-start | bytes 122888 | tf_op jit(solution)/shard_map/ppermute | solution.py:515
  7.8 10.1 %collective-permute-start.3 = (bf16[8,32,128]{2,1,0:T(8,128)(2,1)S(1)}, bf16[8,32,128]{2,1,0:T(8,128)(2,1)S(1)}, u32[]{:S(2)}, u32[]{:S(2)}) collective-permute-start(bf16[8,32,128]{2,1,0:T(8,128)(2,1)S(1)} %copy-done.7), channel_id=1, source_target_pairs={{0,2},{1,3},{2,0},{3,1},{4,6},{5,7},{6,4},{7,5},{8,10},{9,11},{10,... | collective-permute-start | bytes 196616 | tf_op jit(solution)/shard_map/ppermute | solution.py:515
  10.1 7.8 %collective-permute-start.4 = (bf16[8,32,128]{2,1,0:T(8,128)(2,1)S(1)}, bf16[8,32,128]{2,1,0:T(8,128)(2,1)S(1)}, u32[]{:S(2)}, u32[]{:S(2)}) collective-permute-start(bf16[8,32,128]{2,1,0:T(8,128)(2,1)S(1)} %copy-done.7), channel_id=1, source_target_pairs={{0,1},{1,0},{2,3},{3,2},{4,5},{5,4},{6,7},{7,6},{8,9},{9,8},{10,11... | collective-permute-start | bytes 196616 | tf_op jit(solution)/shard_map/ppermute | solution.py:515
  12.1 6.1 %collective-permute-start.5 = (bf16[8,32,128]{2,1,0:T(8,128)(2,1)S(1)}, bf16[8,32,128]{2,1,0:T(8,128)(2,1)S(1)}, u32[]{:S(2)}, u32[]{:S(2)}) collective-permute-start(bf16[8,32,128]{2,1,0:T(8,128)(2,1)S(1)} %copy-done.7), channel_id=1, source_target_pairs={{0,3},{1,2},{2,1},{3,0},{4,7},{5,6},{6,5},{7,4},{8,11},{9,10},{10,... | collective-permute-start | bytes 196616 | tf_op jit(solution)/shard_map/ppermute | solution.py:515
  13.2 4.9 %copy-start.8 = (bf16[128,256]{1,0:T(8,128)(2,1)S(1)}, bf16[128,256]{1,0:T(8,128)(2,1)}, u32[]{:S(2)}) copy-start(bf16[128,256]{1,0:T(8,128)(2,1)} %refs_10_.3) | copy-start | bytes 196612
  13.2 4.9 %copy-start.9 = (bf16[128,256]{1,0:T(8,128)(2,1)S(1)}, bf16[128,256]{1,0:T(8,128)(2,1)}, u32[]{:S(2)}) copy-start(bf16[128,256]{1,0:T(8,128)(2,1)} %refs_11_.3) | copy-start | bytes 196612
  13.2 4.9 %copy-start.12 = (bf16[128,128]{1,0:T(8,128)(2,1)S(1)}, bf16[128,128]{1,0:T(8,128)(2,1)}, u32[]{:S(2)}) copy-start(bf16[128,128]{1,0:T(8,128)(2,1)} %refs_12_.3) | copy-start | bytes 98308
  13.2 4.9 %copy-start.13 = (bf16[128,128]{1,0:T(8,128)(2,1)S(1)}, bf16[128,128]{1,0:T(8,128)(2,1)}, u32[]{:S(2)}) copy-start(bf16[128,128]{1,0:T(8,128)(2,1)} %refs_13_.1) | copy-start | bytes 98308
  (1 other events, 0.7 us)
where the time goes:
time: 20.5 us; the launch traced here: 20.3 us
  starting transfers between devices  11.1 us (54%)
  Pallas kernels  7.24 us (35%)
  between operations  0.91 us (4%)
  local copies, waits for them, and re-layouts  0.81 us (4%)
  waiting for transfers between devices  0.27 us (1%)
    ppermute x6, starting transfers between devices, swap(): return lax.ppermute(array, 'axial', [(i, i ^ r) for i in range(n)])  11.1 us
    pallas_call x4, Pallas kernels, call(): pl.pallas_call(kernel, out_shape=out_shape, in_specs=[vmem] * len(args),...  7.24 us
    unnamed x38, local copies, waits for them, and re-layouts  0.81 us
  transfers between devices with their start and end apart: 6, of which 1 were waited for; matrix products, arithmetic and copies ran while one was open for 0% of the time, Pallas kernels for 23%

commit v1 on v0

--- a/solution.py
+++ b/solution.py
@@ -218,8 +218,8 @@
 F32 = jnp.float32
 SMALL_ROWS = 16
 FLOPS = 3 * 10**9
-PACKET_ORDER = (3, 2, 1)
-PAIR_ORDER = (2, 1, 3)
+PACKET_ORDER = (2, 3, 1)
+PAIR_ORDER = (3, 1, 2)
 
 
 def mul(lhs, rhs, over=((1,), (0,))):
@@ -399,6 +399,53 @@
         )
     mixed = (jnp.concatenate(groups, axis=0) * gate).astype(BF16)
     align = (one + mul(mixed, col_out[...])).astype(BF16)
+    align_ref[...] = align
+
+    opm = normal(align.astype(F32)).astype(BF16)
+    opm = mul(opm, lift[...], ((1,), (1,))).astype(BF16)
+    hidden = MEAN_HIDDEN_SIZE
+    deep = hidden * count
+    spread = zero_one(
+        iota((2 * hidden, deep), 1) // count == iota((2 * hidden, deep), 0)
+    )
+    left = mul(opm, spread)
+    left = jnp.where(
+        iota((tokens, deep), 0) % count == iota((tokens, deep), 1) % count, left, 0.0
+    ).astype(BF16)
+    gather = zero_one(iota((residues, tokens), 1) // count == iota((residues, tokens), 0))
+    left = mul(gather, left).astype(BF16)
+    right = opm[:, hidden:]
+    for c in range(0, hidden, 2):
+        pair_w = jnp.concatenate(
+            [outer_w[(c + k) * hidden : (c + k + 1) * hidden, :] for k in range(2)], axis=1
+        )
+        part = mul(right, pair_w)
+        lifted[c], lifted[c + 1] = part[:, :pair_width], part[:, pair_width:]
+    for j in range(0, residues, 2):
+        part = jnp.concatenate(
+            [
+                lifted[:, (j + k) * count : (j + k + 1) * count, :].reshape(deep, pair_width)
+                for k in range(2)
+            ],
+            axis=1,
+        )
+        part = mul(left, part.astype(BF16)) * (1.0 / count)
+        update_ref[j], update_ref[j + 1] = part[:, :pair_width], part[:, pair_width:]
+
+
+def pair_kernel(*refs):
+    pairs, packets, update, align, column, pair, own_mask = refs[:3], refs[3:6], *refs[6:11]
+    proj, gates, gate_out, w_out, align_ref, out_ref = refs[11:17]
+    state, one, right_at, left_at, valid = refs[17:]
+    res_dev, residues, width = pair.shape
+    per = (packets[0].shape[0] - SMALL_ROWS) // residues
+    me = lax.axis_index("axial")
+    own_valid = own_mask[...].astype(F32)
+    for packet, r in zip((None, *packets), (0, *PACKET_ORDER)):
+        shown = split_small(packet, residues, res_dev, per)[1] if r else own_valid
+        valid[pl.ds(pl.multiple_of((me ^ r) * res_dev, res_dev), res_dev), :] = shown
+    tokens, features = align.shape
+    count = tokens // residues
     own = count * res_dev
     row_at, lane_at = iota((own, tokens), 0), iota((own, tokens), 1)
     sequence = row_at // res_dev
@@ -410,50 +457,8 @@
         lane_at
         == (row_at % res_dev + me * res_dev) * count + where_is * per + sequence % per
     )
-    align_ref[...] = mul(pick, align).reshape(count, res_dev, width).astype(BF16)
-
-    opm = normal(align.astype(F32)).astype(BF16)
-    opm = mul(opm, lift[...], ((1,), (1,))).astype(BF16)
-    hidden = MEAN_HIDDEN_SIZE
-    deep = hidden * count
-    spread = zero_one(
-        iota((2 * hidden, deep), 1) // count == iota((2 * hidden, deep), 0)
-    )
-    left = mul(opm, spread)
-    left = jnp.where(
-        iota((tokens, deep), 0) % count == iota((tokens, deep), 1) % count, left, 0.0
-    ).astype(BF16)
-    gather = zero_one(iota((residues, tokens), 1) // count == iota((residues, tokens), 0))
-    left = mul(gather, left).astype(BF16)
-    right = opm[:, hidden:]
-    for c in range(0, hidden, 2):
-        pair_w = jnp.concatenate(
-            [outer_w[(c + k) * hidden : (c + k + 1) * hidden, :] for k in range(2)], axis=1
-        )
-        part = mul(right, pair_w)
-        lifted[c], lifted[c + 1] = part[:, :pair_width], part[:, pair_width:]
-    for j in range(0, residues, 2):
-        part = jnp.concatenate(
-            [
-                lifted[:, (j + k) * count : (j + k + 1) * count, :].reshape(deep, pair_width)
-                for k in range(2)
-            ],
-            axis=1,
-        )
-        part = mul(left, part.astype(BF16)) * (1.0 / count)
-        update_ref[j], update_ref[j + 1] = part[:, :pair_width], part[:, pair_width:]
-
-
-def pair_kernel(*refs):
-    pairs, packets, update, column, pair, own_mask = refs[:3], refs[3:6], *refs[6:10]
-    proj, gates, gate_out, w_out, out_ref, state, one, right_at, left_at, valid = refs[10:]
-    res_dev, residues, width = pair.shape
-    per = (packets[0].shape[0] - SMALL_ROWS) // residues
-    me = lax.axis_index("axial")
-    own_valid = own_mask[...].astype(F32)
-    for packet, r in zip((None, *packets), (0, *PACKET_ORDER)):
-        shown = split_small(packet, residues, res_dev, per)[1] if r else own_valid
-        valid[pl.ds(pl.multiple_of((me ^ r) * res_dev, res_dev), res_dev), :] = shown
+    align_ref[...] = mul(pick, align[...]).reshape(count, res_dev, features).astype(BF16)
+
     size = res_dev * residues
     for block, r in zip((pair, *pairs), (0, *PAIR_ORDER)):
         state[pl.ds(pl.multiple_of((me ^ r) * size, size), size), :] = (
@@ -569,10 +574,10 @@
     packets = [swap(packet, r, n) for r in PACKET_ORDER]
     _, later = lax.optimization_barrier((packet, pair_state))
     pairs = [swap(later, r, n) for r in PAIR_ORDER]
-    alignment, update = call(
+    align, update = call(
         functools.partial(msa_kernel, n, res_dev),
         (
-            jax.ShapeDtypeStruct((count, res_dev, width), BF16),
+            jax.ShapeDtypeStruct((count * residues, width), BF16),
             jax.ShapeDtypeStruct((residues, residues, pair_width), F32),
         ),
         [
@@ -593,9 +598,12 @@
         tensor_mean_lift_matrix.T,
         outer_product_output_weight,
     )
-    pair_output = call(
+    return call(
         pair_kernel,
-        jax.ShapeDtypeStruct((res_dev, residues, pair_width), BF16),
+        (
+            jax.ShapeDtypeStruct((count, res_dev, width), BF16),
+            jax.ShapeDtypeStruct((res_dev, residues, pair_width), BF16),
+        ),
         [
             pltpu.VMEM((residues * residues, pair_width), F32),
             pltpu.VMEM((residues * residues, pair_width), F32),
@@ -607,6 +615,7 @@
         *pairs,
         *packets,
         update,
+        align,
         column,
         pair_state,
         pair_valid_mask,
@@ -615,7 +624,6 @@
         triangle_output_gate,
         triangle_output_weight,
     )
-    return (alignment, pair_output)
 
 
 def local(homolog_activity, homolog_symbol_ids, residue_present_mask, pair_state, *others):

time: 20.5 us -> 20.1 us (0.980)
  starting transfers between devices: 11.1 us -> 10.1 us
  Pallas kernels: 7.24 us -> 7.69 us
    ppermute x6, starting transfers between devices: 11.1 us -> 10.1 us  [swap(): return lax.ppermute(array, 'axial', [(i, i ^ r) for i in range(n)])]
    pallas_call x4, Pallas kernels: 7.24 us -> 7.69 us  [call(): pl.pallas_call(kernel, out_shape=out_shape, in_specs=[vmem] * len(args),...]
  transfers between devices with their start and end apart: 6 -> 6, of which waited for: 1 -> 1; matrix products, arithmetic and copies ran while one was open for 0% -> 0% of each run, Pallas kernels for 23% -> 25%
where the time goes in v1:
time: 20.1 us; the launch traced here: 19.9 us
  starting transfers between devices  10.1 us (50%)
  Pallas kernels  7.69 us (38%)
  between operations  0.93 us (5%)
  local copies, waits for them, and re-layouts  0.82 us (4%)
  waiting for transfers between devices  0.43 us (2%)
    ppermute x6, starting transfers between devices, swap(): return lax.ppermute(array, 'axial', [(i, i ^ r) for i in range(n)])  10.1 us
    pallas_call x4, Pallas kernels, call(): pl.pallas_call(kernel, out_shape=out_shape, in_specs=[vmem] * len(args),...  7.69 us
    unnamed x38, local copies, waits for them, and re-layouts  0.82 us
    ppermute x6, waiting for transfers between devices, swap(): return lax.ppermute(array, 'axial', [(i, i ^ r) for i in range(n)])  0.43 us
  transfers between devices with their start and end apart: 6, of which 1 were waited for; matrix products, arithmetic and copies ran while one was open for 0% of the time, Pallas kernels for 25%

profile of v1, /device:TPU:0, one launch (start us, length us, event | category | flops | bytes accessed | tf_op | source)
XLA Modules:
  0.0 19.9 jit_solution(74569640535623031)
XLA Ops:
  0.7 0.1 shard_map.194
  0.7 0.0 copy-start.15
  0.8 0.0 copy-start.17
  0.8 0.0 copy-start.18
  0.8 0.6 %copy-done.10 = bf16[2,32,256]{2,1,0:T(8,128)(2,1)S(1)} copy-done((bf16[2,32,256]{2,1,0:T(8,128)(2,1)S(1)}, bf16[2,32,256]{2,1,0:T(8,128)(2,1)}, u32[]{:S(2)}) %copy-start.10) | copy-done | bytes 32792
  1.4 0.1 copy-done.7
  1.5 0.0 copy-start
  1.5 0.0 copy-start.1
  1.6 0.0 copy-start.4
  1.6 0.0 copy-start.5
  1.6 0.0 copy-start.11
  1.6 0.0 copy-start.14
  1.6 0.4 %shard_map.195 = (bf16[80,256]{1,0:T(8,128)(2,1)S(1)}, f32[32,256]{1,0:T(8,128)S(1)}) custom-call(bf16[8,32,128]{2,1,0:T(8,128)(2,1)S(1)} %copy-done.7, bf16[8,128]{1,0:T(8,128)(2,1)S(1)} %bitcast.4, s32[8,32]{1,0:T(8,128)S(1)} %copy-done.15, s32[2,32]{1,0:T(2,128)S(1)} %copy-done.17, bf16[2,32,256]{2,1,0:T(8,128)(2,1)S(1)} %copy-done.10, ...), custom_call_target="tpu_custom_call" | custom-call | flops 3000000000 | tf_op jit(solution)/shard_map/pallas_call | solution.py:508
  2.0 4.1 %collective-permute-start.3 = (bf16[80,256]{1,0:T(8,128)(2,1)S(1)}, bf16[80,256]{1,0:T(8,128)(2,1)S(1)}, u32[]{:S(2)}, u32[]{:S(2)}) collective-permute-start(bf16[80,256]{1,0:T(8,128)(2,1)S(1)} %get-tuple-element.11.refs_0_), channel_id=1, source_target_pairs={{0,2},{1,3},{2,0},{3,1},{4,6},{5,7},{6,4},{7,5},{8,10},{9,11},{10,... | collective-permute-start | bytes 122888 | tf_op jit(solution)/shard_map/ppermute | solution.py:520
  6.1 1.3 %collective-permute-start.4 = (bf16[80,256]{1,0:T(8,128)(2,1)S(1)}, bf16[80,256]{1,0:T(8,128)(2,1)S(1)}, u32[]{:S(2)}, u32[]{:S(2)}) collective-permute-start(bf16[80,256]{1,0:T(8,128)(2,1)S(1)} %get-tuple-element.11.refs_0_), channel_id=1, source_target_pairs={{0,3},{1,2},{2,1},{3,0},{4,7},{5,6},{6,5},{7,4},{8,11},{9,10},{10,... | collective-permute-start | bytes 122888 | tf_op jit(solution)/shard_map/ppermute | solution.py:520
  7.5 0.2 %collective-permute-start.5 = (bf16[80,256]{1,0:T(8,128)(2,1)S(1)}, bf16[80,256]{1,0:T(8,128)(2,1)S(1)}, u32[]{:S(2)}, u32[]{:S(2)}) collective-permute-start(bf16[80,256]{1,0:T(8,128)(2,1)S(1)} %get-tuple-element.11.refs_0_), channel_id=1, source_target_pairs={{0,1},{1,0},{2,3},{3,2},{4,5},{5,4},{6,7},{7,6},{8,9},{9,8},{10,11... | collective-permute-start | bytes 122888 | tf_op jit(solution)/shard_map/ppermute | solution.py:520
  7.7 2.9 %collective-permute-start = (bf16[8,32,128]{2,1,0:T(8,128)(2,1)S(1)}, bf16[8,32,128]{2,1,0:T(8,128)(2,1)S(1)}, u32[]{:S(2)}, u32[]{:S(2)}) collective-permute-start(bf16[8,32,128]{2,1,0:T(8,128)(2,1)S(1)} %copy-done.7), channel_id=1, source_target_pairs={{0,3},{1,2},{2,1},{3,0},{4,7},{5,6},{6,5},{7,4},{8,11},{9,10},{10,... | collective-permute-start | bytes 196616 | tf_op jit(solution)/shard_map/ppermute | solution.py:520
  10.6 0.5 %collective-permute-start.1 = (bf16[8,32,128]{2,1,0:T(8,128)(2,1)S(1)}, bf16[8,32,128]{2,1,0:T(8,128)(2,1)S(1)}, u32[]{:S(2)}, u32[]{:S(2)}) collective-permute-start(bf16[8,32,128]{2,1,0:T(8,128)(2,1)S(1)} %copy-done.7), channel_id=1, source_target_pairs={{0,1},{1,0},{2,3},{3,2},{4,5},{5,4},{6,7},{7,6},{8,9},{9,8},{10,11... | collective-permute-start | bytes 196616 | tf_op jit(solution)/shard_map/ppermute | solution.py:520
  11.1 1.0 %collective-permute-start.2 = (bf16[8,32,128]{2,1,0:T(8,128)(2,1)S(1)}, bf16[8,32,128]{2,1,0:T(8,128)(2,1)S(1)}, u32[]{:S(2)}, u32[]{:S(2)}) collective-permute-start(bf16[8,32,128]{2,1,0:T(8,128)(2,1)S(1)} %copy-done.7), channel_id=1, source_target_pairs={{0,2},{1,3},{2,0},{3,1},{4,6},{5,7},{6,4},{7,5},{8,10},{9,11},{10,... | collective-permute-start | bytes 196616 | tf_op jit(solution)/shard_map/ppermute | solution.py:520
  12.1 0.4 %collective-permute-done.4.refs_2_.refs_4_ = bf16[80,256]{1,0:T(8,128)(2,1)S(1)} collective-permute-done((bf16[80,256]{1,0:T(8,128)(2,1)S(1)}, bf16[80,256]{1,0:T(8,128)(2,1)S(1)}, u32[]{:S(2)}, u32[]{:S(2)}) %collective-permute-start.4) | collective-permute-done | bytes 40992 | tf_op jit(solution)/shard_map/ppermute | solution.py:520
  12.6 0.0 copy-start.8
  12.6 0.0 copy-start.13
  12.6 5.0 %shard_map.196 = (bf16[256,256]{1,0:T(8,128)(2,1)S(1)}, f32[32,32,128]{2,1,0:T(8,128)S(1)}) custom-call(bf16[80,256]{1,0:T(8,128)(2,1)S(1)} %get-tuple-element.11.refs_0_, bf16[80,256]{1,0:T(8,128)(2,1)S(1)} %collective-permute-done.3.refs_1_.refs_3_, bf16[80,256]{1,0:T(8,128)(2,1)S(1)} %collective-permute-done.4.refs_2_.refs_4_, ...), custom_call_target="tpu_custom_call" | custom-call | flops 3000000000 | tf_op jit(solution)/shard_map/pallas_call | solution.py:508
  17.8 2.2 %shard_map.197 = (bf16[8,8,256]{2,1,0:T(8,128)(2,1)}, bf16[8,32,128]{2,1,0:T(8,128)(2,1)}) custom-call(bf16[8,32,128]{2,1,0:T(8,128)(2,1)S(1)} %collective-permute-done.refs_0_, bf16[8,32,128]{2,1,0:T(8,128)(2,1)S(1)} %collective-permute-done.1.refs_1_, bf16[8,32,128]{2,1,0:T(8,128)(2,1)S(1)} %collective-permute-done.2.refs_2_, ...), custom_call_target="tpu_custom_call" | custom-call | flops 3000000000 | tf_op jit(solution)/shard_map/pallas_call | solution.py:508
  (30 shorter events, 0.1 us)
Async XLA Ops:
  0.6 0.8 %copy-start.10 = (bf16[2,32,256]{2,1,0:T(8,128)(2,1)S(1)}, bf16[2,32,256]{2,1,0:T(8,128)(2,1)}, u32[]{:S(2)}) copy-start(bf16[2,32,256]{2,1,0:T(8,128)(2,1)} %refs_4_.1) | copy-start | bytes 98308
  0.6 0.8 %copy-start.7 = (bf16[8,32,128]{2,1,0:T(8,128)(2,1)S(1)}, bf16[8,32,128]{2,1,0:T(8,128)(2,1)}, u32[]{:S(2)}) copy-start(bf16[8,32,128]{2,1,0:T(8,128)(2,1)} %refs_9_.3) | copy-start | bytes 196612
  0.6 0.8 %copy-start.16 = (bf16[128,8]{0,1:T(8,128)(2,1)S(1)}, bf16[128,8]{0,1:T(8,128)(2,1)}, u32[]{:S(2)}) copy-start(bf16[128,8]{0,1:T(8,128)(2,1)} %param.27) | copy-start | bytes 6148
  0.7 0.8 %copy-start.15 = (s32[8,32]{1,0:T(8,128)S(1)}, s32[8,32]{1,0:T(8,128)}, u32[]{:S(2)}) copy-start(s32[8,32]{1,0:T(8,128)} %refs_10_.3) | copy-start | bytes 3076
  0.8 0.7 %copy-start.17 = (s32[2,32]{1,0:T(2,128)S(1)}, s32[2,32]{1,0:T(2,128)}, u32[]{:S(2)}) copy-start(s32[2,32]{1,0:T(2,128)} %refs_3_.1) | copy-start | bytes 772
  1.5 11.0 %copy-start = (bf16[256,768]{1,0:T(8,128)(2,1)S(1)}, bf16[256,768]{1,0:T(8,128)(2,1)}, u32[]{:S(2)}) copy-start(bf16[256,768]{1,0:T(8,128)(2,1)} %refs_8_.1) | copy-start | bytes 1179652
  1.5 11.0 %copy-start.1 = (bf16[256,768]{1,0:T(8,128)(2,1)S(1)}, bf16[256,768]{1,0:T(8,128)(2,1)}, u32[]{:S(2)}) copy-start(bf16[256,768]{1,0:T(8,128)(2,1)} %refs_11_.2) | copy-start | bytes 1179652
  1.5 11.0 %copy-start.2 = (bf16[1024,128]{1,0:T(8,128)(2,1)S(1)}, bf16[1024,128]{1,0:T(8,128)(2,1)}, u32[]{:S(2)}) copy-start(bf16[1024,128]{1,0:T(8,128)(2,1)} %refs_14_.2) | copy-start | bytes 786436
  1.5 11.0 %copy-start.3 = (bf16[256,256]{1,0:T(8,128)(2,1)S(1)}, bf16[256,256]{1,0:T(8,128)(2,1)}, u32[]{:S(2)}) copy-start(bf16[256,256]{1,0:T(8,128)(2,1)} %refs_7_.1) | copy-start | bytes 393220
  1.6 11.0 %copy-start.4 = (bf16[256,256]{1,0:T(8,128)(2,1)S(1)}, bf16[256,256]{1,0:T(8,128)(2,1)}, u32[]{:S(2)}) copy-start(bf16[256,256]{1,0:T(8,128)(2,1)} %refs_9_.2) | copy-start | bytes 393220
  1.6 11.0 %copy-start.5 = (bf16[256,256]{1,0:T(8,128)(2,1)S(1)}, bf16[256,256]{1,0:T(8,128)(2,1)}, u32[]{:S(2)}) copy-start(bf16[256,256]{1,0:T(8,128)(2,1)} %refs_10_.2) | copy-start | bytes 393220
  1.6 11.0 %copy-start.6 = (bf16[256,256]{1,0:T(8,128)(2,1)S(1)}, bf16[256,256]{1,0:T(8,128)(2,1)}, u32[]{:S(2)}) copy-start(bf16[256,256]{1,0:T(8,128)(2,1)} %refs_12_.2) | copy-start | bytes 393220
  1.6 11.0 %copy-start.11 = (bf16[256,64]{0,1:T(8,128)(2,1)S(1)}, bf16[256,64]{0,1:T(8,128)(2,1)}, u32[]{:S(2)}) copy-start(bf16[256,64]{0,1:T(8,128)(2,1)} %param.32) | copy-start | bytes 98308
  1.6 11.0 %copy-start.14 = (bf16[23,256]{1,0:T(8,128)(2,1)S(1)}, bf16[23,256]{1,0:T(8,128)(2,1)}, u32[]{:S(2)}) copy-start(bf16[23,256]{1,0:T(8,128)(2,1)} %refs_6_.1) | copy-start | bytes 35332
  2.0 9.1 %collective-permute-start.3 = (bf16[80,256]{1,0:T(8,128)(2,1)S(1)}, bf16[80,256]{1,0:T(8,128)(2,1)S(1)}, u32[]{:S(2)}, u32[]{:S(2)}) collective-permute-start(bf16[80,256]{1,0:T(8,128)(2,1)S(1)} %get-tuple-element.11.refs_0_), channel_id=1, source_target_pairs={{0,2},{1,3},{2,0},{3,1},{4,6},{5,7},{6,4},{7,5},{8,10},{9,11},{10,... | collective-permute-start | bytes 122888 | tf_op jit(solution)/shard_map/ppermute | solution.py:520
  6.1 6.4 %collective-permute-start.4 = (bf16[80,256]{1,0:T(8,128)(2,1)S(1)}, bf16[80,256]{1,0:T(8,128)(2,1)S(1)}, u32[]{:S(2)}, u32[]{:S(2)}) collective-permute-start(bf16[80,256]{1,0:T(8,128)(2,1)S(1)} %get-tuple-element.11.refs_0_), channel_id=1, source_target_pairs={{0,3},{1,2},{2,1},{3,0},{4,7},{5,6},{6,5},{7,4},{8,11},{9,10},{10,... | collective-permute-start | bytes 122888 | tf_op jit(solution)/shard_map/ppermute | solution.py:520
  7.5 5.0 %collective-permute-start.5 = (bf16[80,256]{1,0:T(8,128)(2,1)S(1)}, bf16[80,256]{1,0:T(8,128)(2,1)S(1)}, u32[]{:S(2)}, u32[]{:S(2)}) collective-permute-start(bf16[80,256]{1,0:T(8,128)(2,1)S(1)} %get-tuple-element.11.refs_0_), channel_id=1, source_target_pairs={{0,1},{1,0},{2,3},{3,2},{4,5},{5,4},{6,7},{7,6},{8,9},{9,8},{10,11... | collective-permute-start | bytes 122888 | tf_op jit(solution)/shard_map/ppermute | solution.py:520
  7.7 10.0 %collective-permute-start = (bf16[8,32,128]{2,1,0:T(8,128)(2,1)S(1)}, bf16[8,32,128]{2,1,0:T(8,128)(2,1)S(1)}, u32[]{:S(2)}, u32[]{:S(2)}) collective-permute-start(bf16[8,32,128]{2,1,0:T(8,128)(2,1)S(1)} %copy-done.7), channel_id=1, source_target_pairs={{0,3},{1,2},{2,1},{3,0},{4,7},{5,6},{6,5},{7,4},{8,11},{9,10},{10,... | collective-permute-start | bytes 196616 | tf_op jit(solution)/shard_map/ppermute | solution.py:520
  10.6 7.1 %collective-permute-start.1 = (bf16[8,32,128]{2,1,0:T(8,128)(2,1)S(1)}, bf16[8,32,128]{2,1,0:T(8,128)(2,1)S(1)}, u32[]{:S(2)}, u32[]{:S(2)}) collective-permute-start(bf16[8,32,128]{2,1,0:T(8,128)(2,1)S(1)} %copy-done.7), channel_id=1, source_target_pairs={{0,1},{1,0},{2,3},{3,2},{4,5},{5,4},{6,7},{7,6},{8,9},{9,8},{10,11... | collective-permute-start | bytes 196616 | tf_op jit(solution)/shard_map/ppermute | solution.py:520
  11.1 6.6 %collective-permute-start.2 = (bf16[8,32,128]{2,1,0:T(8,128)(2,1)S(1)}, bf16[8,32,128]{2,1,0:T(8,128)(2,1)S(1)}, u32[]{:S(2)}, u32[]{:S(2)}) collective-permute-start(bf16[8,32,128]{2,1,0:T(8,128)(2,1)S(1)} %copy-done.7), channel_id=1, source_target_pairs={{0,2},{1,3},{2,0},{3,1},{4,6},{5,7},{6,4},{7,5},{8,10},{9,11},{10,... | collective-permute-start | bytes 196616 | tf_op jit(solution)/shard_map/ppermute | solution.py:520
  12.6 5.1 %copy-start.8 = (bf16[128,256]{1,0:T(8,128)(2,1)S(1)}, bf16[128,256]{1,0:T(8,128)(2,1)}, u32[]{:S(2)}) copy-start(bf16[128,256]{1,0:T(8,128)(2,1)} %refs_11_.3) | copy-start | bytes 196612
  12.6 5.1 %copy-start.9 = (bf16[128,256]{1,0:T(8,128)(2,1)S(1)}, bf16[128,256]{1,0:T(8,128)(2,1)}, u32[]{:S(2)}) copy-start(bf16[128,256]{1,0:T(8,128)(2,1)} %refs_12_.3) | copy-start | bytes 196612
  12.6 5.1 %copy-start.12 = (bf16[128,128]{1,0:T(8,128)(2,1)S(1)}, bf16[128,128]{1,0:T(8,128)(2,1)}, u32[]{:S(2)}) copy-start(bf16[128,128]{1,0:T(8,128)(2,1)} %refs_13_.1) | copy-start | bytes 98308
  12.6 5.1 %copy-start.13 = (bf16[128,128]{1,0:T(8,128)(2,1)S(1)}, bf16[128,128]{1,0:T(8,128)(2,1)}, u32[]{:S(2)}) copy-start(bf16[128,128]{1,0:T(8,128)(2,1)} %refs_14_.3) | copy-start | bytes 98308
  (1 other events, 0.7 us)

commit v2 on v0

--- a/solution.py
+++ b/solution.py
@@ -218,8 +218,8 @@
 F32 = jnp.float32
 SMALL_ROWS = 16
 FLOPS = 3 * 10**9
-PACKET_ORDER = (3, 2, 1)
-PAIR_ORDER = (2, 1, 3)
+PACKET_ORDER = (2, 3, 1)
+PAIR_ORDER = (3, 1, 2)
 
 
 def mul(lhs, rhs, over=((1,), (0,))):

time: 20.5 us -> 19.6 us (0.956)
  starting transfers between devices: 11.1 us -> 10.1 us
    ppermute x6, starting transfers between devices: 11.1 us -> 10.1 us  [swap(): return lax.ppermute(array, 'axial', [(i, i ^ r) for i in range(n)])]
  transfers between devices with their start and end apart: 6 -> 6, of which waited for: 1 -> 1; matrix products, arithmetic and copies ran while one was open for 0% -> 0% of each run, Pallas kernels for 23% -> 24%
where the time goes in v2:
time: 19.6 us; the launch traced here: 19.5 us
  starting transfers between devices  10.1 us (52%)
  Pallas kernels  7.24 us (37%)
  between operations  0.93 us (5%)
  local copies, waits for them, and re-layouts  0.81 us (4%)
  waiting for transfers between devices  0.43 us (2%)
    ppermute x6, starting transfers between devices, swap(): return lax.ppermute(array, 'axial', [(i, i ^ r) for i in range(n)])  10.1 us
    pallas_call x4, Pallas kernels, call(): pl.pallas_call(kernel, out_shape=out_shape, in_specs=[vmem] * len(args),...  7.24 us
    unnamed x38, local copies, waits for them, and re-layouts  0.81 us
    ppermute x6, waiting for transfers between devices, swap(): return lax.ppermute(array, 'axial', [(i, i ^ r) for i in range(n)])  0.43 us
  transfers between devices with their start and end apart: 6, of which 1 were waited for; matrix products, arithmetic and copies ran while one was open for 0% of the time, Pallas kernels for 24%

profile of v2, /device:TPU:0, one launch (start us, length us, event | category | flops | bytes accessed | tf_op | source)
XLA Modules:
  0.0 19.5 jit_solution(513110891694553968)
XLA Ops:
  0.7 0.1 shard_map.194
  0.7 0.0 copy-start.15
  0.8 0.0 copy-start.17
  0.8 0.0 copy-start.18
  0.8 0.7 %copy-done.7 = bf16[8,32,128]{2,1,0:T(8,128)(2,1)S(1)} copy-done((bf16[8,32,128]{2,1,0:T(8,128)(2,1)S(1)}, bf16[8,32,128]{2,1,0:T(8,128)(2,1)}, u32[]{:S(2)}) %copy-start.7) | copy-done | bytes 65560
  1.5 0.0 copy-start
  1.5 0.0 copy-start.1
  1.5 0.0 copy-start.2
  1.5 0.0 copy-start.3
  1.5 0.0 copy-start.4
  1.6 0.0 copy-start.5
  1.6 0.0 copy-start.6
  1.6 0.4 %shard_map.195 = (bf16[80,256]{1,0:T(8,128)(2,1)S(1)}, f32[32,256]{1,0:T(8,128)S(1)}) custom-call(bf16[8,32,128]{2,1,0:T(8,128)(2,1)S(1)} %copy-done.7, bf16[8,128]{1,0:T(8,128)(2,1)S(1)} %bitcast.4, s32[8,32]{1,0:T(8,128)S(1)} %copy-done.15, s32[2,32]{1,0:T(2,128)S(1)} %copy-done.17, bf16[2,32,256]{2,1,0:T(8,128)(2,1)S(1)} %copy-done.10, ...), custom_call_target="tpu_custom_call" | custom-call | flops 3000000000 | tf_op jit(solution)/shard_map/pallas_call | solution.py:503
  2.0 4.1 %collective-permute-start = (bf16[80,256]{1,0:T(8,128)(2,1)S(1)}, bf16[80,256]{1,0:T(8,128)(2,1)S(1)}, u32[]{:S(2)}, u32[]{:S(2)}) collective-permute-start(bf16[80,256]{1,0:T(8,128)(2,1)S(1)} %get-tuple-element.11.refs_0_), channel_id=1, source_target_pairs={{0,2},{1,3},{2,0},{3,1},{4,6},{5,7},{6,4},{7,5},{8,10},{9,11},{10,... | collective-permute-start | bytes 122888 | tf_op jit(solution)/shard_map/ppermute | solution.py:515
  6.1 1.3 %collective-permute-start.1 = (bf16[80,256]{1,0:T(8,128)(2,1)S(1)}, bf16[80,256]{1,0:T(8,128)(2,1)S(1)}, u32[]{:S(2)}, u32[]{:S(2)}) collective-permute-start(bf16[80,256]{1,0:T(8,128)(2,1)S(1)} %get-tuple-element.11.refs_0_), channel_id=1, source_target_pairs={{0,3},{1,2},{2,1},{3,0},{4,7},{5,6},{6,5},{7,4},{8,11},{9,10},{10,... | collective-permute-start | bytes 122888 | tf_op jit(solution)/shard_map/ppermute | solution.py:515
  7.5 0.2 %collective-permute-start.2 = (bf16[80,256]{1,0:T(8,128)(2,1)S(1)}, bf16[80,256]{1,0:T(8,128)(2,1)S(1)}, u32[]{:S(2)}, u32[]{:S(2)}) collective-permute-start(bf16[80,256]{1,0:T(8,128)(2,1)S(1)} %get-tuple-element.11.refs_0_), channel_id=1, source_target_pairs={{0,1},{1,0},{2,3},{3,2},{4,5},{5,4},{6,7},{7,6},{8,9},{9,8},{10,11... | collective-permute-start | bytes 122888 | tf_op jit(solution)/shard_map/ppermute | solution.py:515
  7.7 2.9 %collective-permute-start.3 = (bf16[8,32,128]{2,1,0:T(8,128)(2,1)S(1)}, bf16[8,32,128]{2,1,0:T(8,128)(2,1)S(1)}, u32[]{:S(2)}, u32[]{:S(2)}) collective-permute-start(bf16[8,32,128]{2,1,0:T(8,128)(2,1)S(1)} %copy-done.7), channel_id=1, source_target_pairs={{0,3},{1,2},{2,1},{3,0},{4,7},{5,6},{6,5},{7,4},{8,11},{9,10},{10,... | collective-permute-start | bytes 196616 | tf_op jit(solution)/shard_map/ppermute | solution.py:515
  10.6 0.5 %collective-permute-start.4 = (bf16[8,32,128]{2,1,0:T(8,128)(2,1)S(1)}, bf16[8,32,128]{2,1,0:T(8,128)(2,1)S(1)}, u32[]{:S(2)}, u32[]{:S(2)}) collective-permute-start(bf16[8,32,128]{2,1,0:T(8,128)(2,1)S(1)} %copy-done.7), channel_id=1, source_target_pairs={{0,1},{1,0},{2,3},{3,2},{4,5},{5,4},{6,7},{7,6},{8,9},{9,8},{10,11... | collective-permute-start | bytes 196616 | tf_op jit(solution)/shard_map/ppermute | solution.py:515
  11.1 1.0 %collective-permute-start.5 = (bf16[8,32,128]{2,1,0:T(8,128)(2,1)S(1)}, bf16[8,32,128]{2,1,0:T(8,128)(2,1)S(1)}, u32[]{:S(2)}, u32[]{:S(2)}) collective-permute-start(bf16[8,32,128]{2,1,0:T(8,128)(2,1)S(1)} %copy-done.7), channel_id=1, source_target_pairs={{0,2},{1,3},{2,0},{3,1},{4,6},{5,7},{6,4},{7,5},{8,10},{9,11},{10,... | collective-permute-start | bytes 196616 | tf_op jit(solution)/shard_map/ppermute | solution.py:515
  12.1 0.4 %collective-permute-done.1.refs_2_.refs_4_ = bf16[80,256]{1,0:T(8,128)(2,1)S(1)} collective-permute-done((bf16[80,256]{1,0:T(8,128)(2,1)S(1)}, bf16[80,256]{1,0:T(8,128)(2,1)S(1)}, u32[]{:S(2)}, u32[]{:S(2)}) %collective-permute-start.1) | collective-permute-done | bytes 40992 | tf_op jit(solution)/shard_map/ppermute | solution.py:515
  12.6 0.0 copy-start.8
  12.6 0.0 copy-start.9
  12.6 4.6 %shard_map.196 = (bf16[8,8,256]{2,1,0:T(8,128)(2,1)}, f32[32,32,128]{2,1,0:T(8,128)S(1)}) custom-call(bf16[80,256]{1,0:T(8,128)(2,1)S(1)} %get-tuple-element.11.refs_0_, bf16[80,256]{1,0:T(8,128)(2,1)S(1)} %collective-permute-done.refs_1_.refs_3_, bf16[80,256]{1,0:T(8,128)(2,1)S(1)} %collective-permute-done.1.refs_2_.refs_4_, ...), custom_call_target="tpu_custom_call" | custom-call | flops 3000000000 | tf_op jit(solution)/shard_map/pallas_call | solution.py:503
  17.3 2.2 %shard_map.197 = bf16[8,32,128]{2,1,0:T(8,128)(2,1)} custom-call(bf16[8,32,128]{2,1,0:T(8,128)(2,1)S(1)} %collective-permute-done.3.refs_0_, bf16[8,32,128]{2,1,0:T(8,128)(2,1)S(1)} %collective-permute-done.4.refs_1_, bf16[8,32,128]{2,1,0:T(8,128)(2,1)S(1)} %collective-permute-done.5.refs_2_, bf16[80,256]{1,0:T(8,128)(2,1)S(1)} %collective-permute-done.refs_1_.refs_3_, ...), custom_call_target="tpu_custom_call" | custom-call | flops 3000000000 | tf_op jit(solution)/shard_map/pallas_call | solution.py:503
  (30 shorter events, 0.1 us)
Async XLA Ops:
  0.6 0.8 %copy-start.7 = (bf16[8,32,128]{2,1,0:T(8,128)(2,1)S(1)}, bf16[8,32,128]{2,1,0:T(8,128)(2,1)}, u32[]{:S(2)}) copy-start(bf16[8,32,128]{2,1,0:T(8,128)(2,1)} %refs_8_.3) | copy-start | bytes 196612
  0.6 0.8 %copy-start.10 = (bf16[2,32,256]{2,1,0:T(8,128)(2,1)S(1)}, bf16[2,32,256]{2,1,0:T(8,128)(2,1)}, u32[]{:S(2)}) copy-start(bf16[2,32,256]{2,1,0:T(8,128)(2,1)} %refs_4_.1) | copy-start | bytes 98308
  0.6 0.8 %copy-start.16 = (bf16[128,8]{0,1:T(8,128)(2,1)S(1)}, bf16[128,8]{0,1:T(8,128)(2,1)}, u32[]{:S(2)}) copy-start(bf16[128,8]{0,1:T(8,128)(2,1)} %param.27) | copy-start | bytes 6148
  0.7 0.7 %copy-start.15 = (s32[8,32]{1,0:T(8,128)S(1)}, s32[8,32]{1,0:T(8,128)}, u32[]{:S(2)}) copy-start(s32[8,32]{1,0:T(8,128)} %refs_9_.3) | copy-start | bytes 3076
  0.8 0.7 %copy-start.17 = (s32[2,32]{1,0:T(2,128)S(1)}, s32[2,32]{1,0:T(2,128)}, u32[]{:S(2)}) copy-start(s32[2,32]{1,0:T(2,128)} %refs_3_.1) | copy-start | bytes 772
  1.5 11.0 %copy-start = (bf16[256,768]{1,0:T(8,128)(2,1)S(1)}, bf16[256,768]{1,0:T(8,128)(2,1)}, u32[]{:S(2)}) copy-start(bf16[256,768]{1,0:T(8,128)(2,1)} %refs_8_.2) | copy-start | bytes 1179652
  1.5 11.0 %copy-start.1 = (bf16[256,768]{1,0:T(8,128)(2,1)S(1)}, bf16[256,768]{1,0:T(8,128)(2,1)}, u32[]{:S(2)}) copy-start(bf16[256,768]{1,0:T(8,128)(2,1)} %refs_11_.2) | copy-start | bytes 1179652
  1.5 11.0 %copy-start.2 = (bf16[1024,128]{1,0:T(8,128)(2,1)S(1)}, bf16[1024,128]{1,0:T(8,128)(2,1)}, u32[]{:S(2)}) copy-start(bf16[1024,128]{1,0:T(8,128)(2,1)} %refs_14_.1) | copy-start | bytes 786436
  1.5 11.0 %copy-start.3 = (bf16[256,256]{1,0:T(8,128)(2,1)S(1)}, bf16[256,256]{1,0:T(8,128)(2,1)}, u32[]{:S(2)}) copy-start(bf16[256,256]{1,0:T(8,128)(2,1)} %refs_7_.1) | copy-start | bytes 393220
  1.5 11.0 %copy-start.4 = (bf16[256,256]{1,0:T(8,128)(2,1)S(1)}, bf16[256,256]{1,0:T(8,128)(2,1)}, u32[]{:S(2)}) copy-start(bf16[256,256]{1,0:T(8,128)(2,1)} %refs_9_.2) | copy-start | bytes 393220
  1.6 11.0 %copy-start.5 = (bf16[256,256]{1,0:T(8,128)(2,1)S(1)}, bf16[256,256]{1,0:T(8,128)(2,1)}, u32[]{:S(2)}) copy-start(bf16[256,256]{1,0:T(8,128)(2,1)} %refs_10_.2) | copy-start | bytes 393220
  1.6 11.0 %copy-start.6 = (bf16[256,256]{1,0:T(8,128)(2,1)S(1)}, bf16[256,256]{1,0:T(8,128)(2,1)}, u32[]{:S(2)}) copy-start(bf16[256,256]{1,0:T(8,128)(2,1)} %refs_12_.2) | copy-start | bytes 393220
  1.6 11.0 %copy-start.11 = (bf16[256,64]{0,1:T(8,128)(2,1)S(1)}, bf16[256,64]{0,1:T(8,128)(2,1)}, u32[]{:S(2)}) copy-start(bf16[256,64]{0,1:T(8,128)(2,1)} %param.32) | copy-start | bytes 98308
  1.6 11.0 %copy-start.14 = (bf16[23,256]{1,0:T(8,128)(2,1)S(1)}, bf16[23,256]{1,0:T(8,128)(2,1)}, u32[]{:S(2)}) copy-start(bf16[23,256]{1,0:T(8,128)(2,1)} %refs_6_.1) | copy-start | bytes 35332
  2.0 9.1 %collective-permute-start = (bf16[80,256]{1,0:T(8,128)(2,1)S(1)}, bf16[80,256]{1,0:T(8,128)(2,1)S(1)}, u32[]{:S(2)}, u32[]{:S(2)}) collective-permute-start(bf16[80,256]{1,0:T(8,128)(2,1)S(1)} %get-tuple-element.11.refs_0_), channel_id=1, source_target_pairs={{0,2},{1,3},{2,0},{3,1},{4,6},{5,7},{6,4},{7,5},{8,10},{9,11},{10,... | collective-permute-start | bytes 122888 | tf_op jit(solution)/shard_map/ppermute | solution.py:515
  6.1 6.4 %collective-permute-start.1 = (bf16[80,256]{1,0:T(8,128)(2,1)S(1)}, bf16[80,256]{1,0:T(8,128)(2,1)S(1)}, u32[]{:S(2)}, u32[]{:S(2)}) collective-permute-start(bf16[80,256]{1,0:T(8,128)(2,1)S(1)} %get-tuple-element.11.refs_0_), channel_id=1, source_target_pairs={{0,3},{1,2},{2,1},{3,0},{4,7},{5,6},{6,5},{7,4},{8,11},{9,10},{10,... | collective-permute-start | bytes 122888 | tf_op jit(solution)/shard_map/ppermute | solution.py:515
  7.5 5.0 %collective-permute-start.2 = (bf16[80,256]{1,0:T(8,128)(2,1)S(1)}, bf16[80,256]{1,0:T(8,128)(2,1)S(1)}, u32[]{:S(2)}, u32[]{:S(2)}) collective-permute-start(bf16[80,256]{1,0:T(8,128)(2,1)S(1)} %get-tuple-element.11.refs_0_), channel_id=1, source_target_pairs={{0,1},{1,0},{2,3},{3,2},{4,5},{5,4},{6,7},{7,6},{8,9},{9,8},{10,11... | collective-permute-start | bytes 122888 | tf_op jit(solution)/shard_map/ppermute | solution.py:515
  7.7 9.6 %collective-permute-start.3 = (bf16[8,32,128]{2,1,0:T(8,128)(2,1)S(1)}, bf16[8,32,128]{2,1,0:T(8,128)(2,1)S(1)}, u32[]{:S(2)}, u32[]{:S(2)}) collective-permute-start(bf16[8,32,128]{2,1,0:T(8,128)(2,1)S(1)} %copy-done.7), channel_id=1, source_target_pairs={{0,3},{1,2},{2,1},{3,0},{4,7},{5,6},{6,5},{7,4},{8,11},{9,10},{10,... | collective-permute-start | bytes 196616 | tf_op jit(solution)/shard_map/ppermute | solution.py:515
  10.6 6.7 %collective-permute-start.4 = (bf16[8,32,128]{2,1,0:T(8,128)(2,1)S(1)}, bf16[8,32,128]{2,1,0:T(8,128)(2,1)S(1)}, u32[]{:S(2)}, u32[]{:S(2)}) collective-permute-start(bf16[8,32,128]{2,1,0:T(8,128)(2,1)S(1)} %copy-done.7), channel_id=1, source_target_pairs={{0,1},{1,0},{2,3},{3,2},{4,5},{5,4},{6,7},{7,6},{8,9},{9,8},{10,11... | collective-permute-start | bytes 196616 | tf_op jit(solution)/shard_map/ppermute | solution.py:515
  11.1 6.2 %collective-permute-start.5 = (bf16[8,32,128]{2,1,0:T(8,128)(2,1)S(1)}, bf16[8,32,128]{2,1,0:T(8,128)(2,1)S(1)}, u32[]{:S(2)}, u32[]{:S(2)}) collective-permute-start(bf16[8,32,128]{2,1,0:T(8,128)(2,1)S(1)} %copy-done.7), channel_id=1, source_target_pairs={{0,2},{1,3},{2,0},{3,1},{4,6},{5,7},{6,4},{7,5},{8,10},{9,11},{10,... | collective-permute-start | bytes 196616 | tf_op jit(solution)/shard_map/ppermute | solution.py:515
  12.6 4.7 %copy-start.8 = (bf16[128,256]{1,0:T(8,128)(2,1)S(1)}, bf16[128,256]{1,0:T(8,128)(2,1)}, u32[]{:S(2)}) copy-start(bf16[128,256]{1,0:T(8,128)(2,1)} %refs_10_.3) | copy-start | bytes 196612
  12.6 4.7 %copy-start.9 = (bf16[128,256]{1,0:T(8,128)(2,1)S(1)}, bf16[128,256]{1,0:T(8,128)(2,1)}, u32[]{:S(2)}) copy-start(bf16[128,256]{1,0:T(8,128)(2,1)} %refs_11_.3) | copy-start | bytes 196612
  12.6 4.7 %copy-start.12 = (bf16[128,128]{1,0:T(8,128)(2,1)S(1)}, bf16[128,128]{1,0:T(8,128)(2,1)}, u32[]{:S(2)}) copy-start(bf16[128,128]{1,0:T(8,128)(2,1)} %refs_12_.3) | copy-start | bytes 98308
  12.6 4.7 %copy-start.13 = (bf16[128,128]{1,0:T(8,128)(2,1)S(1)}, bf16[128,128]{1,0:T(8,128)(2,1)}, u32[]{:S(2)}) copy-start(bf16[128,128]{1,0:T(8,128)(2,1)} %refs_13_.1) | copy-start | bytes 98308
  (1 other events, 0.7 us)

commit v3 on v2

--- a/solution.py
+++ b/solution.py
@@ -342,16 +342,16 @@
 
     place = iota((FOCUS_TOTAL * res_dev, lanes), 0)
     place = (place // res_dev) * residues + place % res_dev - iota(place.shape, 1)
-    bias = jnp.zeros((residues, lanes), F32)
-    rows = []
+    parts, places, acts, ids = [], [], [], []
     for packet, r in zip(packets, (0, *PACKET_ORDER)):
         part, _, all_ids = split_small(packet, residues, res_dev, per)
-        bias += mul(part.astype(BF16), zero_one(place == -(me ^ r) * res_dev))
-        for q in range(per):
-            hot = zero_one(iota((kinds, residues), 0).astype(F32) == all_ids[q : q + 1])
-            act = packet[q * residues : (q + 1) * residues, :].astype(F32)
-            rows.append(act + mul(hot, table[...], ((0,), (0,))))
-    zero = jnp.concatenate(rows, axis=0)
+        parts.append(part)
+        places.append(zero_one(place == -(me ^ r) * res_dev))
+        acts.append(packet[: per * residues, :])
+        ids += [all_ids[q : q + 1] for q in range(per)]
+    bias = mul(jnp.concatenate(parts, axis=1).astype(BF16), jnp.concatenate(places, axis=0))
+    hot = zero_one(iota((kinds, tokens), 0).astype(F32) == jnp.concatenate(ids, axis=1))
+    zero = jnp.concatenate(acts, axis=0).astype(F32) + mul(hot, table[...], ((0,), (0,)))
     extra = bias + hidden_keys[...]
     masks = head_masks(width)
 
@@ -379,17 +379,20 @@
     for g in range(tokens // group):
         here = slice(g * group, (g + 1) * group)
         all_weights, all_values = [], []
-        for mask in masks:
-            full = mul(keys[here], query[here] * mask, ((1,), (1,)))
-            scores = full[:count]
-            for b in range(1, sites):
-                scores = jnp.where(block_of == b, full[b * count : (b + 1) * count], scores)
-            weights = column_softmax(scores)
-            weights = jnp.concatenate(
-                [jnp.where(block_of == b, weights, 0.0) for b in range(sites)], axis=0
-            )
-            all_weights.append(weights.astype(BF16))
-            all_values.append(values[here] * mask)
+        for h in range(0, FOCUS_TOTAL, 2):
+            two = jnp.concatenate([query[here] * masks[h + k] for k in range(2)], axis=0)
+            two = mul(keys[here], two, ((1,), (1,)))
+            for k in range(2):
+                full = two[:, k * group : (k + 1) * group]
+                scores = full[:count]
+                for b in range(1, sites):
+                    scores = jnp.where(block_of == b, full[b * count : (b + 1) * count], scores)
+                weights = column_softmax(scores)
+                weights = jnp.concatenate(
+                    [jnp.where(block_of == b, weights, 0.0) for b in range(sites)], axis=0
+                )
+                all_weights.append(weights.astype(BF16))
+                all_values.append(values[here] * masks[h + k])
         groups.append(
             mul(
                 jnp.concatenate(all_weights, axis=0),

time: 19.6 us -> 19.7 us (level)
  no operation moved by 1% of the time
where the time goes in v3:
time: 19.7 us; the launch traced here: 19.5 us
  starting transfers between devices  10.1 us (51%)
  Pallas kernels  7.3 us (37%)
  between operations  0.93 us (5%)
  local copies, waits for them, and re-layouts  0.81 us (4%)
  waiting for transfers between devices  0.43 us (2%)
    ppermute x6, starting transfers between devices, swap(): return lax.ppermute(array, 'axial', [(i, i ^ r) for i in range(n)])  10.1 us
    pallas_call x4, Pallas kernels, call(): pl.pallas_call(kernel, out_shape=out_shape, in_specs=[vmem] * len(args),...  7.3 us
    unnamed x38, local copies, waits for them, and re-layouts  0.81 us
    ppermute x6, waiting for transfers between devices, swap(): return lax.ppermute(array, 'axial', [(i, i ^ r) for i in range(n)])  0.43 us
  transfers between devices with their start and end apart: 6, of which 1 were waited for; matrix products, arithmetic and copies ran while one was open for 0% of the time, Pallas kernels for 24%

profile of v3, /device:TPU:0, one launch (start us, length us, event | category | flops | bytes accessed | tf_op | source)
XLA Modules:
  0.0 19.5 jit_solution(8027190921949652408)
XLA Ops:
  0.7 0.1 shard_map.194
  0.7 0.0 copy-start.15
  0.8 0.0 copy-start.17
  0.8 0.0 copy-start.18
  0.8 0.7 %copy-done.7 = bf16[8,32,128]{2,1,0:T(8,128)(2,1)S(1)} copy-done((bf16[8,32,128]{2,1,0:T(8,128)(2,1)S(1)}, bf16[8,32,128]{2,1,0:T(8,128)(2,1)}, u32[]{:S(2)}) %copy-start.7) | copy-done | bytes 65560
  1.5 0.0 copy-start
  1.5 0.0 copy-start.1
  1.5 0.0 copy-start.2
  1.5 0.0 copy-start.3
  1.5 0.0 copy-start.4
  1.6 0.0 copy-start.5
  1.6 0.0 copy-start.14
  1.6 0.4 %shard_map.195 = (bf16[80,256]{1,0:T(8,128)(2,1)S(1)}, f32[32,256]{1,0:T(8,128)S(1)}) custom-call(bf16[8,32,128]{2,1,0:T(8,128)(2,1)S(1)} %copy-done.7, bf16[8,128]{1,0:T(8,128)(2,1)S(1)} %bitcast.4, s32[8,32]{1,0:T(8,128)S(1)} %copy-done.15, s32[2,32]{1,0:T(2,128)S(1)} %copy-done.17, bf16[2,32,256]{2,1,0:T(8,128)(2,1)S(1)} %copy-done.10, ...), custom_call_target="tpu_custom_call" | custom-call | flops 3000000000 | tf_op jit(solution)/shard_map/pallas_call | solution.py:506
  2.0 4.1 %collective-permute-start = (bf16[80,256]{1,0:T(8,128)(2,1)S(1)}, bf16[80,256]{1,0:T(8,128)(2,1)S(1)}, u32[]{:S(2)}, u32[]{:S(2)}) collective-permute-start(bf16[80,256]{1,0:T(8,128)(2,1)S(1)} %get-tuple-element.11.refs_0_), channel_id=1, source_target_pairs={{0,2},{1,3},{2,0},{3,1},{4,6},{5,7},{6,4},{7,5},{8,10},{9,11},{10,... | collective-permute-start | bytes 122888 | tf_op jit(solution)/shard_map/ppermute | solution.py:518
  6.1 1.3 %collective-permute-start.1 = (bf16[80,256]{1,0:T(8,128)(2,1)S(1)}, bf16[80,256]{1,0:T(8,128)(2,1)S(1)}, u32[]{:S(2)}, u32[]{:S(2)}) collective-permute-start(bf16[80,256]{1,0:T(8,128)(2,1)S(1)} %get-tuple-element.11.refs_0_), channel_id=1, source_target_pairs={{0,3},{1,2},{2,1},{3,0},{4,7},{5,6},{6,5},{7,4},{8,11},{9,10},{10,... | collective-permute-start | bytes 122888 | tf_op jit(solution)/shard_map/ppermute | solution.py:518
  7.5 0.2 %collective-permute-start.2 = (bf16[80,256]{1,0:T(8,128)(2,1)S(1)}, bf16[80,256]{1,0:T(8,128)(2,1)S(1)}, u32[]{:S(2)}, u32[]{:S(2)}) collective-permute-start(bf16[80,256]{1,0:T(8,128)(2,1)S(1)} %get-tuple-element.11.refs_0_), channel_id=1, source_target_pairs={{0,1},{1,0},{2,3},{3,2},{4,5},{5,4},{6,7},{7,6},{8,9},{9,8},{10,11... | collective-permute-start | bytes 122888 | tf_op jit(solution)/shard_map/ppermute | solution.py:518
  7.7 2.9 %collective-permute-start.3 = (bf16[8,32,128]{2,1,0:T(8,128)(2,1)S(1)}, bf16[8,32,128]{2,1,0:T(8,128)(2,1)S(1)}, u32[]{:S(2)}, u32[]{:S(2)}) collective-permute-start(bf16[8,32,128]{2,1,0:T(8,128)(2,1)S(1)} %copy-done.7), channel_id=1, source_target_pairs={{0,3},{1,2},{2,1},{3,0},{4,7},{5,6},{6,5},{7,4},{8,11},{9,10},{10,... | collective-permute-start | bytes 196616 | tf_op jit(solution)/shard_map/ppermute | solution.py:518
  10.6 0.5 %collective-permute-start.4 = (bf16[8,32,128]{2,1,0:T(8,128)(2,1)S(1)}, bf16[8,32,128]{2,1,0:T(8,128)(2,1)S(1)}, u32[]{:S(2)}, u32[]{:S(2)}) collective-permute-start(bf16[8,32,128]{2,1,0:T(8,128)(2,1)S(1)} %copy-done.7), channel_id=1, source_target_pairs={{0,1},{1,0},{2,3},{3,2},{4,5},{5,4},{6,7},{7,6},{8,9},{9,8},{10,11... | collective-permute-start | bytes 196616 | tf_op jit(solution)/shard_map/ppermute | solution.py:518
  11.1 1.0 %collective-permute-start.5 = (bf16[8,32,128]{2,1,0:T(8,128)(2,1)S(1)}, bf16[8,32,128]{2,1,0:T(8,128)(2,1)S(1)}, u32[]{:S(2)}, u32[]{:S(2)}) collective-permute-start(bf16[8,32,128]{2,1,0:T(8,128)(2,1)S(1)} %copy-done.7), channel_id=1, source_target_pairs={{0,2},{1,3},{2,0},{3,1},{4,6},{5,7},{6,4},{7,5},{8,10},{9,11},{10,... | collective-permute-start | bytes 196616 | tf_op jit(solution)/shard_map/ppermute | solution.py:518
  12.1 0.4 %collective-permute-done.1.refs_2_.refs_4_ = bf16[80,256]{1,0:T(8,128)(2,1)S(1)} collective-permute-done((bf16[80,256]{1,0:T(8,128)(2,1)S(1)}, bf16[80,256]{1,0:T(8,128)(2,1)S(1)}, u32[]{:S(2)}, u32[]{:S(2)}) %collective-permute-start.1) | collective-permute-done | bytes 40992 | tf_op jit(solution)/shard_map/ppermute | solution.py:518
  12.6 0.0 copy-start.8
  12.6 0.0 copy-start.9
  12.6 4.7 %shard_map.196 = (bf16[8,8,256]{2,1,0:T(8,128)(2,1)}, f32[32,32,128]{2,1,0:T(8,128)S(1)}) custom-call(bf16[80,256]{1,0:T(8,128)(2,1)S(1)} %get-tuple-element.11.refs_0_, bf16[80,256]{1,0:T(8,128)(2,1)S(1)} %collective-permute-done.refs_1_.refs_3_, bf16[80,256]{1,0:T(8,128)(2,1)S(1)} %collective-permute-done.1.refs_2_.refs_4_, ...), custom_call_target="tpu_custom_call" | custom-call | flops 3000000000 | tf_op jit(solution)/shard_map/pallas_call | solution.py:506
  17.4 2.2 %shard_map.197 = bf16[8,32,128]{2,1,0:T(8,128)(2,1)} custom-call(bf16[8,32,128]{2,1,0:T(8,128)(2,1)S(1)} %collective-permute-done.3.refs_0_, bf16[8,32,128]{2,1,0:T(8,128)(2,1)S(1)} %collective-permute-done.4.refs_1_, bf16[8,32,128]{2,1,0:T(8,128)(2,1)S(1)} %collective-permute-done.5.refs_2_, bf16[80,256]{1,0:T(8,128)(2,1)S(1)} %collective-permute-done.refs_1_.refs_3_, ...), custom_call_target="tpu_custom_call" | custom-call | flops 3000000000 | tf_op jit(solution)/shard_map/pallas_call | solution.py:506
  (30 shorter events, 0.1 us)
Async XLA Ops:
  0.6 0.8 %copy-start.7 = (bf16[8,32,128]{2,1,0:T(8,128)(2,1)S(1)}, bf16[8,32,128]{2,1,0:T(8,128)(2,1)}, u32[]{:S(2)}) copy-start(bf16[8,32,128]{2,1,0:T(8,128)(2,1)} %refs_8_.3) | copy-start | bytes 196612
  0.6 0.8 %copy-start.10 = (bf16[2,32,256]{2,1,0:T(8,128)(2,1)S(1)}, bf16[2,32,256]{2,1,0:T(8,128)(2,1)}, u32[]{:S(2)}) copy-start(bf16[2,32,256]{2,1,0:T(8,128)(2,1)} %refs_4_.1) | copy-start | bytes 98308
  0.6 0.8 %copy-start.16 = (bf16[128,8]{0,1:T(8,128)(2,1)S(1)}, bf16[128,8]{0,1:T(8,128)(2,1)}, u32[]{:S(2)}) copy-start(bf16[128,8]{0,1:T(8,128)(2,1)} %param.27) | copy-start | bytes 6148
  0.7 0.7 %copy-start.15 = (s32[8,32]{1,0:T(8,128)S(1)}, s32[8,32]{1,0:T(8,128)}, u32[]{:S(2)}) copy-start(s32[8,32]{1,0:T(8,128)} %refs_9_.3) | copy-start | bytes 3076
  0.8 0.7 %copy-start.17 = (s32[2,32]{1,0:T(2,128)S(1)}, s32[2,32]{1,0:T(2,128)}, u32[]{:S(2)}) copy-start(s32[2,32]{1,0:T(2,128)} %refs_3_.1) | copy-start | bytes 772
  1.5 11.0 %copy-start = (bf16[256,768]{1,0:T(8,128)(2,1)S(1)}, bf16[256,768]{1,0:T(8,128)(2,1)}, u32[]{:S(2)}) copy-start(bf16[256,768]{1,0:T(8,128)(2,1)} %refs_8_.2) | copy-start | bytes 1179652
  1.5 11.0 %copy-start.1 = (bf16[256,768]{1,0:T(8,128)(2,1)S(1)}, bf16[256,768]{1,0:T(8,128)(2,1)}, u32[]{:S(2)}) copy-start(bf16[256,768]{1,0:T(8,128)(2,1)} %refs_11_.2) | copy-start | bytes 1179652
  1.5 11.0 %copy-start.2 = (bf16[1024,128]{1,0:T(8,128)(2,1)S(1)}, bf16[1024,128]{1,0:T(8,128)(2,1)}, u32[]{:S(2)}) copy-start(bf16[1024,128]{1,0:T(8,128)(2,1)} %refs_14_.1) | copy-start | bytes 786436
  1.5 11.0 %copy-start.3 = (bf16[256,256]{1,0:T(8,128)(2,1)S(1)}, bf16[256,256]{1,0:T(8,128)(2,1)}, u32[]{:S(2)}) copy-start(bf16[256,256]{1,0:T(8,128)(2,1)} %refs_7_.1) | copy-start | bytes 393220
  1.5 11.0 %copy-start.4 = (bf16[256,256]{1,0:T(8,128)(2,1)S(1)}, bf16[256,256]{1,0:T(8,128)(2,1)}, u32[]{:S(2)}) copy-start(bf16[256,256]{1,0:T(8,128)(2,1)} %refs_9_.2) | copy-start | bytes 393220
  1.6 11.0 %copy-start.5 = (bf16[256,256]{1,0:T(8,128)(2,1)S(1)}, bf16[256,256]{1,0:T(8,128)(2,1)}, u32[]{:S(2)}) copy-start(bf16[256,256]{1,0:T(8,128)(2,1)} %refs_10_.2) | copy-start | bytes 393220
  1.6 11.0 %copy-start.6 = (bf16[256,256]{1,0:T(8,128)(2,1)S(1)}, bf16[256,256]{1,0:T(8,128)(2,1)}, u32[]{:S(2)}) copy-start(bf16[256,256]{1,0:T(8,128)(2,1)} %refs_12_.2) | copy-start | bytes 393220
  1.6 11.0 %copy-start.11 = (bf16[256,64]{0,1:T(8,128)(2,1)S(1)}, bf16[256,64]{0,1:T(8,128)(2,1)}, u32[]{:S(2)}) copy-start(bf16[256,64]{0,1:T(8,128)(2,1)} %param.32) | copy-start | bytes 98308
  1.6 11.0 %copy-start.14 = (bf16[23,256]{1,0:T(8,128)(2,1)S(1)}, bf16[23,256]{1,0:T(8,128)(2,1)}, u32[]{:S(2)}) copy-start(bf16[23,256]{1,0:T(8,128)(2,1)} %refs_6_.1) | copy-start | bytes 35332
  2.0 9.1 %collective-permute-start = (bf16[80,256]{1,0:T(8,128)(2,1)S(1)}, bf16[80,256]{1,0:T(8,128)(2,1)S(1)}, u32[]{:S(2)}, u32[]{:S(2)}) collective-permute-start(bf16[80,256]{1,0:T(8,128)(2,1)S(1)} %get-tuple-element.11.refs_0_), channel_id=1, source_target_pairs={{0,2},{1,3},{2,0},{3,1},{4,6},{5,7},{6,4},{7,5},{8,10},{9,11},{10,... | collective-permute-start | bytes 122888 | tf_op jit(solution)/shard_map/ppermute | solution.py:518
  6.1 6.4 %collective-permute-start.1 = (bf16[80,256]{1,0:T(8,128)(2,1)S(1)}, bf16[80,256]{1,0:T(8,128)(2,1)S(1)}, u32[]{:S(2)}, u32[]{:S(2)}) collective-permute-start(bf16[80,256]{1,0:T(8,128)(2,1)S(1)} %get-tuple-element.11.refs_0_), channel_id=1, source_target_pairs={{0,3},{1,2},{2,1},{3,0},{4,7},{5,6},{6,5},{7,4},{8,11},{9,10},{10,... | collective-permute-start | bytes 122888 | tf_op jit(solution)/shard_map/ppermute | solution.py:518
  7.5 5.0 %collective-permute-start.2 = (bf16[80,256]{1,0:T(8,128)(2,1)S(1)}, bf16[80,256]{1,0:T(8,128)(2,1)S(1)}, u32[]{:S(2)}, u32[]{:S(2)}) collective-permute-start(bf16[80,256]{1,0:T(8,128)(2,1)S(1)} %get-tuple-element.11.refs_0_), channel_id=1, source_target_pairs={{0,1},{1,0},{2,3},{3,2},{4,5},{5,4},{6,7},{7,6},{8,9},{9,8},{10,11... | collective-permute-start | bytes 122888 | tf_op jit(solution)/shard_map/ppermute | solution.py:518
  7.7 9.6 %collective-permute-start.3 = (bf16[8,32,128]{2,1,0:T(8,128)(2,1)S(1)}, bf16[8,32,128]{2,1,0:T(8,128)(2,1)S(1)}, u32[]{:S(2)}, u32[]{:S(2)}) collective-permute-start(bf16[8,32,128]{2,1,0:T(8,128)(2,1)S(1)} %copy-done.7), channel_id=1, source_target_pairs={{0,3},{1,2},{2,1},{3,0},{4,7},{5,6},{6,5},{7,4},{8,11},{9,10},{10,... | collective-permute-start | bytes 196616 | tf_op jit(solution)/shard_map/ppermute | solution.py:518
  10.6 6.7 %collective-permute-start.4 = (bf16[8,32,128]{2,1,0:T(8,128)(2,1)S(1)}, bf16[8,32,128]{2,1,0:T(8,128)(2,1)S(1)}, u32[]{:S(2)}, u32[]{:S(2)}) collective-permute-start(bf16[8,32,128]{2,1,0:T(8,128)(2,1)S(1)} %copy-done.7), channel_id=1, source_target_pairs={{0,1},{1,0},{2,3},{3,2},{4,5},{5,4},{6,7},{7,6},{8,9},{9,8},{10,11... | collective-permute-start | bytes 196616 | tf_op jit(solution)/shard_map/ppermute | solution.py:518
  11.1 6.3 %collective-permute-start.5 = (bf16[8,32,128]{2,1,0:T(8,128)(2,1)S(1)}, bf16[8,32,128]{2,1,0:T(8,128)(2,1)S(1)}, u32[]{:S(2)}, u32[]{:S(2)}) collective-permute-start(bf16[8,32,128]{2,1,0:T(8,128)(2,1)S(1)} %copy-done.7), channel_id=1, source_target_pairs={{0,2},{1,3},{2,0},{3,1},{4,6},{5,7},{6,4},{7,5},{8,10},{9,11},{10,... | collective-permute-start | bytes 196616 | tf_op jit(solution)/shard_map/ppermute | solution.py:518
  12.6 4.8 %copy-start.8 = (bf16[128,256]{1,0:T(8,128)(2,1)S(1)}, bf16[128,256]{1,0:T(8,128)(2,1)}, u32[]{:S(2)}) copy-start(bf16[128,256]{1,0:T(8,128)(2,1)} %refs_10_.3) | copy-start | bytes 196612
  12.6 4.8 %copy-start.9 = (bf16[128,256]{1,0:T(8,128)(2,1)S(1)}, bf16[128,256]{1,0:T(8,128)(2,1)}, u32[]{:S(2)}) copy-start(bf16[128,256]{1,0:T(8,128)(2,1)} %refs_11_.3) | copy-start | bytes 196612
  12.6 4.8 %copy-start.12 = (bf16[128,128]{1,0:T(8,128)(2,1)S(1)}, bf16[128,128]{1,0:T(8,128)(2,1)}, u32[]{:S(2)}) copy-start(bf16[128,128]{1,0:T(8,128)(2,1)} %refs_12_.3) | copy-start | bytes 98308
  12.6 4.8 %copy-start.13 = (bf16[128,128]{1,0:T(8,128)(2,1)S(1)}, bf16[128,128]{1,0:T(8,128)(2,1)}, u32[]{:S(2)}) copy-start(bf16[128,128]{1,0:T(8,128)(2,1)} %refs_13_.1) | copy-start | bytes 98308
  (1 other events, 0.7 us)

commit v4 on v2

--- a/solution.py
+++ b/solution.py
@@ -426,22 +426,25 @@
     gather = zero_one(iota((residues, tokens), 1) // count == iota((residues, tokens), 0))
     left = mul(gather, left).astype(BF16)
     right = opm[:, hidden:]
-    for c in range(0, hidden, 2):
-        pair_w = jnp.concatenate(
-            [outer_w[(c + k) * hidden : (c + k + 1) * hidden, :] for k in range(2)], axis=1
-        )
-        part = mul(right, pair_w)
-        lifted[c], lifted[c + 1] = part[:, :pair_width], part[:, pair_width:]
-    for j in range(0, residues, 2):
+
+    def lift_two(c, _):
+        rows = outer_w[pl.ds(pl.multiple_of(c * 2 * hidden, 2 * hidden), 2 * hidden), :]
+        part = mul(right, jnp.concatenate([rows[:hidden], rows[hidden:]], axis=1))
+        lifted[2 * c], lifted[2 * c + 1] = part[:, :pair_width], part[:, pair_width:]
+        return _
+
+    def update_two(j, _):
+        rows = lifted[:, pl.ds(pl.multiple_of(j * 2 * count, 2 * count), 2 * count), :]
         part = jnp.concatenate(
-            [
-                lifted[:, (j + k) * count : (j + k + 1) * count, :].reshape(deep, pair_width)
-                for k in range(2)
-            ],
+            [rows[:, k * count : (k + 1) * count].reshape(deep, pair_width) for k in range(2)],
             axis=1,
         )
         part = mul(left, part.astype(BF16)) * (1.0 / count)
-        update_ref[j], update_ref[j + 1] = part[:, :pair_width], part[:, pair_width:]
+        update_ref[2 * j], update_ref[2 * j + 1] = part[:, :pair_width], part[:, pair_width:]
+        return _
+
+    lax.fori_loop(0, hidden // 2, lift_two, 0, unroll=4)
+    lax.fori_loop(0, residues // 2, update_two, 0, unroll=4)
 
 
 def pair_kernel(*refs):
@@ -488,11 +491,15 @@
     for i in range(res_dev):
         part = left[i * residues : (i + 1) * residues] * shown[:, i * C_TRI : (i + 1) * C_TRI]
         left_at[i * residues : (i + 1) * residues, :] = part.astype(BF16).astype(F32)
+
+    def add_k(k, sums):
+        other = right_at[pl.ds(pl.multiple_of(k * residues, residues), residues), :]
+        return [
+            sums[i] + left_at[pl.ds(i * residues + k, 1), :] * other for i in range(res_dev)
+        ]
+
     sums = [jnp.zeros((residues, C_TRI), F32) for _ in range(res_dev)]
-    for k in range(residues):
-        other = right_at[k * residues : (k + 1) * residues, :]
-        for i in range(res_dev):
-            sums[i] += left_at[i * residues + k : i * residues + k + 1, :] * other
+    sums = lax.fori_loop(0, residues, add_k, sums, unroll=4)
     mixed = normal(jnp.concatenate(sums, axis=0)).astype(BF16)
     result = own + own_gate * mul(mixed, w_out[...])
     out_ref[...] = result.reshape(res_dev, residues, width).astype(BF16)

time: 19.6 us -> 21.4 us (1.092)
  Pallas kernels: 7.24 us -> 9.04 us
    pallas_call x4, Pallas kernels: 7.24 us -> 9.04 us  [call(): pl.pallas_call(kernel, out_shape=out_shape, in_specs=[vmem] * len(args),...]
  transfers between devices with their start and end apart: 6 -> 6, of which waited for: 1 -> 1; matrix products, arithmetic and copies ran while one was open for 0% -> 0% of each run, Pallas kernels for 24% -> 30%
where the time goes in v4:
time: 21.4 us; the launch traced here: 21.3 us
  starting transfers between devices  10.1 us (47%)
  Pallas kernels  9.04 us (42%)
  between operations  0.91 us (4%)
  local copies, waits for them, and re-layouts  0.81 us (4%)
  waiting for transfers between devices  0.43 us (2%)
    ppermute x6, starting transfers between devices, swap(): return lax.ppermute(array, 'axial', [(i, i ^ r) for i in range(n)])  10.1 us
    pallas_call x4, Pallas kernels, call(): pl.pallas_call(kernel, out_shape=out_shape, in_specs=[vmem] * len(args),...  9.04 us
    unnamed x38, local copies, waits for them, and re-layouts  0.81 us
    ppermute x6, waiting for transfers between devices, swap(): return lax.ppermute(array, 'axial', [(i, i ^ r) for i in range(n)])  0.43 us
  transfers between devices with their start and end apart: 6, of which 1 were waited for; matrix products, arithmetic and copies ran while one was open for 0% of the time, Pallas kernels for 30%

profile of v4, /device:TPU:0, one launch (start us, length us, event | category | flops | bytes accessed | tf_op | source)
XLA Modules:
  0.0 21.3 jit_solution(5846150457327448953)
XLA Ops:
  0.7 0.1 shard_map.194
  0.7 0.0 copy-start.15
  0.8 0.0 copy-start.17
  0.8 0.0 copy-start.18
  0.8 0.7 %copy-done.7 = bf16[8,32,128]{2,1,0:T(8,128)(2,1)S(1)} copy-done((bf16[8,32,128]{2,1,0:T(8,128)(2,1)S(1)}, bf16[8,32,128]{2,1,0:T(8,128)(2,1)}, u32[]{:S(2)}) %copy-start.7) | copy-done | bytes 65560
  1.5 0.0 copy-start
  1.5 0.0 copy-start.1
  1.5 0.0 copy-start.2
  1.5 0.0 copy-start.3
  1.5 0.0 copy-start.4
  1.6 0.0 copy-start.11
  1.6 0.0 copy-start.14
  1.6 0.4 %shard_map.195 = (bf16[80,256]{1,0:T(8,128)(2,1)S(1)}, f32[32,256]{1,0:T(8,128)S(1)}) custom-call(bf16[8,32,128]{2,1,0:T(8,128)(2,1)S(1)} %copy-done.7, bf16[8,128]{1,0:T(8,128)(2,1)S(1)} %bitcast.4, s32[8,32]{1,0:T(8,128)S(1)} %copy-done.15, s32[2,32]{1,0:T(2,128)S(1)} %copy-done.17, bf16[2,32,256]{2,1,0:T(8,128)(2,1)S(1)} %copy-done.10, ...), custom_call_target="tpu_custom_call" | custom-call | flops 3000000000 | tf_op jit(solution)/shard_map/pallas_call | solution.py:510
  2.0 4.1 %collective-permute-start = (bf16[80,256]{1,0:T(8,128)(2,1)S(1)}, bf16[80,256]{1,0:T(8,128)(2,1)S(1)}, u32[]{:S(2)}, u32[]{:S(2)}) collective-permute-start(bf16[80,256]{1,0:T(8,128)(2,1)S(1)} %get-tuple-element.11.refs_0_), channel_id=1, source_target_pairs={{0,2},{1,3},{2,0},{3,1},{4,6},{5,7},{6,4},{7,5},{8,10},{9,11},{10,... | collective-permute-start | bytes 122888 | tf_op jit(solution)/shard_map/ppermute | solution.py:522
  6.1 1.3 %collective-permute-start.1 = (bf16[80,256]{1,0:T(8,128)(2,1)S(1)}, bf16[80,256]{1,0:T(8,128)(2,1)S(1)}, u32[]{:S(2)}, u32[]{:S(2)}) collective-permute-start(bf16[80,256]{1,0:T(8,128)(2,1)S(1)} %get-tuple-element.11.refs_0_), channel_id=1, source_target_pairs={{0,3},{1,2},{2,1},{3,0},{4,7},{5,6},{6,5},{7,4},{8,11},{9,10},{10,... | collective-permute-start | bytes 122888 | tf_op jit(solution)/shard_map/ppermute | solution.py:522
  7.5 0.2 %collective-permute-start.2 = (bf16[80,256]{1,0:T(8,128)(2,1)S(1)}, bf16[80,256]{1,0:T(8,128)(2,1)S(1)}, u32[]{:S(2)}, u32[]{:S(2)}) collective-permute-start(bf16[80,256]{1,0:T(8,128)(2,1)S(1)} %get-tuple-element.11.refs_0_), channel_id=1, source_target_pairs={{0,1},{1,0},{2,3},{3,2},{4,5},{5,4},{6,7},{7,6},{8,9},{9,8},{10,11... | collective-permute-start | bytes 122888 | tf_op jit(solution)/shard_map/ppermute | solution.py:522
  7.7 2.9 %collective-permute-start.3 = (bf16[8,32,128]{2,1,0:T(8,128)(2,1)S(1)}, bf16[8,32,128]{2,1,0:T(8,128)(2,1)S(1)}, u32[]{:S(2)}, u32[]{:S(2)}) collective-permute-start(bf16[8,32,128]{2,1,0:T(8,128)(2,1)S(1)} %copy-done.7), channel_id=1, source_target_pairs={{0,3},{1,2},{2,1},{3,0},{4,7},{5,6},{6,5},{7,4},{8,11},{9,10},{10,... | collective-permute-start | bytes 196616 | tf_op jit(solution)/shard_map/ppermute | solution.py:522
  10.6 0.5 %collective-permute-start.4 = (bf16[8,32,128]{2,1,0:T(8,128)(2,1)S(1)}, bf16[8,32,128]{2,1,0:T(8,128)(2,1)S(1)}, u32[]{:S(2)}, u32[]{:S(2)}) collective-permute-start(bf16[8,32,128]{2,1,0:T(8,128)(2,1)S(1)} %copy-done.7), channel_id=1, source_target_pairs={{0,1},{1,0},{2,3},{3,2},{4,5},{5,4},{6,7},{7,6},{8,9},{9,8},{10,11... | collective-permute-start | bytes 196616 | tf_op jit(solution)/shard_map/ppermute | solution.py:522
  11.1 1.0 %collective-permute-start.5 = (bf16[8,32,128]{2,1,0:T(8,128)(2,1)S(1)}, bf16[8,32,128]{2,1,0:T(8,128)(2,1)S(1)}, u32[]{:S(2)}, u32[]{:S(2)}) collective-permute-start(bf16[8,32,128]{2,1,0:T(8,128)(2,1)S(1)} %copy-done.7), channel_id=1, source_target_pairs={{0,2},{1,3},{2,0},{3,1},{4,6},{5,7},{6,4},{7,5},{8,10},{9,11},{10,... | collective-permute-start | bytes 196616 | tf_op jit(solution)/shard_map/ppermute | solution.py:522
  12.1 0.4 %collective-permute-done.1.refs_2_.refs_4_ = bf16[80,256]{1,0:T(8,128)(2,1)S(1)} collective-permute-done((bf16[80,256]{1,0:T(8,128)(2,1)S(1)}, bf16[80,256]{1,0:T(8,128)(2,1)S(1)}, u32[]{:S(2)}, u32[]{:S(2)}) %collective-permute-start.1) | collective-permute-done | bytes 40992 | tf_op jit(solution)/shard_map/ppermute | solution.py:522
  12.6 0.0 copy-start.8
  12.6 0.0 copy-start.13
  12.6 6.3 %shard_map.196 = (bf16[8,8,256]{2,1,0:T(8,128)(2,1)}, f32[32,32,128]{2,1,0:T(8,128)S(1)}) custom-call(bf16[80,256]{1,0:T(8,128)(2,1)S(1)} %get-tuple-element.11.refs_0_, bf16[80,256]{1,0:T(8,128)(2,1)S(1)} %collective-permute-done.refs_1_.refs_3_, bf16[80,256]{1,0:T(8,128)(2,1)S(1)} %collective-permute-done.1.refs_2_.refs_4_, ...), custom_call_target="tpu_custom_call" | custom-call | flops 3000000000 | tf_op jit(solution)/shard_map/pallas_call | solution.py:510
  19.0 2.3 %shard_map.197 = bf16[8,32,128]{2,1,0:T(8,128)(2,1)} custom-call(bf16[8,32,128]{2,1,0:T(8,128)(2,1)S(1)} %collective-permute-done.3.refs_0_, bf16[8,32,128]{2,1,0:T(8,128)(2,1)S(1)} %collective-permute-done.4.refs_1_, bf16[8,32,128]{2,1,0:T(8,128)(2,1)S(1)} %collective-permute-done.5.refs_2_, bf16[80,256]{1,0:T(8,128)(2,1)S(1)} %collective-permute-done.refs_1_.refs_3_, ...), custom_call_target="tpu_custom_call" | custom-call | flops 3000000000 | tf_op jit(solution)/shard_map/pallas_call | solution.py:510
  (30 shorter events, 0.1 us)
Async XLA Ops:
  0.6 0.8 %copy-start.7 = (bf16[8,32,128]{2,1,0:T(8,128)(2,1)S(1)}, bf16[8,32,128]{2,1,0:T(8,128)(2,1)}, u32[]{:S(2)}) copy-start(bf16[8,32,128]{2,1,0:T(8,128)(2,1)} %refs_8_.3) | copy-start | bytes 196612
  0.6 0.8 %copy-start.10 = (bf16[2,32,256]{2,1,0:T(8,128)(2,1)S(1)}, bf16[2,32,256]{2,1,0:T(8,128)(2,1)}, u32[]{:S(2)}) copy-start(bf16[2,32,256]{2,1,0:T(8,128)(2,1)} %refs_4_.1) | copy-start | bytes 98308
  0.6 0.8 %copy-start.16 = (bf16[128,8]{0,1:T(8,128)(2,1)S(1)}, bf16[128,8]{0,1:T(8,128)(2,1)}, u32[]{:S(2)}) copy-start(bf16[128,8]{0,1:T(8,128)(2,1)} %param.27) | copy-start | bytes 6148
  0.7 0.7 %copy-start.15 = (s32[8,32]{1,0:T(8,128)S(1)}, s32[8,32]{1,0:T(8,128)}, u32[]{:S(2)}) copy-start(s32[8,32]{1,0:T(8,128)} %refs_9_.3) | copy-start | bytes 3076
  0.8 0.7 %copy-start.17 = (s32[2,32]{1,0:T(2,128)S(1)}, s32[2,32]{1,0:T(2,128)}, u32[]{:S(2)}) copy-start(s32[2,32]{1,0:T(2,128)} %refs_3_.1) | copy-start | bytes 772
  1.5 11.0 %copy-start = (bf16[256,768]{1,0:T(8,128)(2,1)S(1)}, bf16[256,768]{1,0:T(8,128)(2,1)}, u32[]{:S(2)}) copy-start(bf16[256,768]{1,0:T(8,128)(2,1)} %refs_8_.2) | copy-start | bytes 1179652
  1.5 11.0 %copy-start.1 = (bf16[256,768]{1,0:T(8,128)(2,1)S(1)}, bf16[256,768]{1,0:T(8,128)(2,1)}, u32[]{:S(2)}) copy-start(bf16[256,768]{1,0:T(8,128)(2,1)} %refs_11_.2) | copy-start | bytes 1179652
  1.5 11.0 %copy-start.2 = (bf16[1024,128]{1,0:T(8,128)(2,1)S(1)}, bf16[1024,128]{1,0:T(8,128)(2,1)}, u32[]{:S(2)}) copy-start(bf16[1024,128]{1,0:T(8,128)(2,1)} %refs_14_.1) | copy-start | bytes 786436
  1.5 11.0 %copy-start.3 = (bf16[256,256]{1,0:T(8,128)(2,1)S(1)}, bf16[256,256]{1,0:T(8,128)(2,1)}, u32[]{:S(2)}) copy-start(bf16[256,256]{1,0:T(8,128)(2,1)} %refs_7_.1) | copy-start | bytes 393220
  1.5 11.0 %copy-start.4 = (bf16[256,256]{1,0:T(8,128)(2,1)S(1)}, bf16[256,256]{1,0:T(8,128)(2,1)}, u32[]{:S(2)}) copy-start(bf16[256,256]{1,0:T(8,128)(2,1)} %refs_9_.2) | copy-start | bytes 393220
  1.6 11.0 %copy-start.5 = (bf16[256,256]{1,0:T(8,128)(2,1)S(1)}, bf16[256,256]{1,0:T(8,128)(2,1)}, u32[]{:S(2)}) copy-start(bf16[256,256]{1,0:T(8,128)(2,1)} %refs_10_.2) | copy-start | bytes 393220
  1.6 11.0 %copy-start.6 = (bf16[256,256]{1,0:T(8,128)(2,1)S(1)}, bf16[256,256]{1,0:T(8,128)(2,1)}, u32[]{:S(2)}) copy-start(bf16[256,256]{1,0:T(8,128)(2,1)} %refs_12_.2) | copy-start | bytes 393220
  1.6 11.0 %copy-start.11 = (bf16[256,64]{0,1:T(8,128)(2,1)S(1)}, bf16[256,64]{0,1:T(8,128)(2,1)}, u32[]{:S(2)}) copy-start(bf16[256,64]{0,1:T(8,128)(2,1)} %param.32) | copy-start | bytes 98308
  1.6 11.0 %copy-start.14 = (bf16[23,256]{1,0:T(8,128)(2,1)S(1)}, bf16[23,256]{1,0:T(8,128)(2,1)}, u32[]{:S(2)}) copy-start(bf16[23,256]{1,0:T(8,128)(2,1)} %refs_6_.1) | copy-start | bytes 35332
  2.0 9.1 %collective-permute-start = (bf16[80,256]{1,0:T(8,128)(2,1)S(1)}, bf16[80,256]{1,0:T(8,128)(2,1)S(1)}, u32[]{:S(2)}, u32[]{:S(2)}) collective-permute-start(bf16[80,256]{1,0:T(8,128)(2,1)S(1)} %get-tuple-element.11.refs_0_), channel_id=1, source_target_pairs={{0,2},{1,3},{2,0},{3,1},{4,6},{5,7},{6,4},{7,5},{8,10},{9,11},{10,... | collective-permute-start | bytes 122888 | tf_op jit(solution)/shard_map/ppermute | solution.py:522
  6.1 6.4 %collective-permute-start.1 = (bf16[80,256]{1,0:T(8,128)(2,1)S(1)}, bf16[80,256]{1,0:T(8,128)(2,1)S(1)}, u32[]{:S(2)}, u32[]{:S(2)}) collective-permute-start(bf16[80,256]{1,0:T(8,128)(2,1)S(1)} %get-tuple-element.11.refs_0_), channel_id=1, source_target_pairs={{0,3},{1,2},{2,1},{3,0},{4,7},{5,6},{6,5},{7,4},{8,11},{9,10},{10,... | collective-permute-start | bytes 122888 | tf_op jit(solution)/shard_map/ppermute | solution.py:522
  7.5 5.0 %collective-permute-start.2 = (bf16[80,256]{1,0:T(8,128)(2,1)S(1)}, bf16[80,256]{1,0:T(8,128)(2,1)S(1)}, u32[]{:S(2)}, u32[]{:S(2)}) collective-permute-start(bf16[80,256]{1,0:T(8,128)(2,1)S(1)} %get-tuple-element.11.refs_0_), channel_id=1, source_target_pairs={{0,1},{1,0},{2,3},{3,2},{4,5},{5,4},{6,7},{7,6},{8,9},{9,8},{10,11... | collective-permute-start | bytes 122888 | tf_op jit(solution)/shard_map/ppermute | solution.py:522
  7.7 11.2 %collective-permute-start.3 = (bf16[8,32,128]{2,1,0:T(8,128)(2,1)S(1)}, bf16[8,32,128]{2,1,0:T(8,128)(2,1)S(1)}, u32[]{:S(2)}, u32[]{:S(2)}) collective-permute-start(bf16[8,32,128]{2,1,0:T(8,128)(2,1)S(1)} %copy-done.7), channel_id=1, source_target_pairs={{0,3},{1,2},{2,1},{3,0},{4,7},{5,6},{6,5},{7,4},{8,11},{9,10},{10,... | collective-permute-start | bytes 196616 | tf_op jit(solution)/shard_map/ppermute | solution.py:522
  10.6 8.3 %collective-permute-start.4 = (bf16[8,32,128]{2,1,0:T(8,128)(2,1)S(1)}, bf16[8,32,128]{2,1,0:T(8,128)(2,1)S(1)}, u32[]{:S(2)}, u32[]{:S(2)}) collective-permute-start(bf16[8,32,128]{2,1,0:T(8,128)(2,1)S(1)} %copy-done.7), channel_id=1, source_target_pairs={{0,1},{1,0},{2,3},{3,2},{4,5},{5,4},{6,7},{7,6},{8,9},{9,8},{10,11... | collective-permute-start | bytes 196616 | tf_op jit(solution)/shard_map/ppermute | solution.py:522
  11.1 7.9 %collective-permute-start.5 = (bf16[8,32,128]{2,1,0:T(8,128)(2,1)S(1)}, bf16[8,32,128]{2,1,0:T(8,128)(2,1)S(1)}, u32[]{:S(2)}, u32[]{:S(2)}) collective-permute-start(bf16[8,32,128]{2,1,0:T(8,128)(2,1)S(1)} %copy-done.7), channel_id=1, source_target_pairs={{0,2},{1,3},{2,0},{3,1},{4,6},{5,7},{6,4},{7,5},{8,10},{9,11},{10,... | collective-permute-start | bytes 196616 | tf_op jit(solution)/shard_map/ppermute | solution.py:522
  12.6 6.4 %copy-start.8 = (bf16[128,256]{1,0:T(8,128)(2,1)S(1)}, bf16[128,256]{1,0:T(8,128)(2,1)}, u32[]{:S(2)}) copy-start(bf16[128,256]{1,0:T(8,128)(2,1)} %refs_10_.3) | copy-start | bytes 196612
  12.6 6.4 %copy-start.9 = (bf16[128,256]{1,0:T(8,128)(2,1)S(1)}, bf16[128,256]{1,0:T(8,128)(2,1)}, u32[]{:S(2)}) copy-start(bf16[128,256]{1,0:T(8,128)(2,1)} %refs_11_.3) | copy-start | bytes 196612
  12.6 6.4 %copy-start.12 = (bf16[128,128]{1,0:T(8,128)(2,1)S(1)}, bf16[128,128]{1,0:T(8,128)(2,1)}, u32[]{:S(2)}) copy-start(bf16[128,128]{1,0:T(8,128)(2,1)} %refs_12_.3) | copy-start | bytes 98308
  12.6 6.4 %copy-start.13 = (bf16[128,128]{1,0:T(8,128)(2,1)S(1)}, bf16[128,128]{1,0:T(8,128)(2,1)}, u32[]{:S(2)}) copy-start(bf16[128,128]{1,0:T(8,128)(2,1)} %refs_13_.1) | copy-start | bytes 98308
  (1 other events, 0.7 us)

commit v5 on v2

--- a/solution.py
+++ b/solution.py
@@ -415,6 +415,13 @@
     opm = normal(align.astype(F32)).astype(BF16)
     opm = mul(opm, lift[...], ((1,), (1,))).astype(BF16)
     hidden = MEAN_HIDDEN_SIZE
+    right = opm[:, hidden:]
+    for c in range(0, hidden, 2):
+        pair_w = jnp.concatenate(
+            [outer_w[(c + k) * hidden : (c + k + 1) * hidden, :] for k in range(2)], axis=1
+        )
+        part = mul(right, pair_w)
+        lifted[c], lifted[c + 1] = part[:, :pair_width], part[:, pair_width:]
     deep = hidden * count
     spread = zero_one(
         iota((2 * hidden, deep), 1) // count == iota((2 * hidden, deep), 0)
@@ -425,13 +432,6 @@
     ).astype(BF16)
     gather = zero_one(iota((residues, tokens), 1) // count == iota((residues, tokens), 0))
     left = mul(gather, left).astype(BF16)
-    right = opm[:, hidden:]
-    for c in range(0, hidden, 2):
-        pair_w = jnp.concatenate(
-            [outer_w[(c + k) * hidden : (c + k + 1) * hidden, :] for k in range(2)], axis=1
-        )
-        part = mul(right, pair_w)
-        lifted[c], lifted[c + 1] = part[:, :pair_width], part[:, pair_width:]
     for j in range(0, residues, 2):
         part = jnp.concatenate(
             [
@@ -441,7 +441,9 @@
             axis=1,
         )
         part = mul(left, part.astype(BF16)) * (1.0 / count)
-        update_ref[j], update_ref[j + 1] = part[:, :pair_width], part[:, pair_width:]
+        for k in range(2):
+            at = slice((j + k) * residues, (j + k + 1) * residues)
+            update_ref[at, :] = part[:, k * pair_width : (k + 1) * pair_width]
 
 
 def pair_kernel(*refs):
@@ -454,6 +456,21 @@
     for packet, r in zip((None, *packets), (0, *PACKET_ORDER)):
         shown = split_small(packet, residues, res_dev, per)[1] if r else own_valid
         valid[pl.ds(pl.multiple_of((me ^ r) * res_dev, res_dev), res_dev), :] = shown
+    own = jnp.concatenate(
+        [
+            pair[i].astype(F32) + update[pl.ds(me * res_dev + i, residues, stride=residues), :]
+            for i in range(res_dev)
+        ],
+        axis=0,
+    )
+    left_w = jnp.concatenate([proj[:, :C_TRI], gates[:, :C_TRI], gate_out[...]], axis=1)
+    own_all = mul(normal(own).astype(BF16), left_w)
+    own_gate = sigmoid(own_all[:, 2 * C_TRI :])
+    left = sigmoid(own_all[:, C_TRI : 2 * C_TRI]) * own_all[:, :C_TRI]
+    shown = mul(own_valid.astype(BF16), column[:res_dev, : res_dev * C_TRI], ((0,), (0,)))
+    for i in range(res_dev):
+        part = left[i * residues : (i + 1) * residues] * shown[:, i * C_TRI : (i + 1) * C_TRI]
+        left_at[i * residues : (i + 1) * residues, :] = part.astype(BF16).astype(F32)
     size = res_dev * residues
     for block, r in zip((pair, *pairs), (0, *PAIR_ORDER)):
         state[pl.ds(pl.multiple_of((me ^ r) * size, size), size), :] = (
@@ -461,7 +478,8 @@
         )
     for k in range(residues):
         one[k * residues : (k + 1) * residues, :] = (
-            state[pl.ds(k, residues, stride=residues), :] + update[k]
+            state[pl.ds(k, residues, stride=residues), :]
+            + update[k * residues : (k + 1) * residues, :]
         )
 
     shown = mul(valid[...].astype(BF16), column[...])
@@ -476,18 +494,6 @@
             part = part * shown[:, (k + p) * C_TRI : (k + p + 1) * C_TRI]
             right_at[(k + p) * residues : (k + p + 1) * residues, :] = part.astype(BF16).astype(F32)
 
-    own = jnp.concatenate(
-        [one[pl.ds(me * res_dev + i, residues, stride=residues), :] for i in range(res_dev)],
-        axis=0,
-    )
-    left_w = jnp.concatenate([proj[:, :C_TRI], gates[:, :C_TRI], gate_out[...]], axis=1)
-    own_all = mul(normal(own).astype(BF16), left_w)
-    own_gate = sigmoid(own_all[:, 2 * C_TRI :])
-    left = sigmoid(own_all[:, C_TRI : 2 * C_TRI]) * own_all[:, :C_TRI]
-    shown = mul(own_valid.astype(BF16), column[:res_dev, : res_dev * C_TRI], ((0,), (0,)))
-    for i in range(res_dev):
-        part = left[i * residues : (i + 1) * residues] * shown[:, i * C_TRI : (i + 1) * C_TRI]
-        left_at[i * residues : (i + 1) * residues, :] = part.astype(BF16).astype(F32)
     sums = [jnp.zeros((residues, C_TRI), F32) for _ in range(res_dev)]
     for k in range(residues):
         other = right_at[k * residues : (k + 1) * residues, :]
@@ -573,7 +579,7 @@
         functools.partial(msa_kernel, n, res_dev),
         (
             jax.ShapeDtypeStruct((count, res_dev, width), BF16),
-            jax.ShapeDtypeStruct((residues, residues, pair_width), F32),
+            jax.ShapeDtypeStruct((residues * residues, pair_width), F32),
         ),
         [
             pltpu.VMEM((MEAN_HIDDEN_SIZE, count * residues, pair_width), F32),

time: 19.6 us -> 19.7 us (level)
  no operation moved by 1% of the time
where the time goes in v5:
time: 19.7 us; the launch traced here: 19.6 us
  starting transfers between devices  10.1 us (51%)
  Pallas kernels  7.31 us (37%)
  between operations  0.93 us (5%)
  local copies, waits for them, and re-layouts  0.81 us (4%)
  waiting for transfers between devices  0.45 us (2%)
    ppermute x6, starting transfers between devices, swap(): return lax.ppermute(array, 'axial', [(i, i ^ r) for i in range(n)])  10.1 us
    pallas_call x4, Pallas kernels, call(): pl.pallas_call(kernel, out_shape=out_shape, in_specs=[vmem] * len(args),...  7.31 us
    unnamed x38, local copies, waits for them, and re-layouts  0.81 us
    ppermute x6, waiting for transfers between devices, swap(): return lax.ppermute(array, 'axial', [(i, i ^ r) for i in range(n)])  0.45 us
  transfers between devices with their start and end apart: 6, of which 1 were waited for; matrix products, arithmetic and copies ran while one was open for 0% of the time, Pallas kernels for 24%

profile of v5, /device:TPU:0, one launch (start us, length us, event | category | flops | bytes accessed | tf_op | source)
XLA Modules:
  0.0 19.6 jit_solution(7835220683979078354)
XLA Ops:
  0.7 0.1 shard_map.194
  0.7 0.0 copy-start.15
  0.8 0.0 copy-start.17
  0.8 0.0 copy-start.18
  0.8 0.7 %copy-done.7 = bf16[8,32,128]{2,1,0:T(8,128)(2,1)S(1)} copy-done((bf16[8,32,128]{2,1,0:T(8,128)(2,1)S(1)}, bf16[8,32,128]{2,1,0:T(8,128)(2,1)}, u32[]{:S(2)}) %copy-start.7) | copy-done | bytes 65560
  1.5 0.0 copy-start
  1.5 0.0 copy-start.1
  1.5 0.0 copy-start.4
  1.6 0.0 copy-start.5
  1.6 0.0 copy-start.14
  1.6 0.4 %shard_map.195 = (bf16[80,256]{1,0:T(8,128)(2,1)S(1)}, f32[32,256]{1,0:T(8,128)S(1)}) custom-call(bf16[8,32,128]{2,1,0:T(8,128)(2,1)S(1)} %copy-done.7, bf16[8,128]{1,0:T(8,128)(2,1)S(1)} %bitcast.4, s32[8,32]{1,0:T(8,128)S(1)} %copy-done.15, s32[2,32]{1,0:T(2,128)S(1)} %copy-done.17, bf16[2,32,256]{2,1,0:T(8,128)(2,1)S(1)} %copy-done.10, ...), custom_call_target="tpu_custom_call" | custom-call | flops 3000000000 | tf_op jit(solution)/shard_map/pallas_call | solution.py:509
  2.0 4.1 %collective-permute-start = (bf16[80,256]{1,0:T(8,128)(2,1)S(1)}, bf16[80,256]{1,0:T(8,128)(2,1)S(1)}, u32[]{:S(2)}, u32[]{:S(2)}) collective-permute-start(bf16[80,256]{1,0:T(8,128)(2,1)S(1)} %get-tuple-element.11.refs_0_), channel_id=1, source_target_pairs={{0,2},{1,3},{2,0},{3,1},{4,6},{5,7},{6,4},{7,5},{8,10},{9,11},{10,... | collective-permute-start | bytes 122888 | tf_op jit(solution)/shard_map/ppermute | solution.py:521
  6.1 1.3 %collective-permute-start.1 = (bf16[80,256]{1,0:T(8,128)(2,1)S(1)}, bf16[80,256]{1,0:T(8,128)(2,1)S(1)}, u32[]{:S(2)}, u32[]{:S(2)}) collective-permute-start(bf16[80,256]{1,0:T(8,128)(2,1)S(1)} %get-tuple-element.11.refs_0_), channel_id=1, source_target_pairs={{0,3},{1,2},{2,1},{3,0},{4,7},{5,6},{6,5},{7,4},{8,11},{9,10},{10,... | collective-permute-start | bytes 122888 | tf_op jit(solution)/shard_map/ppermute | solution.py:521
  7.5 0.2 %collective-permute-start.2 = (bf16[80,256]{1,0:T(8,128)(2,1)S(1)}, bf16[80,256]{1,0:T(8,128)(2,1)S(1)}, u32[]{:S(2)}, u32[]{:S(2)}) collective-permute-start(bf16[80,256]{1,0:T(8,128)(2,1)S(1)} %get-tuple-element.11.refs_0_), channel_id=1, source_target_pairs={{0,1},{1,0},{2,3},{3,2},{4,5},{5,4},{6,7},{7,6},{8,9},{9,8},{10,11... | collective-permute-start | bytes 122888 | tf_op jit(solution)/shard_map/ppermute | solution.py:521
  7.7 2.9 %collective-permute-start.3 = (bf16[8,32,128]{2,1,0:T(8,128)(2,1)S(1)}, bf16[8,32,128]{2,1,0:T(8,128)(2,1)S(1)}, u32[]{:S(2)}, u32[]{:S(2)}) collective-permute-start(bf16[8,32,128]{2,1,0:T(8,128)(2,1)S(1)} %copy-done.7), channel_id=1, source_target_pairs={{0,3},{1,2},{2,1},{3,0},{4,7},{5,6},{6,5},{7,4},{8,11},{9,10},{10,... | collective-permute-start | bytes 196616 | tf_op jit(solution)/shard_map/ppermute | solution.py:521
  10.6 0.5 %collective-permute-start.4 = (bf16[8,32,128]{2,1,0:T(8,128)(2,1)S(1)}, bf16[8,32,128]{2,1,0:T(8,128)(2,1)S(1)}, u32[]{:S(2)}, u32[]{:S(2)}) collective-permute-start(bf16[8,32,128]{2,1,0:T(8,128)(2,1)S(1)} %copy-done.7), channel_id=1, source_target_pairs={{0,1},{1,0},{2,3},{3,2},{4,5},{5,4},{6,7},{7,6},{8,9},{9,8},{10,11... | collective-permute-start | bytes 196616 | tf_op jit(solution)/shard_map/ppermute | solution.py:521
  11.1 1.0 %collective-permute-start.5 = (bf16[8,32,128]{2,1,0:T(8,128)(2,1)S(1)}, bf16[8,32,128]{2,1,0:T(8,128)(2,1)S(1)}, u32[]{:S(2)}, u32[]{:S(2)}) collective-permute-start(bf16[8,32,128]{2,1,0:T(8,128)(2,1)S(1)} %copy-done.7), channel_id=1, source_target_pairs={{0,2},{1,3},{2,0},{3,1},{4,6},{5,7},{6,4},{7,5},{8,10},{9,11},{10,... | collective-permute-start | bytes 196616 | tf_op jit(solution)/shard_map/ppermute | solution.py:521
  12.1 0.4 %collective-permute-done.1.refs_2_.refs_4_ = bf16[80,256]{1,0:T(8,128)(2,1)S(1)} collective-permute-done((bf16[80,256]{1,0:T(8,128)(2,1)S(1)}, bf16[80,256]{1,0:T(8,128)(2,1)S(1)}, u32[]{:S(2)}, u32[]{:S(2)}) %collective-permute-start.1) | collective-permute-done | bytes 40992 | tf_op jit(solution)/shard_map/ppermute | solution.py:521
  12.6 0.0 copy-start.8
  12.6 0.0 copy-start.9
  12.6 0.0 copy-start.13
  12.6 4.8 %shard_map.196 = (bf16[8,8,256]{2,1,0:T(8,128)(2,1)}, f32[1024,128]{1,0:T(8,128)S(1)}) custom-call(bf16[80,256]{1,0:T(8,128)(2,1)S(1)} %get-tuple-element.11.refs_0_, bf16[80,256]{1,0:T(8,128)(2,1)S(1)} %collective-permute-done.refs_1_.refs_3_, bf16[80,256]{1,0:T(8,128)(2,1)S(1)} %collective-permute-done.1.refs_2_.refs_4_, ...), custom_call_target="tpu_custom_call" | custom-call | flops 3000000000 | tf_op jit(solution)/shard_map/pallas_call | solution.py:509
  17.4 0.0 collective-permute-done.3.refs_0_
  17.5 2.1 %shard_map.197 = bf16[8,32,128]{2,1,0:T(8,128)(2,1)} custom-call(bf16[8,32,128]{2,1,0:T(8,128)(2,1)S(1)} %collective-permute-done.3.refs_0_, bf16[8,32,128]{2,1,0:T(8,128)(2,1)S(1)} %collective-permute-done.4.refs_1_, bf16[8,32,128]{2,1,0:T(8,128)(2,1)S(1)} %collective-permute-done.5.refs_2_, bf16[80,256]{1,0:T(8,128)(2,1)S(1)} %collective-permute-done.refs_1_.refs_3_, ...), custom_call_target="tpu_custom_call" | custom-call | flops 3000000000 | tf_op jit(solution)/shard_map/pallas_call | solution.py:509
  (30 shorter events, 0.1 us)
Async XLA Ops:
  0.6 0.8 %copy-start.7 = (bf16[8,32,128]{2,1,0:T(8,128)(2,1)S(1)}, bf16[8,32,128]{2,1,0:T(8,128)(2,1)}, u32[]{:S(2)}) copy-start(bf16[8,32,128]{2,1,0:T(8,128)(2,1)} %refs_8_.3) | copy-start | bytes 196612
  0.6 0.8 %copy-start.10 = (bf16[2,32,256]{2,1,0:T(8,128)(2,1)S(1)}, bf16[2,32,256]{2,1,0:T(8,128)(2,1)}, u32[]{:S(2)}) copy-start(bf16[2,32,256]{2,1,0:T(8,128)(2,1)} %refs_4_.1) | copy-start | bytes 98308
  0.6 0.8 %copy-start.16 = (bf16[128,8]{0,1:T(8,128)(2,1)S(1)}, bf16[128,8]{0,1:T(8,128)(2,1)}, u32[]{:S(2)}) copy-start(bf16[128,8]{0,1:T(8,128)(2,1)} %param.27) | copy-start | bytes 6148
  0.7 0.7 %copy-start.15 = (s32[8,32]{1,0:T(8,128)S(1)}, s32[8,32]{1,0:T(8,128)}, u32[]{:S(2)}) copy-start(s32[8,32]{1,0:T(8,128)} %refs_9_.3) | copy-start | bytes 3076
  0.8 0.7 %copy-start.17 = (s32[2,32]{1,0:T(2,128)S(1)}, s32[2,32]{1,0:T(2,128)}, u32[]{:S(2)}) copy-start(s32[2,32]{1,0:T(2,128)} %refs_3_.1) | copy-start | bytes 772
  1.5 11.0 %copy-start = (bf16[256,768]{1,0:T(8,128)(2,1)S(1)}, bf16[256,768]{1,0:T(8,128)(2,1)}, u32[]{:S(2)}) copy-start(bf16[256,768]{1,0:T(8,128)(2,1)} %refs_8_.2) | copy-start | bytes 1179652
  1.5 11.0 %copy-start.1 = (bf16[256,768]{1,0:T(8,128)(2,1)S(1)}, bf16[256,768]{1,0:T(8,128)(2,1)}, u32[]{:S(2)}) copy-start(bf16[256,768]{1,0:T(8,128)(2,1)} %refs_11_.2) | copy-start | bytes 1179652
  1.5 11.0 %copy-start.2 = (bf16[1024,128]{1,0:T(8,128)(2,1)S(1)}, bf16[1024,128]{1,0:T(8,128)(2,1)}, u32[]{:S(2)}) copy-start(bf16[1024,128]{1,0:T(8,128)(2,1)} %refs_14_.1) | copy-start | bytes 786436
  1.5 11.0 %copy-start.3 = (bf16[256,256]{1,0:T(8,128)(2,1)S(1)}, bf16[256,256]{1,0:T(8,128)(2,1)}, u32[]{:S(2)}) copy-start(bf16[256,256]{1,0:T(8,128)(2,1)} %refs_7_.1) | copy-start | bytes 393220
  1.5 11.0 %copy-start.4 = (bf16[256,256]{1,0:T(8,128)(2,1)S(1)}, bf16[256,256]{1,0:T(8,128)(2,1)}, u32[]{:S(2)}) copy-start(bf16[256,256]{1,0:T(8,128)(2,1)} %refs_9_.2) | copy-start | bytes 393220
  1.6 11.0 %copy-start.5 = (bf16[256,256]{1,0:T(8,128)(2,1)S(1)}, bf16[256,256]{1,0:T(8,128)(2,1)}, u32[]{:S(2)}) copy-start(bf16[256,256]{1,0:T(8,128)(2,1)} %refs_10_.2) | copy-start | bytes 393220
  1.6 11.0 %copy-start.6 = (bf16[256,256]{1,0:T(8,128)(2,1)S(1)}, bf16[256,256]{1,0:T(8,128)(2,1)}, u32[]{:S(2)}) copy-start(bf16[256,256]{1,0:T(8,128)(2,1)} %refs_12_.2) | copy-start | bytes 393220
  1.6 11.0 %copy-start.11 = (bf16[256,64]{0,1:T(8,128)(2,1)S(1)}, bf16[256,64]{0,1:T(8,128)(2,1)}, u32[]{:S(2)}) copy-start(bf16[256,64]{0,1:T(8,128)(2,1)} %param.32) | copy-start | bytes 98308
  1.6 11.0 %copy-start.14 = (bf16[23,256]{1,0:T(8,128)(2,1)S(1)}, bf16[23,256]{1,0:T(8,128)(2,1)}, u32[]{:S(2)}) copy-start(bf16[23,256]{1,0:T(8,128)(2,1)} %refs_6_.1) | copy-start | bytes 35332
  2.0 9.1 %collective-permute-start = (bf16[80,256]{1,0:T(8,128)(2,1)S(1)}, bf16[80,256]{1,0:T(8,128)(2,1)S(1)}, u32[]{:S(2)}, u32[]{:S(2)}) collective-permute-start(bf16[80,256]{1,0:T(8,128)(2,1)S(1)} %get-tuple-element.11.refs_0_), channel_id=1, source_target_pairs={{0,2},{1,3},{2,0},{3,1},{4,6},{5,7},{6,4},{7,5},{8,10},{9,11},{10,... | collective-permute-start | bytes 122888 | tf_op jit(solution)/shard_map/ppermute | solution.py:521
  6.1 6.4 %collective-permute-start.1 = (bf16[80,256]{1,0:T(8,128)(2,1)S(1)}, bf16[80,256]{1,0:T(8,128)(2,1)S(1)}, u32[]{:S(2)}, u32[]{:S(2)}) collective-permute-start(bf16[80,256]{1,0:T(8,128)(2,1)S(1)} %get-tuple-element.11.refs_0_), channel_id=1, source_target_pairs={{0,3},{1,2},{2,1},{3,0},{4,7},{5,6},{6,5},{7,4},{8,11},{9,10},{10,... | collective-permute-start | bytes 122888 | tf_op jit(solution)/shard_map/ppermute | solution.py:521
  7.5 5.0 %collective-permute-start.2 = (bf16[80,256]{1,0:T(8,128)(2,1)S(1)}, bf16[80,256]{1,0:T(8,128)(2,1)S(1)}, u32[]{:S(2)}, u32[]{:S(2)}) collective-permute-start(bf16[80,256]{1,0:T(8,128)(2,1)S(1)} %get-tuple-element.11.refs_0_), channel_id=1, source_target_pairs={{0,1},{1,0},{2,3},{3,2},{4,5},{5,4},{6,7},{7,6},{8,9},{9,8},{10,11... | collective-permute-start | bytes 122888 | tf_op jit(solution)/shard_map/ppermute | solution.py:521
  7.7 9.7 %collective-permute-start.3 = (bf16[8,32,128]{2,1,0:T(8,128)(2,1)S(1)}, bf16[8,32,128]{2,1,0:T(8,128)(2,1)S(1)}, u32[]{:S(2)}, u32[]{:S(2)}) collective-permute-start(bf16[8,32,128]{2,1,0:T(8,128)(2,1)S(1)} %copy-done.7), channel_id=1, source_target_pairs={{0,3},{1,2},{2,1},{3,0},{4,7},{5,6},{6,5},{7,4},{8,11},{9,10},{10,... | collective-permute-start | bytes 196616 | tf_op jit(solution)/shard_map/ppermute | solution.py:521
  10.6 6.8 %collective-permute-start.4 = (bf16[8,32,128]{2,1,0:T(8,128)(2,1)S(1)}, bf16[8,32,128]{2,1,0:T(8,128)(2,1)S(1)}, u32[]{:S(2)}, u32[]{:S(2)}) collective-permute-start(bf16[8,32,128]{2,1,0:T(8,128)(2,1)S(1)} %copy-done.7), channel_id=1, source_target_pairs={{0,1},{1,0},{2,3},{3,2},{4,5},{5,4},{6,7},{7,6},{8,9},{9,8},{10,11... | collective-permute-start | bytes 196616 | tf_op jit(solution)/shard_map/ppermute | solution.py:521
  11.1 6.4 %collective-permute-start.5 = (bf16[8,32,128]{2,1,0:T(8,128)(2,1)S(1)}, bf16[8,32,128]{2,1,0:T(8,128)(2,1)S(1)}, u32[]{:S(2)}, u32[]{:S(2)}) collective-permute-start(bf16[8,32,128]{2,1,0:T(8,128)(2,1)S(1)} %copy-done.7), channel_id=1, source_target_pairs={{0,2},{1,3},{2,0},{3,1},{4,6},{5,7},{6,4},{7,5},{8,10},{9,11},{10,... | collective-permute-start | bytes 196616 | tf_op jit(solution)/shard_map/ppermute | solution.py:521
  12.6 4.9 %copy-start.8 = (bf16[128,256]{1,0:T(8,128)(2,1)S(1)}, bf16[128,256]{1,0:T(8,128)(2,1)}, u32[]{:S(2)}) copy-start(bf16[128,256]{1,0:T(8,128)(2,1)} %refs_10_.3) | copy-start | bytes 196612
  12.6 4.9 %copy-start.9 = (bf16[128,256]{1,0:T(8,128)(2,1)S(1)}, bf16[128,256]{1,0:T(8,128)(2,1)}, u32[]{:S(2)}) copy-start(bf16[128,256]{1,0:T(8,128)(2,1)} %refs_11_.3) | copy-start | bytes 196612
  12.6 4.8 %copy-start.12 = (bf16[128,128]{1,0:T(8,128)(2,1)S(1)}, bf16[128,128]{1,0:T(8,128)(2,1)}, u32[]{:S(2)}) copy-start(bf16[128,128]{1,0:T(8,128)(2,1)} %refs_12_.3) | copy-start | bytes 98308
  12.6 4.8 %copy-start.13 = (bf16[128,128]{1,0:T(8,128)(2,1)S(1)}, bf16[128,128]{1,0:T(8,128)(2,1)}, u32[]{:S(2)}) copy-start(bf16[128,128]{1,0:T(8,128)(2,1)} %refs_13_.1) | copy-start | bytes 98308
  (1 other events, 0.7 us)

commit v6 on v5

--- a/solution.py
+++ b/solution.py
@@ -218,8 +218,8 @@
 F32 = jnp.float32
 SMALL_ROWS = 16
 FLOPS = 3 * 10**9
-PACKET_ORDER = (2, 3, 1)
-PAIR_ORDER = (3, 1, 2)
+PACKET_ORDER = (2, 1, 3)
+PAIR_ORDER = (2, 3)
 
 
 def mul(lhs, rhs, over=((1,), (0,))):
@@ -278,7 +278,7 @@
 
 def packet_kernel(*refs):
     pair_ref, weight_ref, valid_ref, ids_ref, act_ref, present_ref, shift_ref = refs[:7]
-    packet_ref, hidden_ref = refs[7:]
+    packet_ref, hidden_ref, full_ref = refs[7:]
     rows, residues, width = pair_ref.shape
     per, _, features = act_ref.shape
     lanes = FOCUS_TOTAL * rows
@@ -296,7 +296,13 @@
     first = jnp.concatenate([bias[:SMALL_ROWS], empty], axis=1) + extra
     second = jnp.concatenate([bias[SMALL_ROWS:], empty], axis=1)
     small = jnp.concatenate([first, second], axis=1).astype(BF16)
-    packet_ref[per * residues :, :] = small
+    top = per * residues
+    packet_ref[top:, :] = small
+    full_ref[top : top + SMALL_ROWS, :] = small
+    full_ref[:top, :] = act_ref[...].reshape(top, features)
+    for k in range(2):
+        half = pair_ref[k * rows // 2 : (k + 1) * rows // 2].reshape(rows * residues // 2, width)
+        full_ref[top + SMALL_ROWS :, k * width : (k + 1) * width] = half
     shown = present_ref[...].astype(F32).astype(BF16)
     shown = mul(shown, jnp.ones((1, hidden_ref.shape[1]), BF16), ((0,), (0,)))
     hidden_ref[...] = 1000000000.0 * (shown - 1.0)
@@ -304,7 +310,7 @@
 
 
 def split_small(packet, residues, res_dev, per):
-    small = packet[per * residues :, :].astype(F32)
+    small = packet[per * residues : per * residues + SMALL_ROWS, :].astype(F32)
     lanes = FOCUS_TOTAL * res_dev
     bias = jnp.concatenate([small[:, :lanes], small[:, 128 : 128 + lanes]], axis=0)
     extra = small[:, lanes : lanes + residues]
@@ -415,6 +421,16 @@
     opm = normal(align.astype(F32)).astype(BF16)
     opm = mul(opm, lift[...], ((1,), (1,))).astype(BF16)
     hidden = MEAN_HIDDEN_SIZE
+    deep = hidden * count
+    spread = zero_one(
+        iota((2 * hidden, deep), 1) // count == iota((2 * hidden, deep), 0)
+    )
+    left = mul(opm, spread)
+    left = jnp.where(
+        iota((tokens, deep), 0) % count == iota((tokens, deep), 1) % count, left, 0.0
+    ).astype(BF16)
+    gather = zero_one(iota((residues, tokens), 1) // count == iota((residues, tokens), 0))
+    left = mul(gather, left).astype(BF16)
     right = opm[:, hidden:]
     for c in range(0, hidden, 2):
         pair_w = jnp.concatenate(
@@ -422,16 +438,6 @@
         )
         part = mul(right, pair_w)
         lifted[c], lifted[c + 1] = part[:, :pair_width], part[:, pair_width:]
-    deep = hidden * count
-    spread = zero_one(
-        iota((2 * hidden, deep), 1) // count == iota((2 * hidden, deep), 0)
-    )
-    left = mul(opm, spread)
-    left = jnp.where(
-        iota((tokens, deep), 0) % count == iota((tokens, deep), 1) % count, left, 0.0
-    ).astype(BF16)
-    gather = zero_one(iota((residues, tokens), 1) // count == iota((residues, tokens), 0))
-    left = mul(gather, left).astype(BF16)
     for j in range(0, residues, 2):
         part = jnp.concatenate(
             [
@@ -447,8 +453,8 @@
 
 
 def pair_kernel(*refs):
-    pairs, packets, update, column, pair, own_mask = refs[:3], refs[3:6], *refs[6:10]
-    proj, gates, gate_out, w_out, out_ref, state, one, right_at, left_at, valid = refs[10:]
+    pairs, packets, update, column, pair, own_mask = refs[:2], refs[2:5], *refs[5:9]
+    proj, gates, gate_out, w_out, out_ref, state, one, right_at, left_at, valid = refs[9:]
     res_dev, residues, width = pair.shape
     per = (packets[0].shape[0] - SMALL_ROWS) // residues
     me = lax.axis_index("axial")
@@ -472,10 +478,12 @@
         part = left[i * residues : (i + 1) * residues] * shown[:, i * C_TRI : (i + 1) * C_TRI]
         left_at[i * residues : (i + 1) * residues, :] = part.astype(BF16).astype(F32)
     size = res_dev * residues
-    for block, r in zip((pair, *pairs), (0, *PAIR_ORDER)):
-        state[pl.ds(pl.multiple_of((me ^ r) * size, size), size), :] = (
-            block[...].astype(F32).reshape(size, width)
-        )
+    beside = packets[PACKET_ORDER.index(1)][per * residues + SMALL_ROWS :, :]
+    beside = jnp.concatenate([beside[:, :width], beside[:, width:]], axis=0)
+    blocks = [pair[...].reshape(size, width), beside]
+    blocks += [block[...].reshape(size, width) for block in pairs]
+    for block, r in zip(blocks, (0, 1, *PAIR_ORDER)):
+        state[pl.ds(pl.multiple_of((me ^ r) * size, size), size), :] = block.astype(F32)
     for k in range(residues):
         one[k * residues : (k + 1) * residues, :] = (
             state[pl.ds(k, residues, stride=residues), :]
@@ -556,11 +564,14 @@
         [],
         2,
     )
-    packet, hidden_keys = call(
+    packet, hidden_keys, full = call(
         packet_kernel,
         (
             jax.ShapeDtypeStruct((per * residues + SMALL_ROWS, width), BF16),
             jax.ShapeDtypeStruct((residues, FOCUS_TOTAL * residues), F32),
+            jax.ShapeDtypeStruct(
+                (per * residues + SMALL_ROWS + res_dev * residues // 2, width), BF16
+            ),
         ),
         [],
         4,
@@ -572,7 +583,7 @@
         residue_present_mask.reshape(1, residues),
         shift,
     )
-    packets = [swap(packet, r, n) for r in PACKET_ORDER]
+    packets = [swap(full if r == 1 else packet, r, n) for r in PACKET_ORDER]
     _, later = lax.optimization_barrier((packet, pair_state))
     pairs = [swap(later, r, n) for r in PAIR_ORDER]
     alignment, update = call(

time: 19.7 us -> 20.9 us (1.061)
  waiting for transfers between devices: 0.45 us -> 2.34 us
  starting transfers between devices: 10.1 us -> 9.5 us
    ppermute x6 -> x5, waiting for transfers between devices: 0.45 us -> 2.34 us  [swap(): return lax.ppermute(array, 'axial', [(i, i ^ r) for i in range(n)])]
    ppermute x6 -> x5, starting transfers between devices: 10.1 us -> 9.5 us  [swap(): return lax.ppermute(array, 'axial', [(i, i ^ r) for i in range(n)])]
  transfers between devices with their start and end apart: 6 -> 5, of which waited for: 1 -> 1; matrix products, arithmetic and copies ran while one was open for 0% -> 0% of each run, Pallas kernels for 24% -> 22%
where the time goes in v6:
time: 20.9 us; the launch traced here: 20.8 us
  starting transfers between devices  9.5 us (45%)
  Pallas kernels  7.16 us (34%)
  waiting for transfers between devices  2.34 us (11%)
  between operations  0.92 us (4%)
  local copies, waits for them, and re-layouts  0.82 us (4%)
    ppermute x5, starting transfers between devices, swap(): return lax.ppermute(array, 'axial', [(i, i ^ r) for i in range(n)])  9.5 us
    pallas_call x4, Pallas kernels, call(): pl.pallas_call(kernel, out_shape=out_shape, in_specs=[vmem] * len(args),...  7.16 us
    ppermute x5, waiting for transfers between devices, swap(): return lax.ppermute(array, 'axial', [(i, i ^ r) for i in range(n)])  2.34 us
    unnamed x38, local copies, waits for them, and re-layouts  0.82 us
  transfers between devices with their start and end apart: 5, of which 1 were waited for; matrix products, arithmetic and copies ran while one was open for 0% of the time, Pallas kernels for 22%

profile of v6, /device:TPU:0, one launch (start us, length us, event | category | flops | bytes accessed | tf_op | source)
XLA Modules:
  0.0 20.8 jit_solution(14265423630336347136)
XLA Ops:
  0.7 0.1 shard_map.194
  0.7 0.0 copy-start.15
  0.8 0.0 copy-start.17
  0.8 0.0 copy-start.18
  0.8 0.6 %copy-done.10 = bf16[2,32,256]{2,1,0:T(8,128)(2,1)S(1)} copy-done((bf16[2,32,256]{2,1,0:T(8,128)(2,1)S(1)}, bf16[2,32,256]{2,1,0:T(8,128)(2,1)}, u32[]{:S(2)}) %copy-start.10) | copy-done | bytes 32792
  1.4 0.1 copy-done.7
  1.5 0.0 copy-start
  1.5 0.0 copy-start.1
  1.5 0.0 copy-start.2
  1.5 0.0 copy-start.3
  1.6 0.0 copy-start.4
  1.6 0.0 copy-start.5
  1.6 0.0 copy-start.6
  1.6 0.0 copy-start.14
  1.6 0.4 %shard_map.195 = (bf16[80,256]{1,0:T(8,128)(2,1)S(1)}, f32[32,256]{1,0:T(8,128)S(1)}, bf16[208,256]{1,0:T(8,128)(2,1)S(1)}) custom-call(bf16[8,32,128]{2,1,0:T(8,128)(2,1)S(1)} %copy-done.7, bf16[8,128]{1,0:T(8,128)(2,1)S(1)} %bitcast.4, s32[8,32]{1,0:T(8,128)S(1)} %copy-done.15, s32[2,32]{1,0:T(2,128)S(1)} %copy-done.17, ...), custom_call_target="tpu_custom_call" | custom-call | flops 3000000000 | tf_op jit(solution)/shard_map/pallas_call | solution.py:517
  2.0 3.1 %collective-permute-start.1 = (bf16[208,256]{1,0:T(8,128)(2,1)S(1)}, bf16[208,256]{1,0:T(8,128)(2,1)S(1)}, u32[]{:S(2)}, u32[]{:S(2)}) collective-permute-start(bf16[208,256]{1,0:T(8,128)(2,1)S(1)} %get-tuple-element.13), channel_id=1, source_target_pairs={{0,1},{1,0},{2,3},{3,2},{4,5},{5,4},{6,7},{7,6},{8,9},{9,8},{10,11... | collective-permute-start | bytes 319496 | tf_op jit(solution)/shard_map/ppermute | solution.py:529
  5.1 2.6 %collective-permute-start = (bf16[80,256]{1,0:T(8,128)(2,1)S(1)}, bf16[80,256]{1,0:T(8,128)(2,1)S(1)}, u32[]{:S(2)}, u32[]{:S(2)}) collective-permute-start(bf16[80,256]{1,0:T(8,128)(2,1)S(1)} %get-tuple-element.12.refs_0_), channel_id=1, source_target_pairs={{0,2},{1,3},{2,0},{3,1},{4,6},{5,7},{6,4},{7,5},{8,10},{9,11},{10,... | collective-permute-start | bytes 122888 | tf_op jit(solution)/shard_map/ppermute | solution.py:529
  7.7 1.9 %collective-permute-start.3 = (bf16[8,32,128]{2,1,0:T(8,128)(2,1)S(1)}, bf16[8,32,128]{2,1,0:T(8,128)(2,1)S(1)}, u32[]{:S(2)}, u32[]{:S(2)}) collective-permute-start(bf16[8,32,128]{2,1,0:T(8,128)(2,1)S(1)} %copy-done.7), channel_id=1, source_target_pairs={{0,2},{1,3},{2,0},{3,1},{4,6},{5,7},{6,4},{7,5},{8,10},{9,11},{10,... | collective-permute-start | bytes 196616 | tf_op jit(solution)/shard_map/ppermute | solution.py:529
  9.6 1.9 %collective-permute-start.4 = (bf16[8,32,128]{2,1,0:T(8,128)(2,1)S(1)}, bf16[8,32,128]{2,1,0:T(8,128)(2,1)S(1)}, u32[]{:S(2)}, u32[]{:S(2)}) collective-permute-start(bf16[8,32,128]{2,1,0:T(8,128)(2,1)S(1)} %copy-done.7), channel_id=1, source_target_pairs={{0,3},{1,2},{2,1},{3,0},{4,7},{5,6},{6,5},{7,4},{8,11},{9,10},{10,... | collective-permute-start | bytes 196616 | tf_op jit(solution)/shard_map/ppermute | solution.py:529
  11.5 2.3 %collective-permute-done.2.refs_3_.refs_4_ = bf16[80,256]{1,0:T(8,128)(2,1)S(1)} collective-permute-done((bf16[80,256]{1,0:T(8,128)(2,1)S(1)}, bf16[80,256]{1,0:T(8,128)(2,1)S(1)}, u32[]{:S(2)}, u32[]{:S(2)}) %collective-permute-start.2) | collective-permute-done | bytes 40992 | tf_op jit(solution)/shard_map/ppermute | solution.py:529
  14.0 0.0 copy-start.9
  14.0 0.0 copy-start.12
  14.0 4.6 %shard_map.196 = (bf16[8,8,256]{2,1,0:T(8,128)(2,1)}, f32[1024,128]{1,0:T(8,128)S(1)}) custom-call(bf16[80,256]{1,0:T(8,128)(2,1)S(1)} %get-tuple-element.12.refs_0_, bf16[80,256]{1,0:T(8,128)(2,1)S(1)} %collective-permute-done.refs_1_.refs_2_, bf16[208,256]{1,0:T(8,128)(2,1)S(1)} %collective-permute-done.1.refs_2_.refs_3_, ...), custom_call_target="tpu_custom_call" | custom-call | flops 3000000000 | tf_op jit(solution)/shard_map/pallas_call | solution.py:517
  18.7 2.1 %shard_map.197 = bf16[8,32,128]{2,1,0:T(8,128)(2,1)} custom-call(bf16[8,32,128]{2,1,0:T(8,128)(2,1)S(1)} %collective-permute-done.3.refs_0_, bf16[8,32,128]{2,1,0:T(8,128)(2,1)S(1)} %collective-permute-done.4.refs_1_, bf16[80,256]{1,0:T(8,128)(2,1)S(1)} %collective-permute-done.refs_1_.refs_2_, bf16[208,256]{1,0:T(8,128)(2,1)S(1)} %collective-permute-done.1.refs_2_.refs_3_, ...), custom_call_target="tpu_custom_call" | custom-call | flops 3000000000 | tf_op jit(solution)/shard_map/pallas_call | solution.py:517
  (28 shorter events, 0.1 us)
Async XLA Ops:
  0.6 0.8 %copy-start.10 = (bf16[2,32,256]{2,1,0:T(8,128)(2,1)S(1)}, bf16[2,32,256]{2,1,0:T(8,128)(2,1)}, u32[]{:S(2)}) copy-start(bf16[2,32,256]{2,1,0:T(8,128)(2,1)} %refs_4_.1) | copy-start | bytes 98308
  0.6 0.8 %copy-start.7 = (bf16[8,32,128]{2,1,0:T(8,128)(2,1)S(1)}, bf16[8,32,128]{2,1,0:T(8,128)(2,1)}, u32[]{:S(2)}) copy-start(bf16[8,32,128]{2,1,0:T(8,128)(2,1)} %refs_7_.3) | copy-start | bytes 196612
  0.6 0.8 %copy-start.16 = (bf16[128,8]{0,1:T(8,128)(2,1)S(1)}, bf16[128,8]{0,1:T(8,128)(2,1)}, u32[]{:S(2)}) copy-start(bf16[128,8]{0,1:T(8,128)(2,1)} %param.27) | copy-start | bytes 6148
  0.7 0.8 %copy-start.15 = (s32[8,32]{1,0:T(8,128)S(1)}, s32[8,32]{1,0:T(8,128)}, u32[]{:S(2)}) copy-start(s32[8,32]{1,0:T(8,128)} %refs_8_.3) | copy-start | bytes 3076
  0.8 0.7 %copy-start.17 = (s32[2,32]{1,0:T(2,128)S(1)}, s32[2,32]{1,0:T(2,128)}, u32[]{:S(2)}) copy-start(s32[2,32]{1,0:T(2,128)} %refs_3_.1) | copy-start | bytes 772
  0.8 0.7 %copy-start.18 = (s32[32]{0:T(128)S(1)}, s32[32]{0:T(128)}, u32[]{:S(2)}) copy-start(s32[32]{0:T(128)} %param.21) | copy-start | bytes 388
  1.5 12.4 %copy-start = (bf16[256,768]{1,0:T(8,128)(2,1)S(1)}, bf16[256,768]{1,0:T(8,128)(2,1)}, u32[]{:S(2)}) copy-start(bf16[256,768]{1,0:T(8,128)(2,1)} %refs_8_.2) | copy-start | bytes 1179652
  1.5 12.4 %copy-start.1 = (bf16[256,768]{1,0:T(8,128)(2,1)S(1)}, bf16[256,768]{1,0:T(8,128)(2,1)}, u32[]{:S(2)}) copy-start(bf16[256,768]{1,0:T(8,128)(2,1)} %refs_11_.2) | copy-start | bytes 1179652
  1.5 12.3 %copy-start.2 = (bf16[1024,128]{1,0:T(8,128)(2,1)S(1)}, bf16[1024,128]{1,0:T(8,128)(2,1)}, u32[]{:S(2)}) copy-start(bf16[1024,128]{1,0:T(8,128)(2,1)} %refs_14_.1) | copy-start | bytes 786436
  1.5 12.3 %copy-start.3 = (bf16[256,256]{1,0:T(8,128)(2,1)S(1)}, bf16[256,256]{1,0:T(8,128)(2,1)}, u32[]{:S(2)}) copy-start(bf16[256,256]{1,0:T(8,128)(2,1)} %refs_7_.2) | copy-start | bytes 393220
  1.6 12.3 %copy-start.4 = (bf16[256,256]{1,0:T(8,128)(2,1)S(1)}, bf16[256,256]{1,0:T(8,128)(2,1)}, u32[]{:S(2)}) copy-start(bf16[256,256]{1,0:T(8,128)(2,1)} %refs_9_.2) | copy-start | bytes 393220
  1.6 12.3 %copy-start.5 = (bf16[256,256]{1,0:T(8,128)(2,1)S(1)}, bf16[256,256]{1,0:T(8,128)(2,1)}, u32[]{:S(2)}) copy-start(bf16[256,256]{1,0:T(8,128)(2,1)} %refs_10_.2) | copy-start | bytes 393220
  1.6 12.3 %copy-start.6 = (bf16[256,256]{1,0:T(8,128)(2,1)S(1)}, bf16[256,256]{1,0:T(8,128)(2,1)}, u32[]{:S(2)}) copy-start(bf16[256,256]{1,0:T(8,128)(2,1)} %refs_12_.2) | copy-start | bytes 393220
  1.6 12.3 %copy-start.11 = (bf16[256,64]{0,1:T(8,128)(2,1)S(1)}, bf16[256,64]{0,1:T(8,128)(2,1)}, u32[]{:S(2)}) copy-start(bf16[256,64]{0,1:T(8,128)(2,1)} %param.32) | copy-start | bytes 98308
  1.6 12.3 %copy-start.14 = (bf16[23,256]{1,0:T(8,128)(2,1)S(1)}, bf16[23,256]{1,0:T(8,128)(2,1)}, u32[]{:S(2)}) copy-start(bf16[23,256]{1,0:T(8,128)(2,1)} %refs_6_.1) | copy-start | bytes 35332
  2.0 11.8 %collective-permute-start.1 = (bf16[208,256]{1,0:T(8,128)(2,1)S(1)}, bf16[208,256]{1,0:T(8,128)(2,1)S(1)}, u32[]{:S(2)}, u32[]{:S(2)}) collective-permute-start(bf16[208,256]{1,0:T(8,128)(2,1)S(1)} %get-tuple-element.13), channel_id=1, source_target_pairs={{0,1},{1,0},{2,3},{3,2},{4,5},{5,4},{6,7},{7,6},{8,9},{9,8},{10,11... | collective-permute-start | bytes 319496 | tf_op jit(solution)/shard_map/ppermute | solution.py:529
  5.1 6.4 %collective-permute-start = (bf16[80,256]{1,0:T(8,128)(2,1)S(1)}, bf16[80,256]{1,0:T(8,128)(2,1)S(1)}, u32[]{:S(2)}, u32[]{:S(2)}) collective-permute-start(bf16[80,256]{1,0:T(8,128)(2,1)S(1)} %get-tuple-element.12.refs_0_), channel_id=1, source_target_pairs={{0,2},{1,3},{2,0},{3,1},{4,6},{5,7},{6,4},{7,5},{8,10},{9,11},{10,... | collective-permute-start | bytes 122888 | tf_op jit(solution)/shard_map/ppermute | solution.py:529
  7.7 6.2 %collective-permute-start.2 = (bf16[80,256]{1,0:T(8,128)(2,1)S(1)}, bf16[80,256]{1,0:T(8,128)(2,1)S(1)}, u32[]{:S(2)}, u32[]{:S(2)}) collective-permute-start(bf16[80,256]{1,0:T(8,128)(2,1)S(1)} %get-tuple-element.12.refs_0_), channel_id=1, source_target_pairs={{0,3},{1,2},{2,1},{3,0},{4,7},{5,6},{6,5},{7,4},{8,11},{9,10},{10,... | collective-permute-start | bytes 122888 | tf_op jit(solution)/shard_map/ppermute | solution.py:529
  7.7 10.9 %collective-permute-start.3 = (bf16[8,32,128]{2,1,0:T(8,128)(2,1)S(1)}, bf16[8,32,128]{2,1,0:T(8,128)(2,1)S(1)}, u32[]{:S(2)}, u32[]{:S(2)}) collective-permute-start(bf16[8,32,128]{2,1,0:T(8,128)(2,1)S(1)} %copy-done.7), channel_id=1, source_target_pairs={{0,2},{1,3},{2,0},{3,1},{4,6},{5,7},{6,4},{7,5},{8,10},{9,11},{10,... | collective-permute-start | bytes 196616 | tf_op jit(solution)/shard_map/ppermute | solution.py:529
  9.6 9.0 %collective-permute-start.4 = (bf16[8,32,128]{2,1,0:T(8,128)(2,1)S(1)}, bf16[8,32,128]{2,1,0:T(8,128)(2,1)S(1)}, u32[]{:S(2)}, u32[]{:S(2)}) collective-permute-start(bf16[8,32,128]{2,1,0:T(8,128)(2,1)S(1)} %copy-done.7), channel_id=1, source_target_pairs={{0,3},{1,2},{2,1},{3,0},{4,7},{5,6},{6,5},{7,4},{8,11},{9,10},{10,... | collective-permute-start | bytes 196616 | tf_op jit(solution)/shard_map/ppermute | solution.py:529
  13.9 4.7 %copy-start.8 = (bf16[128,256]{1,0:T(8,128)(2,1)S(1)}, bf16[128,256]{1,0:T(8,128)(2,1)}, u32[]{:S(2)}) copy-start(bf16[128,256]{1,0:T(8,128)(2,1)} %refs_9_.3) | copy-start | bytes 196612
  14.0 4.7 %copy-start.9 = (bf16[128,256]{1,0:T(8,128)(2,1)S(1)}, bf16[128,256]{1,0:T(8,128)(2,1)}, u32[]{:S(2)}) copy-start(bf16[128,256]{1,0:T(8,128)(2,1)} %refs_10_.3) | copy-start | bytes 196612
  14.0 4.7 %copy-start.12 = (bf16[128,128]{1,0:T(8,128)(2,1)S(1)}, bf16[128,128]{1,0:T(8,128)(2,1)}, u32[]{:S(2)}) copy-start(bf16[128,128]{1,0:T(8,128)(2,1)} %refs_11_.3) | copy-start | bytes 98308
  14.0 4.7 %copy-start.13 = (bf16[128,128]{1,0:T(8,128)(2,1)S(1)}, bf16[128,128]{1,0:T(8,128)(2,1)}, u32[]{:S(2)}) copy-start(bf16[128,128]{1,0:T(8,128)(2,1)} %refs_12_.3) | copy-start | bytes 98308

commit v7 on v5

--- a/solution.py
+++ b/solution.py
@@ -257,10 +257,9 @@
     row_of = iota((width, lanes), 1) % rows
     flat = normal(pair_ref[...].astype(F32).reshape(rows * residues, width)).astype(BF16)
     weight = mul(weight_ref[...], spread, ((0,), (0,)))
-    bias = jnp.zeros((residues, lanes), F32)
-    for i in range(rows):
-        one_row = jnp.where(row_of == i, weight, 0.0).astype(BF16)
-        bias += mul(flat[i * residues : (i + 1) * residues], one_row)
+    side_by_side = [flat[i * residues : (i + 1) * residues] for i in range(rows)]
+    one_row = [jnp.where(row_of == i, weight, 0.0).astype(BF16) for i in range(rows)]
+    bias = mul(jnp.concatenate(side_by_side, axis=1), jnp.concatenate(one_row, axis=0))
     return bias
 
 
@@ -415,13 +414,6 @@
     opm = normal(align.astype(F32)).astype(BF16)
     opm = mul(opm, lift[...], ((1,), (1,))).astype(BF16)
     hidden = MEAN_HIDDEN_SIZE
-    right = opm[:, hidden:]
-    for c in range(0, hidden, 2):
-        pair_w = jnp.concatenate(
-            [outer_w[(c + k) * hidden : (c + k + 1) * hidden, :] for k in range(2)], axis=1
-        )
-        part = mul(right, pair_w)
-        lifted[c], lifted[c + 1] = part[:, :pair_width], part[:, pair_width:]
     deep = hidden * count
     spread = zero_one(
         iota((2 * hidden, deep), 1) // count == iota((2 * hidden, deep), 0)
@@ -432,6 +424,13 @@
     ).astype(BF16)
     gather = zero_one(iota((residues, tokens), 1) // count == iota((residues, tokens), 0))
     left = mul(gather, left).astype(BF16)
+    right = opm[:, hidden:]
+    for c in range(0, hidden, 2):
+        pair_w = jnp.concatenate(
+            [outer_w[(c + k) * hidden : (c + k + 1) * hidden, :] for k in range(2)], axis=1
+        )
+        part = mul(right, pair_w)
+        lifted[c], lifted[c + 1] = part[:, :pair_width], part[:, pair_width:]
     for j in range(0, residues, 2):
         part = jnp.concatenate(
             [

time: 19.7 us -> 19.5 us (0.990)
  Pallas kernels: 7.31 us -> 7.1 us
    pallas_call x4, Pallas kernels: 7.31 us -> 7.1 us  [call(): pl.pallas_call(kernel, out_shape=out_shape, in_specs=[vmem] * len(args),...]
where the time goes in v7:
time: 19.5 us; the launch traced here: 19.3 us
  starting transfers between devices  10.1 us (52%)
  Pallas kernels  7.1 us (36%)
  between operations  0.93 us (5%)
  local copies, waits for them, and re-layouts  0.81 us (4%)
  waiting for transfers between devices  0.43 us (2%)
    ppermute x6, starting transfers between devices, swap(): return lax.ppermute(array, 'axial', [(i, i ^ r) for i in range(n)])  10.1 us
    pallas_call x4, Pallas kernels, call(): pl.pallas_call(kernel, out_shape=out_shape, in_specs=[vmem] * len(args),...  7.1 us
    unnamed x38, local copies, waits for them, and re-layouts  0.81 us
    ppermute x6, waiting for transfers between devices, swap(): return lax.ppermute(array, 'axial', [(i, i ^ r) for i in range(n)])  0.43 us
  transfers between devices with their start and end apart: 6, of which 1 were waited for; matrix products, arithmetic and copies ran while one was open for 0% of the time, Pallas kernels for 24%

profile of v7, /device:TPU:0, one launch (start us, length us, event | category | flops | bytes accessed | tf_op | source)
XLA Modules:
  0.0 19.3 jit_solution(1843397354588673326)
XLA Ops:
  0.7 0.1 shard_map.194
  0.7 0.0 copy-start.15
  0.8 0.0 copy-start.17
  0.8 0.0 copy-start.18
  0.8 0.7 %copy-done.7 = bf16[8,32,128]{2,1,0:T(8,128)(2,1)S(1)} copy-done((bf16[8,32,128]{2,1,0:T(8,128)(2,1)S(1)}, bf16[8,32,128]{2,1,0:T(8,128)(2,1)}, u32[]{:S(2)}) %copy-start.7) | copy-done | bytes 65560
  1.5 0.0 copy-start
  1.5 0.0 copy-start.1
  1.5 0.0 copy-start.2
  1.5 0.0 copy-start.3
  1.5 0.0 copy-start.4
  1.6 0.0 copy-start.11
  1.6 0.0 copy-start.14
  1.6 0.3 %shard_map.195 = (bf16[80,256]{1,0:T(8,128)(2,1)S(1)}, f32[32,256]{1,0:T(8,128)S(1)}) custom-call(bf16[8,32,128]{2,1,0:T(8,128)(2,1)S(1)} %copy-done.7, bf16[8,128]{1,0:T(8,128)(2,1)S(1)} %bitcast.4, s32[8,32]{1,0:T(8,128)S(1)} %copy-done.15, s32[2,32]{1,0:T(2,128)S(1)} %copy-done.17, bf16[2,32,256]{2,1,0:T(8,128)(2,1)S(1)} %copy-done.10, ...), custom_call_target="tpu_custom_call" | custom-call | flops 3000000000 | tf_op jit(solution)/shard_map/pallas_call | solution.py:508
  2.0 4.1 %collective-permute-start = (bf16[80,256]{1,0:T(8,128)(2,1)S(1)}, bf16[80,256]{1,0:T(8,128)(2,1)S(1)}, u32[]{:S(2)}, u32[]{:S(2)}) collective-permute-start(bf16[80,256]{1,0:T(8,128)(2,1)S(1)} %get-tuple-element.11.refs_0_), channel_id=1, source_target_pairs={{0,2},{1,3},{2,0},{3,1},{4,6},{5,7},{6,4},{7,5},{8,10},{9,11},{10,... | collective-permute-start | bytes 122888 | tf_op jit(solution)/shard_map/ppermute | solution.py:520
  6.1 1.3 %collective-permute-start.1 = (bf16[80,256]{1,0:T(8,128)(2,1)S(1)}, bf16[80,256]{1,0:T(8,128)(2,1)S(1)}, u32[]{:S(2)}, u32[]{:S(2)}) collective-permute-start(bf16[80,256]{1,0:T(8,128)(2,1)S(1)} %get-tuple-element.11.refs_0_), channel_id=1, source_target_pairs={{0,3},{1,2},{2,1},{3,0},{4,7},{5,6},{6,5},{7,4},{8,11},{9,10},{10,... | collective-permute-start | bytes 122888 | tf_op jit(solution)/shard_map/ppermute | solution.py:520
  7.4 0.2 %collective-permute-start.2 = (bf16[80,256]{1,0:T(8,128)(2,1)S(1)}, bf16[80,256]{1,0:T(8,128)(2,1)S(1)}, u32[]{:S(2)}, u32[]{:S(2)}) collective-permute-start(bf16[80,256]{1,0:T(8,128)(2,1)S(1)} %get-tuple-element.11.refs_0_), channel_id=1, source_target_pairs={{0,1},{1,0},{2,3},{3,2},{4,5},{5,4},{6,7},{7,6},{8,9},{9,8},{10,11... | collective-permute-start | bytes 122888 | tf_op jit(solution)/shard_map/ppermute | solution.py:520
  7.6 2.9 %collective-permute-start.3 = (bf16[8,32,128]{2,1,0:T(8,128)(2,1)S(1)}, bf16[8,32,128]{2,1,0:T(8,128)(2,1)S(1)}, u32[]{:S(2)}, u32[]{:S(2)}) collective-permute-start(bf16[8,32,128]{2,1,0:T(8,128)(2,1)S(1)} %copy-done.7), channel_id=1, source_target_pairs={{0,3},{1,2},{2,1},{3,0},{4,7},{5,6},{6,5},{7,4},{8,11},{9,10},{10,... | collective-permute-start | bytes 196616 | tf_op jit(solution)/shard_map/ppermute | solution.py:520
  10.6 0.5 %collective-permute-start.4 = (bf16[8,32,128]{2,1,0:T(8,128)(2,1)S(1)}, bf16[8,32,128]{2,1,0:T(8,128)(2,1)S(1)}, u32[]{:S(2)}, u32[]{:S(2)}) collective-permute-start(bf16[8,32,128]{2,1,0:T(8,128)(2,1)S(1)} %copy-done.7), channel_id=1, source_target_pairs={{0,1},{1,0},{2,3},{3,2},{4,5},{5,4},{6,7},{7,6},{8,9},{9,8},{10,11... | collective-permute-start | bytes 196616 | tf_op jit(solution)/shard_map/ppermute | solution.py:520
  11.0 1.0 %collective-permute-start.5 = (bf16[8,32,128]{2,1,0:T(8,128)(2,1)S(1)}, bf16[8,32,128]{2,1,0:T(8,128)(2,1)S(1)}, u32[]{:S(2)}, u32[]{:S(2)}) collective-permute-start(bf16[8,32,128]{2,1,0:T(8,128)(2,1)S(1)} %copy-done.7), channel_id=1, source_target_pairs={{0,2},{1,3},{2,0},{3,1},{4,6},{5,7},{6,4},{7,5},{8,10},{9,11},{10,... | collective-permute-start | bytes 196616 | tf_op jit(solution)/shard_map/ppermute | solution.py:520
  12.0 0.4 %collective-permute-done.1.refs_2_.refs_4_ = bf16[80,256]{1,0:T(8,128)(2,1)S(1)} collective-permute-done((bf16[80,256]{1,0:T(8,128)(2,1)S(1)}, bf16[80,256]{1,0:T(8,128)(2,1)S(1)}, u32[]{:S(2)}, u32[]{:S(2)}) %collective-permute-start.1) | collective-permute-done | bytes 40992 | tf_op jit(solution)/shard_map/ppermute | solution.py:520
  12.5 0.0 copy-start.8
  12.5 0.0 copy-start.9
  12.6 4.6 %shard_map.196 = (bf16[8,8,256]{2,1,0:T(8,128)(2,1)}, f32[1024,128]{1,0:T(8,128)S(1)}) custom-call(bf16[80,256]{1,0:T(8,128)(2,1)S(1)} %get-tuple-element.11.refs_0_, bf16[80,256]{1,0:T(8,128)(2,1)S(1)} %collective-permute-done.refs_1_.refs_3_, bf16[80,256]{1,0:T(8,128)(2,1)S(1)} %collective-permute-done.1.refs_2_.refs_4_, ...), custom_call_target="tpu_custom_call" | custom-call | flops 3000000000 | tf_op jit(solution)/shard_map/pallas_call | solution.py:508
  17.3 2.1 %shard_map.197 = bf16[8,32,128]{2,1,0:T(8,128)(2,1)} custom-call(bf16[8,32,128]{2,1,0:T(8,128)(2,1)S(1)} %collective-permute-done.3.refs_0_, bf16[8,32,128]{2,1,0:T(8,128)(2,1)S(1)} %collective-permute-done.4.refs_1_, bf16[8,32,128]{2,1,0:T(8,128)(2,1)S(1)} %collective-permute-done.5.refs_2_, bf16[80,256]{1,0:T(8,128)(2,1)S(1)} %collective-permute-done.refs_1_.refs_3_, ...), custom_call_target="tpu_custom_call" | custom-call | flops 3000000000 | tf_op jit(solution)/shard_map/pallas_call | solution.py:508
  (30 shorter events, 0.1 us)
Async XLA Ops:
  0.6 0.8 %copy-start.7 = (bf16[8,32,128]{2,1,0:T(8,128)(2,1)S(1)}, bf16[8,32,128]{2,1,0:T(8,128)(2,1)}, u32[]{:S(2)}) copy-start(bf16[8,32,128]{2,1,0:T(8,128)(2,1)} %refs_8_.3) | copy-start | bytes 196612
  0.6 0.8 %copy-start.10 = (bf16[2,32,256]{2,1,0:T(8,128)(2,1)S(1)}, bf16[2,32,256]{2,1,0:T(8,128)(2,1)}, u32[]{:S(2)}) copy-start(bf16[2,32,256]{2,1,0:T(8,128)(2,1)} %refs_4_.1) | copy-start | bytes 98308
  0.6 0.8 %copy-start.16 = (bf16[128,8]{0,1:T(8,128)(2,1)S(1)}, bf16[128,8]{0,1:T(8,128)(2,1)}, u32[]{:S(2)}) copy-start(bf16[128,8]{0,1:T(8,128)(2,1)} %param.27) | copy-start | bytes 6148
  0.7 0.7 %copy-start.15 = (s32[8,32]{1,0:T(8,128)S(1)}, s32[8,32]{1,0:T(8,128)}, u32[]{:S(2)}) copy-start(s32[8,32]{1,0:T(8,128)} %refs_9_.3) | copy-start | bytes 3076
  0.8 0.7 %copy-start.17 = (s32[2,32]{1,0:T(2,128)S(1)}, s32[2,32]{1,0:T(2,128)}, u32[]{:S(2)}) copy-start(s32[2,32]{1,0:T(2,128)} %refs_3_.1) | copy-start | bytes 772
  1.5 11.0 %copy-start = (bf16[256,768]{1,0:T(8,128)(2,1)S(1)}, bf16[256,768]{1,0:T(8,128)(2,1)}, u32[]{:S(2)}) copy-start(bf16[256,768]{1,0:T(8,128)(2,1)} %refs_8_.2) | copy-start | bytes 1179652
  1.5 11.0 %copy-start.1 = (bf16[256,768]{1,0:T(8,128)(2,1)S(1)}, bf16[256,768]{1,0:T(8,128)(2,1)}, u32[]{:S(2)}) copy-start(bf16[256,768]{1,0:T(8,128)(2,1)} %refs_11_.2) | copy-start | bytes 1179652
  1.5 10.9 %copy-start.2 = (bf16[1024,128]{1,0:T(8,128)(2,1)S(1)}, bf16[1024,128]{1,0:T(8,128)(2,1)}, u32[]{:S(2)}) copy-start(bf16[1024,128]{1,0:T(8,128)(2,1)} %refs_14_.1) | copy-start | bytes 786436
  1.5 10.9 %copy-start.3 = (bf16[256,256]{1,0:T(8,128)(2,1)S(1)}, bf16[256,256]{1,0:T(8,128)(2,1)}, u32[]{:S(2)}) copy-start(bf16[256,256]{1,0:T(8,128)(2,1)} %refs_7_.1) | copy-start | bytes 393220
  1.5 10.9 %copy-start.4 = (bf16[256,256]{1,0:T(8,128)(2,1)S(1)}, bf16[256,256]{1,0:T(8,128)(2,1)}, u32[]{:S(2)}) copy-start(bf16[256,256]{1,0:T(8,128)(2,1)} %refs_9_.2) | copy-start | bytes 393220
  1.6 10.9 %copy-start.5 = (bf16[256,256]{1,0:T(8,128)(2,1)S(1)}, bf16[256,256]{1,0:T(8,128)(2,1)}, u32[]{:S(2)}) copy-start(bf16[256,256]{1,0:T(8,128)(2,1)} %refs_10_.2) | copy-start | bytes 393220
  1.6 10.9 %copy-start.6 = (bf16[256,256]{1,0:T(8,128)(2,1)S(1)}, bf16[256,256]{1,0:T(8,128)(2,1)}, u32[]{:S(2)}) copy-start(bf16[256,256]{1,0:T(8,128)(2,1)} %refs_12_.2) | copy-start | bytes 393220
  1.6 10.9 %copy-start.11 = (bf16[256,64]{0,1:T(8,128)(2,1)S(1)}, bf16[256,64]{0,1:T(8,128)(2,1)}, u32[]{:S(2)}) copy-start(bf16[256,64]{0,1:T(8,128)(2,1)} %param.32) | copy-start | bytes 98308
  1.6 10.9 %copy-start.14 = (bf16[23,256]{1,0:T(8,128)(2,1)S(1)}, bf16[23,256]{1,0:T(8,128)(2,1)}, u32[]{:S(2)}) copy-start(bf16[23,256]{1,0:T(8,128)(2,1)} %refs_6_.1) | copy-start | bytes 35332
  2.0 9.1 %collective-permute-start = (bf16[80,256]{1,0:T(8,128)(2,1)S(1)}, bf16[80,256]{1,0:T(8,128)(2,1)S(1)}, u32[]{:S(2)}, u32[]{:S(2)}) collective-permute-start(bf16[80,256]{1,0:T(8,128)(2,1)S(1)} %get-tuple-element.11.refs_0_), channel_id=1, source_target_pairs={{0,2},{1,3},{2,0},{3,1},{4,6},{5,7},{6,4},{7,5},{8,10},{9,11},{10,... | collective-permute-start | bytes 122888 | tf_op jit(solution)/shard_map/ppermute | solution.py:520
  6.1 6.4 %collective-permute-start.1 = (bf16[80,256]{1,0:T(8,128)(2,1)S(1)}, bf16[80,256]{1,0:T(8,128)(2,1)S(1)}, u32[]{:S(2)}, u32[]{:S(2)}) collective-permute-start(bf16[80,256]{1,0:T(8,128)(2,1)S(1)} %get-tuple-element.11.refs_0_), channel_id=1, source_target_pairs={{0,3},{1,2},{2,1},{3,0},{4,7},{5,6},{6,5},{7,4},{8,11},{9,10},{10,... | collective-permute-start | bytes 122888 | tf_op jit(solution)/shard_map/ppermute | solution.py:520
  7.4 5.0 %collective-permute-start.2 = (bf16[80,256]{1,0:T(8,128)(2,1)S(1)}, bf16[80,256]{1,0:T(8,128)(2,1)S(1)}, u32[]{:S(2)}, u32[]{:S(2)}) collective-permute-start(bf16[80,256]{1,0:T(8,128)(2,1)S(1)} %get-tuple-element.11.refs_0_), channel_id=1, source_target_pairs={{0,1},{1,0},{2,3},{3,2},{4,5},{5,4},{6,7},{7,6},{8,9},{9,8},{10,11... | collective-permute-start | bytes 122888 | tf_op jit(solution)/shard_map/ppermute | solution.py:520
  7.6 9.6 %collective-permute-start.3 = (bf16[8,32,128]{2,1,0:T(8,128)(2,1)S(1)}, bf16[8,32,128]{2,1,0:T(8,128)(2,1)S(1)}, u32[]{:S(2)}, u32[]{:S(2)}) collective-permute-start(bf16[8,32,128]{2,1,0:T(8,128)(2,1)S(1)} %copy-done.7), channel_id=1, source_target_pairs={{0,3},{1,2},{2,1},{3,0},{4,7},{5,6},{6,5},{7,4},{8,11},{9,10},{10,... | collective-permute-start | bytes 196616 | tf_op jit(solution)/shard_map/ppermute | solution.py:520
  10.6 6.7 %collective-permute-start.4 = (bf16[8,32,128]{2,1,0:T(8,128)(2,1)S(1)}, bf16[8,32,128]{2,1,0:T(8,128)(2,1)S(1)}, u32[]{:S(2)}, u32[]{:S(2)}) collective-permute-start(bf16[8,32,128]{2,1,0:T(8,128)(2,1)S(1)} %copy-done.7), channel_id=1, source_target_pairs={{0,1},{1,0},{2,3},{3,2},{4,5},{5,4},{6,7},{7,6},{8,9},{9,8},{10,11... | collective-permute-start | bytes 196616 | tf_op jit(solution)/shard_map/ppermute | solution.py:520
  11.0 6.2 %collective-permute-start.5 = (bf16[8,32,128]{2,1,0:T(8,128)(2,1)S(1)}, bf16[8,32,128]{2,1,0:T(8,128)(2,1)S(1)}, u32[]{:S(2)}, u32[]{:S(2)}) collective-permute-start(bf16[8,32,128]{2,1,0:T(8,128)(2,1)S(1)} %copy-done.7), channel_id=1, source_target_pairs={{0,2},{1,3},{2,0},{3,1},{4,6},{5,7},{6,4},{7,5},{8,10},{9,11},{10,... | collective-permute-start | bytes 196616 | tf_op jit(solution)/shard_map/ppermute | solution.py:520
  12.5 4.7 %copy-start.8 = (bf16[128,256]{1,0:T(8,128)(2,1)S(1)}, bf16[128,256]{1,0:T(8,128)(2,1)}, u32[]{:S(2)}) copy-start(bf16[128,256]{1,0:T(8,128)(2,1)} %refs_10_.3) | copy-start | bytes 196612
  12.5 4.7 %copy-start.9 = (bf16[128,256]{1,0:T(8,128)(2,1)S(1)}, bf16[128,256]{1,0:T(8,128)(2,1)}, u32[]{:S(2)}) copy-start(bf16[128,256]{1,0:T(8,128)(2,1)} %refs_11_.3) | copy-start | bytes 196612
  12.6 4.7 %copy-start.12 = (bf16[128,128]{1,0:T(8,128)(2,1)S(1)}, bf16[128,128]{1,0:T(8,128)(2,1)}, u32[]{:S(2)}) copy-start(bf16[128,128]{1,0:T(8,128)(2,1)} %refs_12_.3) | copy-start | bytes 98308
  12.6 4.7 %copy-start.13 = (bf16[128,128]{1,0:T(8,128)(2,1)S(1)}, bf16[128,128]{1,0:T(8,128)(2,1)}, u32[]{:S(2)}) copy-start(bf16[128,128]{1,0:T(8,128)(2,1)} %refs_13_.1) | copy-start | bytes 98308
  (1 other events, 0.7 us)

commit v8 on v7

--- a/solution.py
+++ b/solution.py
@@ -425,22 +425,23 @@
     gather = zero_one(iota((residues, tokens), 1) // count == iota((residues, tokens), 0))
     left = mul(gather, left).astype(BF16)
     right = opm[:, hidden:]
-    for c in range(0, hidden, 2):
-        pair_w = jnp.concatenate(
-            [outer_w[(c + k) * hidden : (c + k + 1) * hidden, :] for k in range(2)], axis=1
-        )
-        part = mul(right, pair_w)
-        lifted[c], lifted[c + 1] = part[:, :pair_width], part[:, pair_width:]
-    for j in range(0, residues, 2):
+    for c in range(0, hidden, 4):
+        four_w = jnp.concatenate(
+            [outer_w[(c + k) * hidden : (c + k + 1) * hidden, :] for k in range(4)], axis=1
+        )
+        part = mul(right, four_w)
+        for k in range(4):
+            lifted[c + k] = part[:, k * pair_width : (k + 1) * pair_width]
+    for j in range(0, residues, 4):
         part = jnp.concatenate(
             [
                 lifted[:, (j + k) * count : (j + k + 1) * count, :].reshape(deep, pair_width)
-                for k in range(2)
+                for k in range(4)
             ],
             axis=1,
         )
         part = mul(left, part.astype(BF16)) * (1.0 / count)
-        for k in range(2):
+        for k in range(4):
             at = slice((j + k) * residues, (j + k + 1) * residues)
             update_ref[at, :] = part[:, k * pair_width : (k + 1) * pair_width]
 
@@ -483,7 +484,7 @@
 
     shown = mul(valid[...].astype(BF16), column[...])
     right_w = jnp.concatenate([proj[:, C_TRI:], gates[:, C_TRI:]], axis=1)
-    step = 8
+    step = min(residues, 16)
     for k in range(0, residues, step):
         here = slice(k * residues, (k + step) * residues)
         both = mul(normal(one[here, :]).astype(BF16), right_w)

time: 19.5 us -> 19.5 us (level)
  no operation moved by 1% of the time
where the time goes in v8:
time: 19.5 us; the launch traced here: 19.4 us
  starting transfers between devices  10.1 us (52%)
  Pallas kernels  7.11 us (36%)
  between operations  0.93 us (5%)
  local copies, waits for them, and re-layouts  0.81 us (4%)
  waiting for transfers between devices  0.43 us (2%)
    ppermute x6, starting transfers between devices, swap(): return lax.ppermute(array, 'axial', [(i, i ^ r) for i in range(n)])  10.1 us
    pallas_call x4, Pallas kernels, call(): pl.pallas_call(kernel, out_shape=out_shape, in_specs=[vmem] * len(args),...  7.11 us
    unnamed x38, local copies, waits for them, and re-layouts  0.81 us
    ppermute x6, waiting for transfers between devices, swap(): return lax.ppermute(array, 'axial', [(i, i ^ r) for i in range(n)])  0.43 us
  transfers between devices with their start and end apart: 6, of which 1 were waited for; matrix products, arithmetic and copies ran while one was open for 0% of the time, Pallas kernels for 24%

profile of v8, /device:TPU:0, one launch (start us, length us, event | category | flops | bytes accessed | tf_op | source)
XLA Modules:
  0.0 19.4 jit_solution(13385561851311999315)
XLA Ops:
  0.7 0.1 shard_map.194
  0.7 0.0 copy-start.15
  0.8 0.0 copy-start.17
  0.8 0.0 copy-start.18
  0.8 0.7 %copy-done.7 = bf16[8,32,128]{2,1,0:T(8,128)(2,1)S(1)} copy-done((bf16[8,32,128]{2,1,0:T(8,128)(2,1)S(1)}, bf16[8,32,128]{2,1,0:T(8,128)(2,1)}, u32[]{:S(2)}) %copy-start.7) | copy-done | bytes 65560
  1.5 0.0 copy-start
  1.5 0.0 copy-start.1
  1.5 0.0 copy-start.2
  1.5 0.0 copy-start.3
  1.5 0.0 copy-start.4
  1.6 0.0 copy-start.5
  1.6 0.0 copy-start.14
  1.6 0.3 %shard_map.195 = (bf16[80,256]{1,0:T(8,128)(2,1)S(1)}, f32[32,256]{1,0:T(8,128)S(1)}) custom-call(bf16[8,32,128]{2,1,0:T(8,128)(2,1)S(1)} %copy-done.7, bf16[8,128]{1,0:T(8,128)(2,1)S(1)} %bitcast.4, s32[8,32]{1,0:T(8,128)S(1)} %copy-done.15, s32[2,32]{1,0:T(2,128)S(1)} %copy-done.17, bf16[2,32,256]{2,1,0:T(8,128)(2,1)S(1)} %copy-done.10, ...), custom_call_target="tpu_custom_call" | custom-call | flops 3000000000 | tf_op jit(solution)/shard_map/pallas_call | solution.py:509
  2.0 4.1 %collective-permute-start = (bf16[80,256]{1,0:T(8,128)(2,1)S(1)}, bf16[80,256]{1,0:T(8,128)(2,1)S(1)}, u32[]{:S(2)}, u32[]{:S(2)}) collective-permute-start(bf16[80,256]{1,0:T(8,128)(2,1)S(1)} %get-tuple-element.11.refs_0_), channel_id=1, source_target_pairs={{0,2},{1,3},{2,0},{3,1},{4,6},{5,7},{6,4},{7,5},{8,10},{9,11},{10,... | collective-permute-start | bytes 122888 | tf_op jit(solution)/shard_map/ppermute | solution.py:521
  6.1 1.3 %collective-permute-start.1 = (bf16[80,256]{1,0:T(8,128)(2,1)S(1)}, bf16[80,256]{1,0:T(8,128)(2,1)S(1)}, u32[]{:S(2)}, u32[]{:S(2)}) collective-permute-start(bf16[80,256]{1,0:T(8,128)(2,1)S(1)} %get-tuple-element.11.refs_0_), channel_id=1, source_target_pairs={{0,3},{1,2},{2,1},{3,0},{4,7},{5,6},{6,5},{7,4},{8,11},{9,10},{10,... | collective-permute-start | bytes 122888 | tf_op jit(solution)/shard_map/ppermute | solution.py:521
  7.4 0.2 %collective-permute-start.2 = (bf16[80,256]{1,0:T(8,128)(2,1)S(1)}, bf16[80,256]{1,0:T(8,128)(2,1)S(1)}, u32[]{:S(2)}, u32[]{:S(2)}) collective-permute-start(bf16[80,256]{1,0:T(8,128)(2,1)S(1)} %get-tuple-element.11.refs_0_), channel_id=1, source_target_pairs={{0,1},{1,0},{2,3},{3,2},{4,5},{5,4},{6,7},{7,6},{8,9},{9,8},{10,11... | collective-permute-start | bytes 122888 | tf_op jit(solution)/shard_map/ppermute | solution.py:521
  7.6 2.9 %collective-permute-start.3 = (bf16[8,32,128]{2,1,0:T(8,128)(2,1)S(1)}, bf16[8,32,128]{2,1,0:T(8,128)(2,1)S(1)}, u32[]{:S(2)}, u32[]{:S(2)}) collective-permute-start(bf16[8,32,128]{2,1,0:T(8,128)(2,1)S(1)} %copy-done.7), channel_id=1, source_target_pairs={{0,3},{1,2},{2,1},{3,0},{4,7},{5,6},{6,5},{7,4},{8,11},{9,10},{10,... | collective-permute-start | bytes 196616 | tf_op jit(solution)/shard_map/ppermute | solution.py:521
  10.6 0.5 %collective-permute-start.4 = (bf16[8,32,128]{2,1,0:T(8,128)(2,1)S(1)}, bf16[8,32,128]{2,1,0:T(8,128)(2,1)S(1)}, u32[]{:S(2)}, u32[]{:S(2)}) collective-permute-start(bf16[8,32,128]{2,1,0:T(8,128)(2,1)S(1)} %copy-done.7), channel_id=1, source_target_pairs={{0,1},{1,0},{2,3},{3,2},{4,5},{5,4},{6,7},{7,6},{8,9},{9,8},{10,11... | collective-permute-start | bytes 196616 | tf_op jit(solution)/shard_map/ppermute | solution.py:521
  11.0 1.0 %collective-permute-start.5 = (bf16[8,32,128]{2,1,0:T(8,128)(2,1)S(1)}, bf16[8,32,128]{2,1,0:T(8,128)(2,1)S(1)}, u32[]{:S(2)}, u32[]{:S(2)}) collective-permute-start(bf16[8,32,128]{2,1,0:T(8,128)(2,1)S(1)} %copy-done.7), channel_id=1, source_target_pairs={{0,2},{1,3},{2,0},{3,1},{4,6},{5,7},{6,4},{7,5},{8,10},{9,11},{10,... | collective-permute-start | bytes 196616 | tf_op jit(solution)/shard_map/ppermute | solution.py:521
  12.0 0.4 %collective-permute-done.1.refs_2_.refs_4_ = bf16[80,256]{1,0:T(8,128)(2,1)S(1)} collective-permute-done((bf16[80,256]{1,0:T(8,128)(2,1)S(1)}, bf16[80,256]{1,0:T(8,128)(2,1)S(1)}, u32[]{:S(2)}, u32[]{:S(2)}) %collective-permute-start.1) | collective-permute-done | bytes 40992 | tf_op jit(solution)/shard_map/ppermute | solution.py:521
  12.5 0.0 copy-start.9
  12.6 0.0 copy-start.12
  12.6 4.6 %shard_map.196 = (bf16[8,8,256]{2,1,0:T(8,128)(2,1)}, f32[1024,128]{1,0:T(8,128)S(1)}) custom-call(bf16[80,256]{1,0:T(8,128)(2,1)S(1)} %get-tuple-element.11.refs_0_, bf16[80,256]{1,0:T(8,128)(2,1)S(1)} %collective-permute-done.refs_1_.refs_3_, bf16[80,256]{1,0:T(8,128)(2,1)S(1)} %collective-permute-done.1.refs_2_.refs_4_, ...), custom_call_target="tpu_custom_call" | custom-call | flops 3000000000 | tf_op jit(solution)/shard_map/pallas_call | solution.py:509
  17.3 2.1 %shard_map.197 = bf16[8,32,128]{2,1,0:T(8,128)(2,1)} custom-call(bf16[8,32,128]{2,1,0:T(8,128)(2,1)S(1)} %collective-permute-done.3.refs_0_, bf16[8,32,128]{2,1,0:T(8,128)(2,1)S(1)} %collective-permute-done.4.refs_1_, bf16[8,32,128]{2,1,0:T(8,128)(2,1)S(1)} %collective-permute-done.5.refs_2_, bf16[80,256]{1,0:T(8,128)(2,1)S(1)} %collective-permute-done.refs_1_.refs_3_, ...), custom_call_target="tpu_custom_call" | custom-call | flops 3000000000 | tf_op jit(solution)/shard_map/pallas_call | solution.py:509
  (30 shorter events, 0.1 us)
Async XLA Ops:
  0.6 0.8 %copy-start.7 = (bf16[8,32,128]{2,1,0:T(8,128)(2,1)S(1)}, bf16[8,32,128]{2,1,0:T(8,128)(2,1)}, u32[]{:S(2)}) copy-start(bf16[8,32,128]{2,1,0:T(8,128)(2,1)} %refs_8_.3) | copy-start | bytes 196612
  0.6 0.8 %copy-start.10 = (bf16[2,32,256]{2,1,0:T(8,128)(2,1)S(1)}, bf16[2,32,256]{2,1,0:T(8,128)(2,1)}, u32[]{:S(2)}) copy-start(bf16[2,32,256]{2,1,0:T(8,128)(2,1)} %refs_4_.1) | copy-start | bytes 98308
  0.6 0.8 %copy-start.16 = (bf16[128,8]{0,1:T(8,128)(2,1)S(1)}, bf16[128,8]{0,1:T(8,128)(2,1)}, u32[]{:S(2)}) copy-start(bf16[128,8]{0,1:T(8,128)(2,1)} %param.27) | copy-start | bytes 6148
  0.7 0.7 %copy-start.15 = (s32[8,32]{1,0:T(8,128)S(1)}, s32[8,32]{1,0:T(8,128)}, u32[]{:S(2)}) copy-start(s32[8,32]{1,0:T(8,128)} %refs_9_.3) | copy-start | bytes 3076
  0.8 0.7 %copy-start.17 = (s32[2,32]{1,0:T(2,128)S(1)}, s32[2,32]{1,0:T(2,128)}, u32[]{:S(2)}) copy-start(s32[2,32]{1,0:T(2,128)} %refs_3_.1) | copy-start | bytes 772
  1.5 11.0 %copy-start = (bf16[256,768]{1,0:T(8,128)(2,1)S(1)}, bf16[256,768]{1,0:T(8,128)(2,1)}, u32[]{:S(2)}) copy-start(bf16[256,768]{1,0:T(8,128)(2,1)} %refs_8_.2) | copy-start | bytes 1179652
  1.5 11.0 %copy-start.1 = (bf16[256,768]{1,0:T(8,128)(2,1)S(1)}, bf16[256,768]{1,0:T(8,128)(2,1)}, u32[]{:S(2)}) copy-start(bf16[256,768]{1,0:T(8,128)(2,1)} %refs_11_.2) | copy-start | bytes 1179652
  1.5 10.9 %copy-start.2 = (bf16[1024,128]{1,0:T(8,128)(2,1)S(1)}, bf16[1024,128]{1,0:T(8,128)(2,1)}, u32[]{:S(2)}) copy-start(bf16[1024,128]{1,0:T(8,128)(2,1)} %refs_14_.1) | copy-start | bytes 786436
  1.5 10.9 %copy-start.3 = (bf16[256,256]{1,0:T(8,128)(2,1)S(1)}, bf16[256,256]{1,0:T(8,128)(2,1)}, u32[]{:S(2)}) copy-start(bf16[256,256]{1,0:T(8,128)(2,1)} %refs_7_.1) | copy-start | bytes 393220
  1.5 10.9 %copy-start.4 = (bf16[256,256]{1,0:T(8,128)(2,1)S(1)}, bf16[256,256]{1,0:T(8,128)(2,1)}, u32[]{:S(2)}) copy-start(bf16[256,256]{1,0:T(8,128)(2,1)} %refs_9_.2) | copy-start | bytes 393220
  1.6 10.9 %copy-start.5 = (bf16[256,256]{1,0:T(8,128)(2,1)S(1)}, bf16[256,256]{1,0:T(8,128)(2,1)}, u32[]{:S(2)}) copy-start(bf16[256,256]{1,0:T(8,128)(2,1)} %refs_10_.2) | copy-start | bytes 393220
  1.6 10.9 %copy-start.6 = (bf16[256,256]{1,0:T(8,128)(2,1)S(1)}, bf16[256,256]{1,0:T(8,128)(2,1)}, u32[]{:S(2)}) copy-start(bf16[256,256]{1,0:T(8,128)(2,1)} %refs_12_.2) | copy-start | bytes 393220
  1.6 10.9 %copy-start.11 = (bf16[256,64]{0,1:T(8,128)(2,1)S(1)}, bf16[256,64]{0,1:T(8,128)(2,1)}, u32[]{:S(2)}) copy-start(bf16[256,64]{0,1:T(8,128)(2,1)} %param.32) | copy-start | bytes 98308
  1.6 10.9 %copy-start.14 = (bf16[23,256]{1,0:T(8,128)(2,1)S(1)}, bf16[23,256]{1,0:T(8,128)(2,1)}, u32[]{:S(2)}) copy-start(bf16[23,256]{1,0:T(8,128)(2,1)} %refs_6_.1) | copy-start | bytes 35332
  2.0 9.1 %collective-permute-start = (bf16[80,256]{1,0:T(8,128)(2,1)S(1)}, bf16[80,256]{1,0:T(8,128)(2,1)S(1)}, u32[]{:S(2)}, u32[]{:S(2)}) collective-permute-start(bf16[80,256]{1,0:T(8,128)(2,1)S(1)} %get-tuple-element.11.refs_0_), channel_id=1, source_target_pairs={{0,2},{1,3},{2,0},{3,1},{4,6},{5,7},{6,4},{7,5},{8,10},{9,11},{10,... | collective-permute-start | bytes 122888 | tf_op jit(solution)/shard_map/ppermute | solution.py:521
  6.1 6.4 %collective-permute-start.1 = (bf16[80,256]{1,0:T(8,128)(2,1)S(1)}, bf16[80,256]{1,0:T(8,128)(2,1)S(1)}, u32[]{:S(2)}, u32[]{:S(2)}) collective-permute-start(bf16[80,256]{1,0:T(8,128)(2,1)S(1)} %get-tuple-element.11.refs_0_), channel_id=1, source_target_pairs={{0,3},{1,2},{2,1},{3,0},{4,7},{5,6},{6,5},{7,4},{8,11},{9,10},{10,... | collective-permute-start | bytes 122888 | tf_op jit(solution)/shard_map/ppermute | solution.py:521
  7.4 5.0 %collective-permute-start.2 = (bf16[80,256]{1,0:T(8,128)(2,1)S(1)}, bf16[80,256]{1,0:T(8,128)(2,1)S(1)}, u32[]{:S(2)}, u32[]{:S(2)}) collective-permute-start(bf16[80,256]{1,0:T(8,128)(2,1)S(1)} %get-tuple-element.11.refs_0_), channel_id=1, source_target_pairs={{0,1},{1,0},{2,3},{3,2},{4,5},{5,4},{6,7},{7,6},{8,9},{9,8},{10,11... | collective-permute-start | bytes 122888 | tf_op jit(solution)/shard_map/ppermute | solution.py:521
  7.6 9.6 %collective-permute-start.3 = (bf16[8,32,128]{2,1,0:T(8,128)(2,1)S(1)}, bf16[8,32,128]{2,1,0:T(8,128)(2,1)S(1)}, u32[]{:S(2)}, u32[]{:S(2)}) collective-permute-start(bf16[8,32,128]{2,1,0:T(8,128)(2,1)S(1)} %copy-done.7), channel_id=1, source_target_pairs={{0,3},{1,2},{2,1},{3,0},{4,7},{5,6},{6,5},{7,4},{8,11},{9,10},{10,... | collective-permute-start | bytes 196616 | tf_op jit(solution)/shard_map/ppermute | solution.py:521
  10.6 6.7 %collective-permute-start.4 = (bf16[8,32,128]{2,1,0:T(8,128)(2,1)S(1)}, bf16[8,32,128]{2,1,0:T(8,128)(2,1)S(1)}, u32[]{:S(2)}, u32[]{:S(2)}) collective-permute-start(bf16[8,32,128]{2,1,0:T(8,128)(2,1)S(1)} %copy-done.7), channel_id=1, source_target_pairs={{0,1},{1,0},{2,3},{3,2},{4,5},{5,4},{6,7},{7,6},{8,9},{9,8},{10,11... | collective-permute-start | bytes 196616 | tf_op jit(solution)/shard_map/ppermute | solution.py:521
  11.0 6.2 %collective-permute-start.5 = (bf16[8,32,128]{2,1,0:T(8,128)(2,1)S(1)}, bf16[8,32,128]{2,1,0:T(8,128)(2,1)S(1)}, u32[]{:S(2)}, u32[]{:S(2)}) collective-permute-start(bf16[8,32,128]{2,1,0:T(8,128)(2,1)S(1)} %copy-done.7), channel_id=1, source_target_pairs={{0,2},{1,3},{2,0},{3,1},{4,6},{5,7},{6,4},{7,5},{8,10},{9,11},{10,... | collective-permute-start | bytes 196616 | tf_op jit(solution)/shard_map/ppermute | solution.py:521
  12.5 4.7 %copy-start.8 = (bf16[128,256]{1,0:T(8,128)(2,1)S(1)}, bf16[128,256]{1,0:T(8,128)(2,1)}, u32[]{:S(2)}) copy-start(bf16[128,256]{1,0:T(8,128)(2,1)} %refs_10_.3) | copy-start | bytes 196612
  12.5 4.7 %copy-start.9 = (bf16[128,256]{1,0:T(8,128)(2,1)S(1)}, bf16[128,256]{1,0:T(8,128)(2,1)}, u32[]{:S(2)}) copy-start(bf16[128,256]{1,0:T(8,128)(2,1)} %refs_11_.3) | copy-start | bytes 196612
  12.6 4.7 %copy-start.12 = (bf16[128,128]{1,0:T(8,128)(2,1)S(1)}, bf16[128,128]{1,0:T(8,128)(2,1)}, u32[]{:S(2)}) copy-start(bf16[128,128]{1,0:T(8,128)(2,1)} %refs_12_.3) | copy-start | bytes 98308
  12.6 4.7 %copy-start.13 = (bf16[128,128]{1,0:T(8,128)(2,1)S(1)}, bf16[128,128]{1,0:T(8,128)(2,1)}, u32[]{:S(2)}) copy-start(bf16[128,128]{1,0:T(8,128)(2,1)} %refs_13_.1) | copy-start | bytes 98308
  (1 other events, 0.7 us)

commit v9 on v8

--- a/solution.py
+++ b/solution.py
@@ -330,7 +330,7 @@
     packets, turn, hidden_keys, table = refs[:n], refs[n], refs[n + 1], refs[n + 2]
     refs = refs[n + 3 :]
     row_q, row_kvg, row_out, col_q, col_kvg, col_out, lift, outer_w = refs[:8]
-    align_ref, update_ref, lifted = refs[8:]
+    align_ref, update_ref, lifted, held = refs[8:]
     kinds, width = table.shape
     residues, lanes = hidden_keys.shape
     pair_width = outer_w.shape[1]
@@ -369,7 +369,8 @@
     mixed = (jnp.concatenate(rows, axis=0) * gate).astype(BF16)
     msa_one = (zero + mul(mixed, row_out[...])).astype(BF16)
 
-    one = mul(turn[...], msa_one)
+    held[...] = mul(turn[...], msa_one)
+    one = held[...]
     query, keys, values, gate = project(one, col_q, col_kvg)
     group = min(tokens, 128)
     sites = group // count
@@ -583,6 +584,7 @@
         ),
         [
             pltpu.VMEM((MEAN_HIDDEN_SIZE, count * residues, pair_width), F32),
+            pltpu.VMEM((count * residues, width), F32),
         ],
         16,
         packet,

time: 19.5 us -> 19.5 us (level)
  no operation moved by 1% of the time
where the time goes in v9:
time: 19.5 us; the launch traced here: 19.4 us
  starting transfers between devices  10.1 us (52%)
  Pallas kernels  7.11 us (36%)
  between operations  0.93 us (5%)
  local copies, waits for them, and re-layouts  0.81 us (4%)
  waiting for transfers between devices  0.43 us (2%)
    ppermute x6, starting transfers between devices, swap(): return lax.ppermute(array, 'axial', [(i, i ^ r) for i in range(n)])  10.1 us
    pallas_call x4, Pallas kernels, call(): pl.pallas_call(kernel, out_shape=out_shape, in_specs=[vmem] * len(args),...  7.11 us
    unnamed x38, local copies, waits for them, and re-layouts  0.81 us
    ppermute x6, waiting for transfers between devices, swap(): return lax.ppermute(array, 'axial', [(i, i ^ r) for i in range(n)])  0.43 us
  transfers between devices with their start and end apart: 6, of which 1 were waited for; matrix products, arithmetic and copies ran while one was open for 0% of the time, Pallas kernels for 24%

profile of v9, /device:TPU:0, one launch (start us, length us, event | category | flops | bytes accessed | tf_op | source)
XLA Modules:
  0.0 19.4 jit_solution(13385561851311999315)
XLA Ops:
  0.7 0.1 shard_map.194
  0.7 0.0 copy-start.15
  0.8 0.0 copy-start.17
  0.8 0.0 copy-start.18
  0.8 0.7 %copy-done.7 = bf16[8,32,128]{2,1,0:T(8,128)(2,1)S(1)} copy-done((bf16[8,32,128]{2,1,0:T(8,128)(2,1)S(1)}, bf16[8,32,128]{2,1,0:T(8,128)(2,1)}, u32[]{:S(2)}) %copy-start.7) | copy-done | bytes 65560
  1.5 0.0 copy-start
  1.5 0.0 copy-start.1
  1.5 0.0 copy-start.2
  1.5 0.0 copy-start.3
  1.5 0.0 copy-start.4
  1.6 0.0 copy-start.5
  1.6 0.0 copy-start.14
  1.6 0.3 %shard_map.195 = (bf16[80,256]{1,0:T(8,128)(2,1)S(1)}, f32[32,256]{1,0:T(8,128)S(1)}) custom-call(bf16[8,32,128]{2,1,0:T(8,128)(2,1)S(1)} %copy-done.7, bf16[8,128]{1,0:T(8,128)(2,1)S(1)} %bitcast.4, s32[8,32]{1,0:T(8,128)S(1)} %copy-done.15, s32[2,32]{1,0:T(2,128)S(1)} %copy-done.17, bf16[2,32,256]{2,1,0:T(8,128)(2,1)S(1)} %copy-done.10, ...), custom_call_target="tpu_custom_call" | custom-call | flops 3000000000 | tf_op jit(solution)/shard_map/pallas_call | solution.py:510
  2.0 4.1 %collective-permute-start = (bf16[80,256]{1,0:T(8,128)(2,1)S(1)}, bf16[80,256]{1,0:T(8,128)(2,1)S(1)}, u32[]{:S(2)}, u32[]{:S(2)}) collective-permute-start(bf16[80,256]{1,0:T(8,128)(2,1)S(1)} %get-tuple-element.11.refs_0_), channel_id=1, source_target_pairs={{0,2},{1,3},{2,0},{3,1},{4,6},{5,7},{6,4},{7,5},{8,10},{9,11},{10,... | collective-permute-start | bytes 122888 | tf_op jit(solution)/shard_map/ppermute | solution.py:522
  6.1 1.3 %collective-permute-start.1 = (bf16[80,256]{1,0:T(8,128)(2,1)S(1)}, bf16[80,256]{1,0:T(8,128)(2,1)S(1)}, u32[]{:S(2)}, u32[]{:S(2)}) collective-permute-start(bf16[80,256]{1,0:T(8,128)(2,1)S(1)} %get-tuple-element.11.refs_0_), channel_id=1, source_target_pairs={{0,3},{1,2},{2,1},{3,0},{4,7},{5,6},{6,5},{7,4},{8,11},{9,10},{10,... | collective-permute-start | bytes 122888 | tf_op jit(solution)/shard_map/ppermute | solution.py:522
  7.4 0.2 %collective-permute-start.2 = (bf16[80,256]{1,0:T(8,128)(2,1)S(1)}, bf16[80,256]{1,0:T(8,128)(2,1)S(1)}, u32[]{:S(2)}, u32[]{:S(2)}) collective-permute-start(bf16[80,256]{1,0:T(8,128)(2,1)S(1)} %get-tuple-element.11.refs_0_), channel_id=1, source_target_pairs={{0,1},{1,0},{2,3},{3,2},{4,5},{5,4},{6,7},{7,6},{8,9},{9,8},{10,11... | collective-permute-start | bytes 122888 | tf_op jit(solution)/shard_map/ppermute | solution.py:522
  7.6 2.9 %collective-permute-start.3 = (bf16[8,32,128]{2,1,0:T(8,128)(2,1)S(1)}, bf16[8,32,128]{2,1,0:T(8,128)(2,1)S(1)}, u32[]{:S(2)}, u32[]{:S(2)}) collective-permute-start(bf16[8,32,128]{2,1,0:T(8,128)(2,1)S(1)} %copy-done.7), channel_id=1, source_target_pairs={{0,3},{1,2},{2,1},{3,0},{4,7},{5,6},{6,5},{7,4},{8,11},{9,10},{10,... | collective-permute-start | bytes 196616 | tf_op jit(solution)/shard_map/ppermute | solution.py:522
  10.6 0.5 %collective-permute-start.4 = (bf16[8,32,128]{2,1,0:T(8,128)(2,1)S(1)}, bf16[8,32,128]{2,1,0:T(8,128)(2,1)S(1)}, u32[]{:S(2)}, u32[]{:S(2)}) collective-permute-start(bf16[8,32,128]{2,1,0:T(8,128)(2,1)S(1)} %copy-done.7), channel_id=1, source_target_pairs={{0,1},{1,0},{2,3},{3,2},{4,5},{5,4},{6,7},{7,6},{8,9},{9,8},{10,11... | collective-permute-start | bytes 196616 | tf_op jit(solution)/shard_map/ppermute | solution.py:522
  11.0 1.0 %collective-permute-start.5 = (bf16[8,32,128]{2,1,0:T(8,128)(2,1)S(1)}, bf16[8,32,128]{2,1,0:T(8,128)(2,1)S(1)}, u32[]{:S(2)}, u32[]{:S(2)}) collective-permute-start(bf16[8,32,128]{2,1,0:T(8,128)(2,1)S(1)} %copy-done.7), channel_id=1, source_target_pairs={{0,2},{1,3},{2,0},{3,1},{4,6},{5,7},{6,4},{7,5},{8,10},{9,11},{10,... | collective-permute-start | bytes 196616 | tf_op jit(solution)/shard_map/ppermute | solution.py:522
  12.0 0.4 %collective-permute-done.1.refs_2_.refs_4_ = bf16[80,256]{1,0:T(8,128)(2,1)S(1)} collective-permute-done((bf16[80,256]{1,0:T(8,128)(2,1)S(1)}, bf16[80,256]{1,0:T(8,128)(2,1)S(1)}, u32[]{:S(2)}, u32[]{:S(2)}) %collective-permute-start.1) | collective-permute-done | bytes 40992 | tf_op jit(solution)/shard_map/ppermute | solution.py:522
  12.5 0.0 copy-start.9
  12.6 0.0 copy-start.12
  12.6 4.6 %shard_map.196 = (bf16[8,8,256]{2,1,0:T(8,128)(2,1)}, f32[1024,128]{1,0:T(8,128)S(1)}) custom-call(bf16[80,256]{1,0:T(8,128)(2,1)S(1)} %get-tuple-element.11.refs_0_, bf16[80,256]{1,0:T(8,128)(2,1)S(1)} %collective-permute-done.refs_1_.refs_3_, bf16[80,256]{1,0:T(8,128)(2,1)S(1)} %collective-permute-done.1.refs_2_.refs_4_, ...), custom_call_target="tpu_custom_call" | custom-call | flops 3000000000 | tf_op jit(solution)/shard_map/pallas_call | solution.py:510
  17.3 2.1 %shard_map.197 = bf16[8,32,128]{2,1,0:T(8,128)(2,1)} custom-call(bf16[8,32,128]{2,1,0:T(8,128)(2,1)S(1)} %collective-permute-done.3.refs_0_, bf16[8,32,128]{2,1,0:T(8,128)(2,1)S(1)} %collective-permute-done.4.refs_1_, bf16[8,32,128]{2,1,0:T(8,128)(2,1)S(1)} %collective-permute-done.5.refs_2_, bf16[80,256]{1,0:T(8,128)(2,1)S(1)} %collective-permute-done.refs_1_.refs_3_, ...), custom_call_target="tpu_custom_call" | custom-call | flops 3000000000 | tf_op jit(solution)/shard_map/pallas_call | solution.py:510
  (30 shorter events, 0.1 us)
Async XLA Ops:
  0.6 0.8 %copy-start.7 = (bf16[8,32,128]{2,1,0:T(8,128)(2,1)S(1)}, bf16[8,32,128]{2,1,0:T(8,128)(2,1)}, u32[]{:S(2)}) copy-start(bf16[8,32,128]{2,1,0:T(8,128)(2,1)} %refs_8_.3) | copy-start | bytes 196612
  0.6 0.8 %copy-start.10 = (bf16[2,32,256]{2,1,0:T(8,128)(2,1)S(1)}, bf16[2,32,256]{2,1,0:T(8,128)(2,1)}, u32[]{:S(2)}) copy-start(bf16[2,32,256]{2,1,0:T(8,128)(2,1)} %refs_4_.1) | copy-start | bytes 98308
  0.6 0.8 %copy-start.16 = (bf16[128,8]{0,1:T(8,128)(2,1)S(1)}, bf16[128,8]{0,1:T(8,128)(2,1)}, u32[]{:S(2)}) copy-start(bf16[128,8]{0,1:T(8,128)(2,1)} %param.27) | copy-start | bytes 6148
  0.7 0.7 %copy-start.15 = (s32[8,32]{1,0:T(8,128)S(1)}, s32[8,32]{1,0:T(8,128)}, u32[]{:S(2)}) copy-start(s32[8,32]{1,0:T(8,128)} %refs_9_.3) | copy-start | bytes 3076
  0.8 0.7 %copy-start.17 = (s32[2,32]{1,0:T(2,128)S(1)}, s32[2,32]{1,0:T(2,128)}, u32[]{:S(2)}) copy-start(s32[2,32]{1,0:T(2,128)} %refs_3_.1) | copy-start | bytes 772
  1.5 11.0 %copy-start = (bf16[256,768]{1,0:T(8,128)(2,1)S(1)}, bf16[256,768]{1,0:T(8,128)(2,1)}, u32[]{:S(2)}) copy-start(bf16[256,768]{1,0:T(8,128)(2,1)} %refs_8_.2) | copy-start | bytes 1179652
  1.5 11.0 %copy-start.1 = (bf16[256,768]{1,0:T(8,128)(2,1)S(1)}, bf16[256,768]{1,0:T(8,128)(2,1)}, u32[]{:S(2)}) copy-start(bf16[256,768]{1,0:T(8,128)(2,1)} %refs_11_.2) | copy-start | bytes 1179652
  1.5 10.9 %copy-start.2 = (bf16[1024,128]{1,0:T(8,128)(2,1)S(1)}, bf16[1024,128]{1,0:T(8,128)(2,1)}, u32[]{:S(2)}) copy-start(bf16[1024,128]{1,0:T(8,128)(2,1)} %refs_14_.1) | copy-start | bytes 786436
  1.5 10.9 %copy-start.3 = (bf16[256,256]{1,0:T(8,128)(2,1)S(1)}, bf16[256,256]{1,0:T(8,128)(2,1)}, u32[]{:S(2)}) copy-start(bf16[256,256]{1,0:T(8,128)(2,1)} %refs_7_.1) | copy-start | bytes 393220
  1.5 10.9 %copy-start.4 = (bf16[256,256]{1,0:T(8,128)(2,1)S(1)}, bf16[256,256]{1,0:T(8,128)(2,1)}, u32[]{:S(2)}) copy-start(bf16[256,256]{1,0:T(8,128)(2,1)} %refs_9_.2) | copy-start | bytes 393220
  1.6 10.9 %copy-start.5 = (bf16[256,256]{1,0:T(8,128)(2,1)S(1)}, bf16[256,256]{1,0:T(8,128)(2,1)}, u32[]{:S(2)}) copy-start(bf16[256,256]{1,0:T(8,128)(2,1)} %refs_10_.2) | copy-start | bytes 393220
  1.6 10.9 %copy-start.6 = (bf16[256,256]{1,0:T(8,128)(2,1)S(1)}, bf16[256,256]{1,0:T(8,128)(2,1)}, u32[]{:S(2)}) copy-start(bf16[256,256]{1,0:T(8,128)(2,1)} %refs_12_.2) | copy-start | bytes 393220
  1.6 10.9 %copy-start.11 = (bf16[256,64]{0,1:T(8,128)(2,1)S(1)}, bf16[256,64]{0,1:T(8,128)(2,1)}, u32[]{:S(2)}) copy-start(bf16[256,64]{0,1:T(8,128)(2,1)} %param.32) | copy-start | bytes 98308
  1.6 10.9 %copy-start.14 = (bf16[23,256]{1,0:T(8,128)(2,1)S(1)}, bf16[23,256]{1,0:T(8,128)(2,1)}, u32[]{:S(2)}) copy-start(bf16[23,256]{1,0:T(8,128)(2,1)} %refs_6_.1) | copy-start | bytes 35332
  2.0 9.1 %collective-permute-start = (bf16[80,256]{1,0:T(8,128)(2,1)S(1)}, bf16[80,256]{1,0:T(8,128)(2,1)S(1)}, u32[]{:S(2)}, u32[]{:S(2)}) collective-permute-start(bf16[80,256]{1,0:T(8,128)(2,1)S(1)} %get-tuple-element.11.refs_0_), channel_id=1, source_target_pairs={{0,2},{1,3},{2,0},{3,1},{4,6},{5,7},{6,4},{7,5},{8,10},{9,11},{10,... | collective-permute-start | bytes 122888 | tf_op jit(solution)/shard_map/ppermute | solution.py:522
  6.1 6.4 %collective-permute-start.1 = (bf16[80,256]{1,0:T(8,128)(2,1)S(1)}, bf16[80,256]{1,0:T(8,128)(2,1)S(1)}, u32[]{:S(2)}, u32[]{:S(2)}) collective-permute-start(bf16[80,256]{1,0:T(8,128)(2,1)S(1)} %get-tuple-element.11.refs_0_), channel_id=1, source_target_pairs={{0,3},{1,2},{2,1},{3,0},{4,7},{5,6},{6,5},{7,4},{8,11},{9,10},{10,... | collective-permute-start | bytes 122888 | tf_op jit(solution)/shard_map/ppermute | solution.py:522
  7.4 5.0 %collective-permute-start.2 = (bf16[80,256]{1,0:T(8,128)(2,1)S(1)}, bf16[80,256]{1,0:T(8,128)(2,1)S(1)}, u32[]{:S(2)}, u32[]{:S(2)}) collective-permute-start(bf16[80,256]{1,0:T(8,128)(2,1)S(1)} %get-tuple-element.11.refs_0_), channel_id=1, source_target_pairs={{0,1},{1,0},{2,3},{3,2},{4,5},{5,4},{6,7},{7,6},{8,9},{9,8},{10,11... | collective-permute-start | bytes 122888 | tf_op jit(solution)/shard_map/ppermute | solution.py:522
  7.6 9.6 %collective-permute-start.3 = (bf16[8,32,128]{2,1,0:T(8,128)(2,1)S(1)}, bf16[8,32,128]{2,1,0:T(8,128)(2,1)S(1)}, u32[]{:S(2)}, u32[]{:S(2)}) collective-permute-start(bf16[8,32,128]{2,1,0:T(8,128)(2,1)S(1)} %copy-done.7), channel_id=1, source_target_pairs={{0,3},{1,2},{2,1},{3,0},{4,7},{5,6},{6,5},{7,4},{8,11},{9,10},{10,... | collective-permute-start | bytes 196616 | tf_op jit(solution)/shard_map/ppermute | solution.py:522
  10.6 6.7 %collective-permute-start.4 = (bf16[8,32,128]{2,1,0:T(8,128)(2,1)S(1)}, bf16[8,32,128]{2,1,0:T(8,128)(2,1)S(1)}, u32[]{:S(2)}, u32[]{:S(2)}) collective-permute-start(bf16[8,32,128]{2,1,0:T(8,128)(2,1)S(1)} %copy-done.7), channel_id=1, source_target_pairs={{0,1},{1,0},{2,3},{3,2},{4,5},{5,4},{6,7},{7,6},{8,9},{9,8},{10,11... | collective-permute-start | bytes 196616 | tf_op jit(solution)/shard_map/ppermute | solution.py:522
  11.0 6.2 %collective-permute-start.5 = (bf16[8,32,128]{2,1,0:T(8,128)(2,1)S(1)}, bf16[8,32,128]{2,1,0:T(8,128)(2,1)S(1)}, u32[]{:S(2)}, u32[]{:S(2)}) collective-permute-start(bf16[8,32,128]{2,1,0:T(8,128)(2,1)S(1)} %copy-done.7), channel_id=1, source_target_pairs={{0,2},{1,3},{2,0},{3,1},{4,6},{5,7},{6,4},{7,5},{8,10},{9,11},{10,... | collective-permute-start | bytes 196616 | tf_op jit(solution)/shard_map/ppermute | solution.py:522
  12.5 4.7 %copy-start.8 = (bf16[128,256]{1,0:T(8,128)(2,1)S(1)}, bf16[128,256]{1,0:T(8,128)(2,1)}, u32[]{:S(2)}) copy-start(bf16[128,256]{1,0:T(8,128)(2,1)} %refs_10_.3) | copy-start | bytes 196612
  12.5 4.7 %copy-start.9 = (bf16[128,256]{1,0:T(8,128)(2,1)S(1)}, bf16[128,256]{1,0:T(8,128)(2,1)}, u32[]{:S(2)}) copy-start(bf16[128,256]{1,0:T(8,128)(2,1)} %refs_11_.3) | copy-start | bytes 196612
  12.6 4.7 %copy-start.12 = (bf16[128,128]{1,0:T(8,128)(2,1)S(1)}, bf16[128,128]{1,0:T(8,128)(2,1)}, u32[]{:S(2)}) copy-start(bf16[128,128]{1,0:T(8,128)(2,1)} %refs_12_.3) | copy-start | bytes 98308
  12.6 4.7 %copy-start.13 = (bf16[128,128]{1,0:T(8,128)(2,1)S(1)}, bf16[128,128]{1,0:T(8,128)(2,1)}, u32[]{:S(2)}) copy-start(bf16[128,128]{1,0:T(8,128)(2,1)} %refs_13_.1) | copy-start | bytes 98308
  (1 other events, 0.7 us)
